TPU v7x, 512 devices: a whole 4x4x16 slice. The times are simulated.
512 devices in a mesh: row: 16 (over y_hi, x, core), col: 32 (over z, y_lo).
Axes of the slice: x: 4, y: 4 (y_hi: 2, y_lo: 2; y = y_hi * 2 + y_lo), z: 16, core: 2. Of those that a mesh axis runs over, the one named last changes fastest.
Arguments:
- object_field: float32 [2, 4096, 8192], P(None, 'row', 'col'), may hold values from -6 to 6
- probe_field: float32 [2, 256, 256], replicated, may hold values from -4 to 4
- intensity: float32 [16, 32, 6, 256, 256], P('row', 'col'), may hold values from 0.05 to 2
- positions: int32 [16, 32, 6, 2], P('row', 'col'), may hold values from -128 to 127
- counts: int32 [16, 32], P('row', 'col'), may hold values from 1 to 6, as said below
Outputs:
- object_new: float32 [2, 4096, 8192], P(None, 'row', 'col')
- probe_update: float32 [2, 256, 256], replicated
Inputs may be any that keep to these rules, and one draw needn't show every extreme that they name: Slots at or after counts of a tile are padding and are ignored; some tile has exactly 6 live slots. `positions`: each window's first pixel lies within 128 pixels before or inside its tile, so windows reach only the eight neighbouring tiles.
All inputs are finite; a program needn't handle non-finite values.
Results may differ from a plain program's by a relative error of at most 0.0003.
Values sent between devices are 32-bit elements; how exact they have to be, the bound alone decides.
No kernel may reach another device: no remote copies, remote signals or barrier semaphores. Data moves between devices by JAX's collectives and lax.ppermute only.
A program may use at most 64 MiB of HBM per device.

v0:
```python
import math

import jax
import jax.numpy as jnp
from jax import lax
from jax.sharding import PartitionSpec as P

OBJECT_RATE = 0.5


def padded(array, sides, width):
    for axis, dim in sides:
        count, length = (lax.axis_size(axis), array.shape[dim])
        up = [(i, (i + 1) % count) for i in range(count - 1)]
        down = [(j, i) for i, j in up]
        last = lax.slice_in_dim(array, length - width, length, axis=dim)
        first = lax.slice_in_dim(array, 0, width, axis=dim)
        before = lax.ppermute(last, axis, up)
        after = lax.ppermute(first, axis, down)
        array = jnp.concatenate([before, array, after], axis=dim)
    return array


def shifted(block, axis, distance):
    devices = range(lax.axis_size(axis))
    route = [(i - distance, i) for i in devices if i - distance in devices]
    return lax.ppermute(block, axis, route)


def spectral_tables(extent):
    indices = jnp.arange(extent, dtype=jnp.int32)
    phase_index = indices[:, None] * indices[None, :] % extent
    angles = phase_index.astype(jnp.float32) * (2.0 * math.pi / extent)
    norm_factor = 1.0 / math.sqrt(extent)
    return (jnp.cos(angles) * norm_factor, jnp.sin(angles) * norm_factor)


def complex_product(left_real, left_imag, right_real, right_imag):
    highest = lax.Precision.HIGHEST
    out_real = jnp.dot(left_real, right_real, precision=highest) - jnp.dot(
        left_imag, right_imag, precision=highest
    )
    out_imag = jnp.dot(left_real, right_imag, precision=highest) + jnp.dot(
        left_imag, right_real, precision=highest
    )
    return (out_real, out_imag)


def two_sided(field_real, field_imag, cos_table, sin_signed):
    half_real, half_imag = complex_product(cos_table, sin_signed, field_real, field_imag)
    return complex_product(half_real, half_imag, cos_table, sin_signed)


def rim_bounds(direction, width, tile):
    if direction == 1:
        return (width + tile, 0, width)
    if direction == -1:
        return (0, tile - width, width)
    return (width, 0, tile)


def shards(object_field, probe_field, intensity, positions, counts):
    extent = probe_field.shape[1]
    width = extent // 2
    tile = object_field.shape[1]
    extended = padded(object_field, (("row", 1), ("col", 2)), width)
    cos_table, sin_table = spectral_tables(extent)
    probe_real = probe_field[0]
    probe_imag = probe_field[1]

    def one_slot(slot_index, totals):
        grad_ext, grad_probe = totals
        row_start = positions[0, 0, slot_index, 0] + width
        col_start = positions[0, 0, slot_index, 1] + width
        anchor = jnp.zeros((), jnp.int32)
        window = lax.dynamic_slice(extended, (anchor, row_start, col_start), (2, extent, extent))
        object_real = window[0]
        object_imag = window[1]
        exit_real = probe_real * object_real - probe_imag * object_imag
        exit_imag = probe_real * object_imag + probe_imag * object_real
        far_real, far_imag = two_sided(exit_real, exit_imag, cos_table, -sin_table)
        misfit = far_real * far_real + far_imag * far_imag - intensity[0, 0, slot_index]
        back_real, back_imag = two_sided(misfit * far_real, misfit * far_imag, cos_table, sin_table)
        object_grad = jnp.stack(
            [
                probe_real * back_real + probe_imag * back_imag,
                probe_real * back_imag - probe_imag * back_real,
            ]
        )
        probe_grad = jnp.stack(
            [
                object_real * back_real + object_imag * back_imag,
                object_real * back_imag - object_imag * back_real,
            ]
        )
        current = lax.dynamic_slice(grad_ext, (anchor, row_start, col_start), (2, extent, extent))
        grad_ext = lax.dynamic_update_slice(
            grad_ext, current + object_grad, (anchor, row_start, col_start)
        )
        return (grad_ext, grad_probe + probe_grad)

    start_totals = (jnp.zeros_like(extended), jnp.zeros_like(probe_field))
    grad_ext, grad_probe = lax.fori_loop(0, counts[0, 0], one_slot, start_totals)
    gathered = grad_ext[:, width : width + tile, width : width + tile]
    for row_dir in (-1, 0, 1):
        for col_dir in (-1, 0, 1):
            if row_dir == 0 and col_dir == 0:
                continue
            row_source, row_target, row_length = rim_bounds(row_dir, width, tile)
            col_source, col_target, col_length = rim_bounds(col_dir, width, tile)
            rim_part = grad_ext[
                :, row_source : row_source + row_length, col_source : col_source + col_length
            ]
            if row_dir != 0:
                rim_part = shifted(rim_part, "row", row_dir)
            if col_dir != 0:
                rim_part = shifted(rim_part, "col", col_dir)
            gathered = gathered.at[
                :, row_target : row_target + row_length, col_target : col_target + col_length
            ].add(rim_part)
    probe_gradient = lax.psum(grad_probe, ("row", "col"))
    total_slots = lax.axis_size("row") * lax.axis_size("col") * positions.shape[2]
    probe_update = probe_gradient * (1.0 / math.sqrt(total_slots))
    object_new = object_field - OBJECT_RATE * gathered
    return (object_new, probe_update)


def solution(mesh):
    placed = (
        P(None, "row", "col"),
        P(),
        P("row", "col", None, None, None),
        P("row", "col", None, None),
        P("row", "col"),
    )
    return jax.shard_map(
        shards, mesh=mesh, in_specs=placed, out_specs=(P(None, "row", "col"), P()), check_vma=False
    )
```

profile of v0, /device:TPU:1, one launch (start us, length us, event | category | flops | bytes accessed | tf_op | source)
XLA Modules:
  0.0 780.2 jit_solution(8546924960436026346)
XLA Ops:
  8.3 4.5 collective-permute-start
  12.8 5.7 collective-permute-start.1
  21.7 3.2 collective-permute-start.2
  27.7 17.8 %collective-permute-done.2 = f32[2,512,128]{2,1,0:T(8,128)S(1)} collective-permute-done((f32[2,512,128]{2,1,0:T(8,128)S(1)}, f32[2,512,128]{2,1,0:T(8,128)S(1)}, u32[]{:S(2)}, u32[]{:S(2)}) %collective-permute-start.2) | collective-permute-done | bytes 524320 | tf_op jit(solution)/shard_map/ppermute | solution.py:18
  47.2 1.6 broadcast_in_dim.8
  49.6 189.3 %while.25 = (s32[]{:T(128)}, f32[2,512,512]{2,1,0:T(8,128)}, f32[2,256,256]{2,1,0:T(8,128)}, s32[]{:T(128)}, s32[1,1,6,2]{2,3,1,0:T(2,128)S(1)}, /*index=5*/f32[...) while((s32[]{:T(128)}, f32[2,512,512]{2,1,0:T(8,128)}, ...), condition=%wide.region_1.2_spmd.clone.clone, body=%wide.region_0.1_spmd.clone.clone.sunk | while | flops 3239837696 | bytes 23331212 | solution.py:103
  64.2 2.4 fusion.185
  80.9 6.3 dynamic_update_slice.10
  101.7 2.4 fusion.185
  118.4 6.6 dynamic_update_slice.10
  139.5 2.4 fusion.185
  156.2 6.7 dynamic_update_slice.10
  177.5 2.4 fusion.185
  194.2 6.2 dynamic_update_slice.10
  215.0 2.4 fusion.185
  231.7 6.5 dynamic_update_slice.10
  239.0 1.9 fusion.111
  240.9 1.9 fusion.110
  242.8 1.9 collective-permute-start.4
  244.8 1.9 collective-permute-start.6
  246.7 1.9 collective-permute-start.7
  250.8 4.0 collective-permute-start.10
  256.1 485.9 %all-reduce.2.cloned.1.call-done = f32[2,256,256]{2,1,0:T(8,128)} async-done(((f32[2,256,256]{2,1,0:T(8,128)}), f32[2,256,256]{2,1,0:T(8,128)}) %all-reduce.2.cloned.1.call-update) | async-done | bytes 524304 | tf_op jit(solution)/shard_map/psum | solution.py:121
  742.0 1.9 broadcast_multiply_fusion
  743.9 5.0 collective-permute-start.11
  748.9 1.9 collective-permute-start.14
  750.9 3.0 collective-permute-start.8
  755.0 3.9 collective-permute-start.13
  760.2 4.0 collective-permute-start.15
  764.4 3.5 collective-permute-done.12
  767.9 2.0 add_select_fusion.1
  769.9 2.4 scatter-add.35
  (163 shorter events, 143.1 us)
Async XLA Ops:
  7.2 734.9 %all-reduce.2.cloned.1.call-start = ((), (), s32[]{:S(2)}) async-start(), calls=%async_computation | async-start | bytes 1048576 | tf_op jit(solution)/shard_map/psum | solution.py:121
  8.3 10.3 %collective-permute-start = (f32[2,128,256]{2,1,0:T(8,128)S(1)}, f32[2,128,256]{2,1,0:T(8,128)S(1)}, u32[]{:S(2)}, u32[]{:S(2)}) collective-permute-start(f32[2,128,256]{2,1,0:T(8,128)S(1)} %get-tuple-element.434), channel_id=1, source_target_pairs={{0,32},{32,64},{64,96},{96,128},{128,160},{160,192},{192,224},{224... | collective-permute-start | bytes 786440 | tf_op jit(solution)/shard_map/ppermute | solution.py:18
  12.8 14.1 %copy-start.7 = (s32[3]{0:T(128)S(1)}, s32[3]{0:T(128)}, u32[]{:S(2)}) copy-start(s32[3]{0:T(128)} %constant.279.clone.1) | copy-start | bytes 40
  12.8 14.9 %copy-start.5 = (f32[2,256,256]{2,1,0:T(8,128)S(1)}, f32[2,256,256]{2,1,0:T(8,128)}, u32[]{:S(2)}) copy-start(f32[2,256,256]{2,1,0:T(8,128)} %param.24) | copy-start | bytes 1572868
  12.8 7.8 %collective-permute-start.1 = (f32[2,128,256]{2,1,0:T(8,128)S(1)}, f32[2,128,256]{2,1,0:T(8,128)S(1)}, u32[]{:S(2)}, u32[]{:S(2)}) collective-permute-start(f32[2,128,256]{2,1,0:T(8,128)S(1)} %get-tuple-element.433), channel_id=1, source_target_pairs={{32,0},{64,32},{96,64},{128,96},{160,128},{192,160},{224,192},{256... | collective-permute-start | bytes 786440 | tf_op jit(solution)/shard_map/ppermute | solution.py:19
  20.7 1.0 copy-start.3
  21.7 23.9 %collective-permute-start.2 = (f32[2,512,128]{2,1,0:T(8,128)S(1)}, f32[2,512,128]{2,1,0:T(8,128)S(1)}, u32[]{:S(2)}, u32[]{:S(2)}) collective-permute-start(f32[2,512,128]{2,1,0:T(8,128)S(1)} %get-tuple-element.429), channel_id=1, source_target_pairs={{0,1},{1,2},{2,3},{3,4},{4,5},{5,6},{6,7},{7,8},{8,9},{9,10},{10,1... | collective-permute-start | bytes 1572872 | tf_op jit(solution)/shard_map/ppermute | solution.py:18
  25.0 20.6 %collective-permute-start.3 = (f32[2,512,128]{2,1,0:T(8,128)S(1)}, f32[2,512,128]{2,1,0:T(8,128)}, u32[]{:S(2)}, u32[]{:S(2)}) collective-permute-start(f32[2,512,128]{2,1,0:T(8,128)S(1)} %get-tuple-element.430), channel_id=1, source_target_pairs={{1,0},{2,1},{3,2},{4,3},{5,4},{6,5},{7,6},{8,7},{9,8},{10,9},{11,1... | collective-permute-start | bytes 1572872 | tf_op jit(solution)/shard_map/ppermute | solution.py:19
  47.2 2.4 copy-start.6
  75.5 3.1 copy-start
  80.1 0.8 copy-start.1
  113.0 3.1 copy-start
  117.6 0.8 copy-start.1
  150.8 3.1 copy-start
  155.4 0.8 copy-start.1
  188.8 3.1 copy-start
  193.4 0.8 copy-start.1
  226.3 3.1 copy-start
  239.0 3.9 copy-start.2
  242.8 11.9 %collective-permute-start.4 = (f32[2,128,128]{2,1,0:T(8,128)S(1)}, f32[2,128,128]{2,1,0:T(8,128)}, u32[]{:S(2)}, u32[]{:S(2)}) collective-permute-start(f32[2,128,128]{2,1,0:T(8,128)S(1)} %get-tuple-element.424), channel_id=1, source_target_pairs={{32,0},{64,32},{96,64},{128,96},{160,128},{192,160},{224,192},{256... | collective-permute-start | bytes 393224 | tf_op jit(solution)/shard_map/ppermute | solution.py:27
  244.8 506.1 %collective-permute-start.6 = (f32[2,128,256]{2,1,0:T(8,128)}, f32[2,128,256]{2,1,0:T(8,128)}, u32[]{:S(2)}, u32[]{:S(2)}) collective-permute-start(f32[2,128,256]{2,1,0:T(8,128)} %get-tuple-element.426), channel_id=1, source_target_pairs={{32,0},{64,32},{96,64},{128,96},{160,128},{192,160},{224,192},{256... | collective-permute-start | bytes 786440 | tf_op jit(solution)/shard_map/ppermute | solution.py:27
  246.7 502.2 %collective-permute-start.7 = (f32[2,128,128]{2,1,0:T(8,128)}, f32[2,128,128]{2,1,0:T(8,128)}, u32[]{:S(2)}, u32[]{:S(2)}) collective-permute-start(f32[2,128,128]{2,1,0:T(8,128)} %get-tuple-element.423), channel_id=1, source_target_pairs={{32,0},{64,32},{96,64},{128,96},{160,128},{192,160},{224,192},{256... | collective-permute-start | bytes 393224 | tf_op jit(solution)/shard_map/ppermute | solution.py:27
  249.5 514.8 %collective-permute-start.9 = (f32[2,256,128]{2,1,0:T(8,128)}, f32[2,256,128]{2,1,0:T(8,128)S(1)}, u32[]{:S(2)}, u32[]{:S(2)}) collective-permute-start(f32[2,256,128]{2,1,0:T(8,128)} %get-tuple-element.428), channel_id=1, source_target_pairs={{1,0},{2,1},{3,2},{4,3},{5,4},{6,5},{7,6},{8,7},{9,8},{10,9},{11,1... | collective-permute-start | bytes 786440 | tf_op jit(solution)/shard_map/ppermute | solution.py:27
  250.8 513.6 %collective-permute-start.10 = (f32[2,256,128]{2,1,0:T(8,128)}, f32[2,256,128]{2,1,0:T(8,128)S(1)}, u32[]{:S(2)}, u32[]{:S(2)}) collective-permute-start(f32[2,256,128]{2,1,0:T(8,128)} %get-tuple-element.427), channel_id=1, source_target_pairs={{0,1},{1,2},{2,3},{3,4},{4,5},{5,6},{6,7},{7,8},{8,9},{9,10},{10,1... | collective-permute-start | bytes 786440 | tf_op jit(solution)/shard_map/ppermute | solution.py:27
  254.8 489.1 %collective-permute-start.5 = (f32[2,128,128]{2,1,0:T(8,128)}, f32[2,128,128]{2,1,0:T(8,128)S(1)}, u32[]{:S(2)}, u32[]{:S(2)}) collective-permute-start(f32[2,128,128]{2,1,0:T(8,128)} %collective-permute-done.4), channel_id=1, source_target_pairs={{1,0},{2,1},{3,2},{4,3},{5,4},{6,5},{7,6},{8,7},{9,8},{10,9},{11,1... | collective-permute-start | bytes 393224 | tf_op jit(solution)/shard_map/ppermute | solution.py:27
  743.9 11.1 %collective-permute-start.11 = (f32[2,128,128]{2,1,0:T(8,128)}, f32[2,128,128]{2,1,0:T(8,128)S(1)}, u32[]{:S(2)}, u32[]{:S(2)}) collective-permute-start(f32[2,128,128]{2,1,0:T(8,128)} %get-tuple-element.422), channel_id=1, source_target_pairs={{0,32},{32,64},{64,96},{96,128},{128,160},{160,192},{192,224},{224... | collective-permute-start | bytes 393224 | tf_op jit(solution)/shard_map/ppermute | solution.py:27
  748.9 10.0 %collective-permute-start.14 = (f32[2,128,128]{2,1,0:T(8,128)}, f32[2,128,128]{2,1,0:T(8,128)S(1)}, u32[]{:S(2)}, u32[]{:S(2)}) collective-permute-start(f32[2,128,128]{2,1,0:T(8,128)} %get-tuple-element.421), channel_id=1, source_target_pairs={{0,32},{32,64},{64,96},{96,128},{128,160},{160,192},{192,224},{224... | collective-permute-start | bytes 393224 | tf_op jit(solution)/shard_map/ppermute | solution.py:27
  750.9 9.4 %collective-permute-start.8 = (f32[2,128,128]{2,1,0:T(8,128)}, f32[2,128,128]{2,1,0:T(8,128)S(1)}, u32[]{:S(2)}, u32[]{:S(2)}) collective-permute-start(f32[2,128,128]{2,1,0:T(8,128)} %collective-permute-done.7), channel_id=1, source_target_pairs={{0,1},{1,2},{2,3},{3,4},{4,5},{5,6},{6,7},{7,8},{8,9},{9,10},{10,1... | collective-permute-start | bytes 393224 | tf_op jit(solution)/shard_map/ppermute | solution.py:27
  755.0 17.5 %copy-start.4 = (f32[2,256,256]{2,1,0:T(8,128)S(1)}, f32[2,256,256]{2,1,0:T(8,128)}, u32[]{:S(2)}) copy-start(f32[2,256,256]{2,1,0:T(8,128)} %param.23) | copy-start | bytes 1572868
  755.0 17.4 %collective-permute-start.13 = (f32[2,128,256]{2,1,0:T(8,128)S(1)}, f32[2,128,256]{2,1,0:T(8,128)S(1)}, u32[]{:S(2)}, u32[]{:S(2)}) collective-permute-start(f32[2,128,256]{2,1,0:T(8,128)S(1)} %get-tuple-element.425), channel_id=1, source_target_pairs={{0,32},{32,64},{64,96},{96,128},{128,160},{160,192},{192,224},{224... | collective-permute-start | bytes 786440 | tf_op jit(solution)/shard_map/ppermute | solution.py:27
  758.9 9.0 %collective-permute-start.12 = (f32[2,128,128]{2,1,0:T(8,128)S(1)}, f32[2,128,128]{2,1,0:T(8,128)S(1)}, u32[]{:S(2)}, u32[]{:S(2)}) collective-permute-start(f32[2,128,128]{2,1,0:T(8,128)S(1)} %collective-permute-done.11), channel_id=1, source_target_pairs={{1,0},{2,1},{3,2},{4,3},{5,4},{6,5},{7,6},{8,7},{9,8},{10,9},{11,1... | collective-permute-start | bytes 393224 | tf_op jit(solution)/shard_map/ppermute | solution.py:27
  760.2 12.2 %collective-permute-start.15 = (f32[2,128,128]{2,1,0:T(8,128)S(1)}, f32[2,128,128]{2,1,0:T(8,128)S(1)}, u32[]{:S(2)}, u32[]{:S(2)}) collective-permute-start(f32[2,128,128]{2,1,0:T(8,128)S(1)} %collective-permute-done.14), channel_id=1, source_target_pairs={{0,1},{1,2},{2,3},{3,4},{4,5},{5,6},{6,7},{7,8},{8,9},{9,10},{10,1... | collective-permute-start | bytes 393224 | tf_op jit(solution)/shard_map/ppermute | solution.py:27
  (1 other events, 0.8 us)
Sparse Core Ops, SparseCore 0:
  241.0 500.9 all-reduce.1
where the time goes:
time: 783 us; the launch traced here: 780 us
  waiting for transfers between devices  508 us (65%)
  matrix products  123 us (16%)
  local copies, waits for them, and re-layouts  53 us (7%)
  starting transfers between devices  46.3 us (6%)
  loops' own time  18.2 us (2%)
  other arithmetic  17.1 us (2%)
  between operations  14.4 us (2%)
    psum x1, waiting for transfers between devices, shards(): probe_gradient = lax.psum(grad_probe, ('row', 'col'))  486 us
    dot_general x20, matrix products, complex_product(): jnp.dot(left_imag, right_real, precision=highest)  34.3 us
    dynamic_update_slice x5, local copies, waits for them, and re-layouts, one_slot(): lax.dynamic_update_slice(grad_ext, current + object_grad, (anchor, row_st...  32.2 us
    ppermute x12, starting transfers between devices, shifted(): return lax.ppermute(block, axis, route)  31.5 us
    dot_general x20, matrix products, complex_product(): jnp.dot(left_imag, right_imag, precision=highest)  30 us
    dot_general x20, matrix products, complex_product(): jnp.dot(left_real, right_imag, precision=highest)  29.4 us
    dot_general x20, matrix products, complex_product(): jnp.dot(left_real, right_real, precision=highest)  29.3 us
    another operation x1, loops' own time, shards(): lax.fori_loop(0, counts[0, 0], one_slot, start_totals)  18.2 us
  transfers between devices with their start and end apart: 17, of which 4 were waited for; matrix products, arithmetic and copies ran while one was open for 2% of the time, Pallas kernels for 0%

commit v1 on v0

v1 whole, which is shorter than its diff:
```python
import math

import jax
import jax.numpy as jnp
import ml_dtypes
import numpy as np
from jax import lax
from jax.experimental import pallas as pl
from jax.experimental.pallas import tpu as pltpu
from jax.sharding import Mesh, PartitionSpec as P

OBJECT_RATE = 0.5
ROW = ("yh", "x", "core")
COL = ("z", "yl")
PLANE = ("yh", "x", "core", "yl")
DEEP = "z"
SIDE = 256
RIM = 128
WIDE = 2 * SIDE
F32 = jnp.float32
BF16 = jnp.bfloat16


def two_terms(table):
    high = table.astype(np.float32).astype(ml_dtypes.bfloat16)
    low = (table - high.astype(np.float64)).astype(np.float32).astype(ml_dtypes.bfloat16)
    return high, low


def spectral_tables():
    index = np.arange(SIDE)
    angles = (index[:, None] * index[None, :] % SIDE) * (2.0 * math.pi / SIDE)
    cos, sin = np.cos(angles) / 16.0, np.sin(angles) / 16.0
    out = []
    for sign in (1.0, -1.0):
        left = np.concatenate([cos, sign * sin], 1)
        right = np.block([[cos, -sign * sin], [sign * sin, cos]])
        high, low = two_terms(left)
        out.append(np.concatenate([high, high, low], 1))
        high, low = two_terms(right)
        out.append(np.concatenate([high, high, low], 0))
    return out


def split(value):
    high = value.astype(BF16)
    low = (value - high.astype(F32)).astype(BF16)
    return high, low


def slots_kernel(
    counts_ref, pos_ref, tile_ref, side_l_ref, side_r_ref, top_ref, bot_ref, ctop_ref, cbot_ref,
    probe_ref, intensity_ref, left_fwd_ref, right_fwd_ref, left_inv_ref, right_inv_ref,
    gprobe_ref, gtop_ref, gbot_ref, gmid_ref,
    ext_ref, twice_ref, shifted_ref, window_ref, stack_ref, mid_ref, back_ref,
):
    dot = lambda a, b: jnp.dot(a, b, preferred_element_type=F32)
    for c in range(2):
        ext_ref[c, RIM : RIM + SIDE, RIM : RIM + SIDE] = tile_ref[c]
        ext_ref[c, RIM : RIM + SIDE, 0:RIM] = side_l_ref[c]
        ext_ref[c, RIM : RIM + SIDE, RIM + SIDE :] = side_r_ref[c]
        ext_ref[c, 0:RIM, RIM : RIM + SIDE] = top_ref[c]
        ext_ref[c, RIM + SIDE :, RIM : RIM + SIDE] = bot_ref[c]
        ext_ref[c, 0:RIM, 0:RIM] = ctop_ref[c, :, 0:RIM]
        ext_ref[c, 0:RIM, RIM + SIDE :] = ctop_ref[c, :, RIM:]
        ext_ref[c, RIM + SIDE :, 0:RIM] = cbot_ref[c, :, 0:RIM]
        ext_ref[c, RIM + SIDE :, RIM + SIDE :] = cbot_ref[c, :, RIM:]
        twice_ref[c, 0:SIDE] = probe_ref[c]
        twice_ref[c, SIDE:WIDE] = probe_ref[c]
        gprobe_ref[c] = jnp.zeros((SIDE, SIDE), F32)
        gtop_ref[c] = jnp.zeros((RIM, WIDE), F32)
        gbot_ref[c] = jnp.zeros((RIM, WIDE), F32)
        gmid_ref[c] = jnp.zeros((SIDE, WIDE), F32)

    step = 64
    blocks = [slice(k, k + step) for k in range(0, SIDE, step)]

    def rows_from(ref, c, offset, start):
        over = offset & 7
        base = pl.multiple_of(offset - over + start, 8)
        return pltpu.roll(ref[c, pl.ds(base, step + 8), :], jnp.where(over == 0, 0, step + 8 - over), 0)[0:step]

    def put(rows, real, imag):
        real_high, real_low = split(real)
        imag_high, imag_low = split(imag)
        for base, re, im in ((0, real_high, imag_high), (WIDE, real_low, imag_low), (2 * WIDE, real_high, imag_high)):
            upper = slice(base + rows.start, base + rows.stop)
            lower = slice(base + SIDE + rows.start, base + SIDE + rows.stop)
            stack_ref[upper, 0:SIDE] = re
            stack_ref[upper, SIDE:] = im
            stack_ref[lower, 0:SIDE] = im
            stack_ref[lower, SIDE:] = -re

    def wide(value):
        high, low = split(value)
        return jnp.concatenate([high, low, high], axis=1)

    def one_slot(slot, carry):
        row = pos_ref[2 * slot] + RIM
        col = pos_ref[2 * slot + 1] + RIM
        col_ids = lax.broadcasted_iota(jnp.int32, (step, SIDE), 1)
        row_ids = lax.broadcasted_iota(jnp.int32, (step, SIDE), 0)
        here_col = col_ids >= col
        for rows in blocks:
            here_row = row_ids >= row - rows.start
            far_rows = slice(rows.start + SIDE, rows.stop + SIDE)
            for c in range(2):
                first = jnp.where(here_row, ext_ref[c, rows, 0:SIDE], ext_ref[c, far_rows, 0:SIDE])
                second = jnp.where(here_row, ext_ref[c, rows, SIDE:], ext_ref[c, far_rows, SIDE:])
                window_ref[c, rows] = jnp.where(here_col, first, second)
                turned = rows_from(twice_ref, c, SIDE - row, rows.start)
                shifted_ref[c, rows] = pltpu.roll(turned, col, 1)
            pr, pi = shifted_ref[0, rows], shifted_ref[1, rows]
            wr, wi = window_ref[0, rows], window_ref[1, rows]
            put(rows, pr * wr - pi * wi, pr * wi + pi * wr)
        mid_ref[...] = dot(left_fwd_ref[...], stack_ref[...])
        for rows in blocks:
            far = dot(wide(mid_ref[rows]), right_fwd_ref[...])
            far_real, far_imag = far[:, 0:SIDE], far[:, SIDE:]
            misfit = far_real * far_real + far_imag * far_imag - intensity_ref[slot, rows]
            bent = jnp.concatenate([misfit * far_real, misfit * far_imag], axis=1)
            turned = dot(wide(bent), right_inv_ref[...])
            put(rows, turned[:, 0:SIDE], turned[:, SIDE:])
        mid_ref[...] = dot(left_inv_ref[...], stack_ref[...])
        for rows in blocks:
            here_row = row_ids >= row - rows.start
            far_rows = slice(rows.start + SIDE, rows.stop + SIDE)
            br, bi = mid_ref[rows, 0:SIDE], mid_ref[rows, SIDE:]
            pr, pi = shifted_ref[0, rows], shifted_ref[1, rows]
            wr, wi = window_ref[0, rows], window_ref[1, rows]
            for c, grad in enumerate((pr * br + pi * bi, pr * bi - pi * br)):
                first = jnp.where(here_col, grad, 0.0)
                second = jnp.where(here_col, 0.0, grad)
                for piece, cols in ((first, slice(0, SIDE)), (second, slice(SIDE, WIDE))):
                    near = jnp.where(here_row, piece, 0.0)
                    away = jnp.where(here_row, 0.0, piece)
                    if rows.start < RIM:
                        gtop_ref[c, rows, cols] += near
                        gmid_ref[c, rows.start + RIM : rows.stop + RIM, cols] += away
                    else:
                        gmid_ref[c, rows.start - RIM : rows.stop - RIM, cols] += near
                        gbot_ref[c, rows.start - RIM : rows.stop - RIM, cols] += away
            for c, grad in enumerate((wr * br + wi * bi, wr * bi - wi * br)):
                back_ref[c, rows] = grad
                back_ref[c, far_rows] = grad
        for rows in blocks:
            for c in range(2):
                turned = rows_from(back_ref, c, row, rows.start)
                gprobe_ref[c, rows] += pltpu.roll(turned, (SIDE - col) & (SIDE - 1), 1)
        return carry

    lax.fori_loop(0, counts_ref[0], one_slot, 0)


def all_slots(counts, positions, *arrays):
    smem = pl.BlockSpec(memory_space=pltpu.SMEM)
    vmem = pl.BlockSpec(memory_space=pltpu.VMEM)
    return pl.pallas_call(
        slots_kernel,
        out_shape=[
            jax.ShapeDtypeStruct((2, SIDE, SIDE), F32),
            jax.ShapeDtypeStruct((2, RIM, WIDE), F32),
            jax.ShapeDtypeStruct((2, RIM, WIDE), F32),
            jax.ShapeDtypeStruct((2, SIDE, WIDE), F32),
        ],
        in_specs=[smem, smem] + [vmem] * len(arrays),
        out_specs=[vmem] * 4,
        scratch_shapes=[
            pltpu.VMEM((2, WIDE, WIDE), F32),
            pltpu.VMEM((2, WIDE + 8, SIDE), F32),
            pltpu.VMEM((2, SIDE, SIDE), F32),
            pltpu.VMEM((2, SIDE, SIDE), F32),
            pltpu.VMEM((3 * WIDE, WIDE), BF16),
            pltpu.VMEM((SIDE, WIDE), F32),
            pltpu.VMEM((2, WIDE + 8, SIDE), F32),
        ],
        compiler_params=pltpu.CompilerParams(vmem_limit_bytes=32 * 1024 * 1024),
        cost_estimate=pl.CostEstimate(flops=10_000_000_000, bytes_accessed=20_000_000, transcendentals=0),
    )(counts, positions, *arrays)


def shifted(block, axes, distance):
    count = lax.axis_size(axes)
    route = [(i, i + distance) for i in range(count) if 0 <= i + distance < count]
    return lax.ppermute(block, axes, route)


def swap(pieces, axes):
    return lax.all_to_all(pieces, axes, split_axis=0, concat_axis=0, tiled=True)


def spread(block, axes):
    count = lax.axis_size(axes)
    return swap(jnp.broadcast_to(block[None], (count,) + block.shape), axes)


def summed_everywhere(grad):
    count = lax.axis_size(PLANE)
    pieces = swap(grad.reshape(count, 2 * SIDE // count, SIDE), PLANE)
    part = spread(jnp.sum(pieces, axis=0), DEEP)
    whole = spread(jnp.sum(part, axis=0), PLANE)
    return whole.reshape(2, SIDE, SIDE)


def shards(object_field, probe_field, intensity, positions, counts):
    tables = [jnp.asarray(t) for t in spectral_tables()]
    side_l = shifted(object_field[:, :, RIM:], COL, 1)
    side_r = shifted(object_field[:, :, :RIM], COL, -1)
    top = shifted(object_field[:, RIM:], ROW, 1)
    bottom = shifted(object_field[:, :RIM], ROW, -1)
    sides = jnp.concatenate([side_l, side_r], axis=2)
    corner_top = shifted(sides[:, RIM:], ROW, 1)
    corner_bottom = shifted(sides[:, :RIM], ROW, -1)
    grad_probe, grad_top, grad_bottom, grad_mid = all_slots(
        counts.reshape(1),
        positions.reshape(-1),
        object_field,
        side_l,
        side_r,
        top,
        bottom,
        corner_top,
        corner_bottom,
        probe_field,
        intensity[0, 0],
        *tables,
    )
    from_above = shifted(grad_bottom, ROW, 1)
    from_below = shifted(grad_top, ROW, -1)
    probe_gradient = summed_everywhere(grad_probe)
    rows = grad_mid + jnp.concatenate([from_above, from_below], axis=1)
    from_left = shifted(rows[:, :, RIM + SIDE :], COL, 1)
    from_right = shifted(rows[:, :, :RIM], COL, -1)
    gathered = rows[:, :, RIM : RIM + SIDE] + jnp.concatenate([from_left, from_right], axis=2)
    total_slots = lax.axis_size(ROW) * lax.axis_size(COL) * positions.shape[2]
    probe_update = probe_gradient * (1.0 / math.sqrt(total_slots))
    object_new = object_field - OBJECT_RATE * gathered
    return (object_new, probe_update)


def solution(mesh):
    chips = Mesh(mesh.devices.reshape(2, 4, 2, 16, 2), ("yh", "x", "core", "z", "yl"))
    placed = (
        P(None, ROW, COL),
        P(),
        P(ROW, COL, None, None, None),
        P(ROW, COL, None, None),
        P(ROW, COL),
    )
    return jax.shard_map(
        shards, mesh=chips, in_specs=placed, out_specs=(P(None, ROW, COL), P()), check_vma=False
    )
```

time: 783 us -> 142 us (0.18)
  waiting for transfers between devices: 508 us -> 23.4 us
  matrix products: 123 us -> 0 us
  local copies, waits for them, and re-layouts: 53 us -> 17.8 us
  starting transfers between devices: 46.3 us -> 80.4 us
  loops' own time: 18.2 us -> 0 us
  Pallas kernels: 0 us -> 15 us
  other arithmetic: 17.1 us -> 3.2 us
  between operations: 14.4 us -> 1.54 us
    psum x1 -> x0, waiting for transfers between devices: 486 us -> none  [shards(): probe_gradient = lax.psum(grad_probe, ('row', 'col'))]
    dot_general x80 -> x0, matrix products: 123 us -> none  [the longest x20 34.3 us: complex_product(): jnp.dot(left_imag, right_real, precision=highest)]
    all_to_all x0 -> x3, starting transfers between devices: none -> 51.2 us  [swap(): return lax.all_to_all(pieces, axes, split_axis=0, concat_axis=0, tiled=True)]
    dynamic_update_slice x5 -> x0, local copies, waits for them, and re-layouts: 32.2 us -> none  [one_slot(): lax.dynamic_update_slice(grad_ext, current + object_grad, (anchor, row_st...]
    all_to_all x0 -> x3, waiting for transfers between devices: none -> 22.3 us  [swap(): return lax.all_to_all(pieces, axes, split_axis=0, concat_axis=0, tiled=True)]
    ppermute x16 -> x10, waiting for transfers between devices: 22.4 us -> 1.07 us  [shifted(): return lax.ppermute(block, axes, route)]
    another operation x1 -> x0, loops' own time: 18.2 us -> none  [shards(): lax.fori_loop(0, counts[0, 0], one_slot, start_totals)]
    ppermute x16 -> x10, starting transfers between devices: 46.2 us -> 29.3 us  [shifted(): return lax.ppermute(block, axes, route)]
  transfers between devices with their start and end apart: 17 -> 13, of which waited for: 4 -> 5; matrix products, arithmetic and copies ran while one was open for 2% -> 4% of each run, Pallas kernels for 0% -> 0%
where the time goes in v1:
time: 142 us; the launch traced here: 141 us
  starting transfers between devices  80.4 us (57%)
  waiting for transfers between devices  23.4 us (16%)
  local copies, waits for them, and re-layouts  17.8 us (13%)
  Pallas kernels  15 us (11%)
  other arithmetic  3.2 us (2%)
  between operations  1.54 us (1%)
    all_to_all x3, starting transfers between devices, swap(): return lax.all_to_all(pieces, axes, split_axis=0, concat_axis=0, tiled=True)  51.2 us
    ppermute x10, starting transfers between devices, shifted(): return lax.ppermute(block, axes, route)  29.3 us
    all_to_all x3, waiting for transfers between devices, swap(): return lax.all_to_all(pieces, axes, split_axis=0, concat_axis=0, tiled=True)  22.3 us
    pallas_call x1, Pallas kernels, all_slots(): pl.pallas_call(slots_kernel, out_shape=[jax.ShapeDtypeStruct((2, SIDE, SI...  15 us
    unnamed x34, local copies, waits for them, and re-layouts  13.1 us
  transfers between devices with their start and end apart: 13, of which 5 were waited for; matrix products, arithmetic and copies ran while one was open for 4% of the time, Pallas kernels for 0%

profile of v1, /device:TPU:1, one launch (start us, length us, event | category | flops | bytes accessed | tf_op | source)
XLA Modules:
  0.0 141.3 jit_solution(4238012472440972999)
XLA Ops:
  0.6 1.1 fusion.5
  1.7 4.0 %collective-permute-start = (f32[2,256,128]{2,1,0:T(8,128)S(1)}, f32[2,256,128]{2,1,0:T(8,128)S(1)}, u32[]{:S(2)}, u32[]{:S(2)}) collective-permute-start(f32[2,256,128]{2,1,0:T(8,128)S(1)} %get-tuple-element.17), channel_id=1, source_target_pairs={{0,1},{1,2},{2,3},{3,4},{4,5},{5,6},{6,7},{7,8},{8,9},{9,10},{10,1... | collective-permute-start | bytes 786440 | tf_op jit(solution)/shard_map/ppermute | solution.py:185
  5.8 1.4 %collective-permute-start.1 = (f32[2,256,128]{2,1,0:T(8,128)S(1)}, f32[2,256,128]{2,1,0:T(8,128)S(1)}, u32[]{:S(2)}, u32[]{:S(2)}) collective-permute-start(f32[2,256,128]{2,1,0:T(8,128)S(1)} %get-tuple-element.16), channel_id=1, source_target_pairs={{1,0},{2,1},{3,2},{4,3},{5,4},{6,5},{7,6},{8,7},{9,8},{10,9},{11,1... | collective-permute-start | bytes 786440 | tf_op jit(solution)/shard_map/ppermute | solution.py:185
  7.2 1.1 fusion.4
  8.3 6.0 %collective-permute-start.3 = (f32[2,128,256]{2,1,0:T(8,128)S(1)}, f32[2,128,256]{2,1,0:T(8,128)S(1)}, u32[]{:S(2)}, u32[]{:S(2)}) collective-permute-start(f32[2,128,256]{2,1,0:T(8,128)S(1)} %get-tuple-element.14), channel_id=1, source_target_pairs={{32,0},{64,32},{96,64},{128,96},{160,128},{192,160},{224,192},{256... | collective-permute-start | bytes 786440 | tf_op jit(solution)/shard_map/ppermute | solution.py:185
  14.4 1.9 %collective-permute-start.2 = (f32[2,128,256]{2,1,0:T(8,128)S(1)}, f32[2,128,256]{2,1,0:T(8,128)S(1)}, u32[]{:S(2)}, u32[]{:S(2)}) collective-permute-start(f32[2,128,256]{2,1,0:T(8,128)S(1)} %get-tuple-element.15), channel_id=1, source_target_pairs={{0,32},{32,64},{64,96},{96,128},{128,160},{160,192},{192,224},{224... | collective-permute-start | bytes 786440 | tf_op jit(solution)/shard_map/ppermute | solution.py:185
  17.1 5.0 %collective-permute-start.5 = (f32[2,128,256]{2,1,0:T(8,128)}, f32[2,128,256]{2,1,0:T(8,128)S(1)}, u32[]{:S(2)}, u32[]{:S(2)}) collective-permute-start(f32[2,128,256]{2,1,0:T(8,128)} %get-tuple-element.12), channel_id=1, source_target_pairs={{32,0},{64,32},{96,64},{128,96},{160,128},{192,160},{224,192},{256... | collective-permute-start | bytes 786440 | tf_op jit(solution)/shard_map/ppermute | solution.py:185
  22.1 1.9 %collective-permute-start.4 = (f32[2,128,256]{2,1,0:T(8,128)S(1)}, f32[2,128,256]{2,1,0:T(8,128)S(1)}, u32[]{:S(2)}, u32[]{:S(2)}) collective-permute-start(f32[2,128,256]{2,1,0:T(8,128)S(1)} %get-tuple-element.13), channel_id=1, source_target_pairs={{0,32},{32,64},{64,96},{96,128},{128,160},{160,192},{192,224},{224... | collective-permute-start | bytes 786440 | tf_op jit(solution)/shard_map/ppermute | solution.py:185
  28.0 1.4 copy-done.1
  29.4 0.9 copy-done.5
  30.4 0.9 copy-done.7
  31.3 0.9 copy-done.9
  32.3 1.4 copy-done.10
  33.7 1.4 copy-done.11
  35.1 1.1 copy-done.12
  36.2 1.1 copy-done.13
  37.4 15.0 %shard_map.104 = (f32[2,256,256]{2,1,0:T(8,128)}, f32[2,128,512]{2,1,0:T(8,128)S(1)}, f32[2,128,512]{2,1,0:T(8,128)S(1)}, f32[2,256,512]{2,1,0:T(8,128)S(1)}) custom-call(s32[1]{0:T(128)} %bitcast.4.counts_ref, s32[12]{0:T(128)S(1)} %reshape.19.pos_ref, f32[2,256,256]{2,1,0:T(8,128)S(1)} %copy-done, f32[2,256,128]{2,1,0:T(8,128)S(1)} %collective-permute-done.side_l_ref, ...), custom_call_target="tpu_custom_call" | custom-call | flops 10000000000 | bytes 20000000 | tf_op jit(solution)/shard_map/pallas_call | solution.py:158
  52.3 0.8 copy-done.3
  53.1 21.0 %all-to-all-start = ((f32[32,16,256]{2,1,0:T(8,128)}), f32[32,16,256]{2,1,0:T(8,128)S(1)}, u32[]{:S(2)}, u32[]{:S(2)}) async-start(f32[32,16,256]{2,1,0:T(8,128)} %bitcast.2), calls=%async_computation | async-start | bytes 1048576 | tf_op jit(solution)/shard_map/all_to_all | solution.py:189
  74.1 3.5 %collective-permute-start.6 = (f32[2,128,512]{2,1,0:T(8,128)}, f32[2,128,512]{2,1,0:T(8,128)S(1)}, u32[]{:S(2)}, u32[]{:S(2)}) collective-permute-start(f32[2,128,512]{2,1,0:T(8,128)} %copy-done.3), channel_id=1, source_target_pairs={{0,32},{32,64},{64,96},{96,128},{128,160},{160,192},{192,224},{224... | collective-permute-start | bytes 1572872 | tf_op jit(solution)/shard_map/ppermute | solution.py:185
  77.6 1.9 %collective-permute-start.7 = (f32[2,128,512]{2,1,0:T(8,128)S(1)}, f32[2,128,512]{2,1,0:T(8,128)}, u32[]{:S(2)}, u32[]{:S(2)}) collective-permute-start(f32[2,128,512]{2,1,0:T(8,128)S(1)} %get-tuple-element.8), channel_id=1, source_target_pairs={{32,0},{64,32},{96,64},{128,96},{160,128},{192,160},{224,192},{256... | collective-permute-start | bytes 1572872 | tf_op jit(solution)/shard_map/ppermute | solution.py:185
  79.6 5.4 %all-to-all-done = f32[32,16,256]{2,1,0:T(8,128)S(1)} async-done(((f32[32,16,256]{2,1,0:T(8,128)}), f32[32,16,256]{2,1,0:T(8,128)S(1)}, u32[]{:S(2)}, u32[]{:S(2)}) %all-to-all-start) | async-done | bytes 524320 | tf_op jit(solution)/shard_map/all_to_all | solution.py:189
  85.7 17.2 %all-to-all-start.1 = ((f32[16,16,256]{2,1,0:T(8,128)}), f32[16,16,256]{2,1,0:T(8,128)S(1)}, u32[]{:S(2)}, u32[]{:S(2)}) async-start(f32[16,16,256]{2,1,0:T(8,128)} %broadcast_in_dim.4), calls=%async_computation.1 | async-start | bytes 524288 | tf_op jit(solution)/shard_map/all_to_all | solution.py:189
  103.7 1.4 maximum_add_fusion
  105.1 2.2 %collective-permute-start.8 = (f32[2,256,128]{2,1,0:T(8,128)S(1)}, f32[2,256,128]{2,1,0:T(8,128)S(1)}, u32[]{:S(2)}, u32[]{:S(2)}) collective-permute-start(f32[2,256,128]{2,1,0:T(8,128)S(1)} %get-tuple-element.10), channel_id=1, source_target_pairs={{0,1},{1,2},{2,3},{3,4},{4,5},{5,6},{6,7},{7,8},{8,9},{9,10},{10,1... | collective-permute-start | bytes 786440 | tf_op jit(solution)/shard_map/ppermute | solution.py:185
  107.3 1.3 collective-permute-start.9
  108.6 7.0 %all-to-all-done.1 = f32[16,16,256]{2,1,0:T(8,128)S(1)} async-done(((f32[16,16,256]{2,1,0:T(8,128)}), f32[16,16,256]{2,1,0:T(8,128)S(1)}, u32[]{:S(2)}, u32[]{:S(2)}) %all-to-all-start.1) | async-done | bytes 262176 | tf_op jit(solution)/shard_map/all_to_all | solution.py:189
  115.7 0.9 broadcast_in_dim.5
  116.5 13.0 %all-to-all-start.2 = ((f32[32,16,256]{2,1,0:T(8,128)}), f32[32,16,256]{2,1,0:T(8,128)S(1)}, u32[]{:S(2)}, u32[]{:S(2)}) async-start(f32[32,16,256]{2,1,0:T(8,128)} %broadcast_in_dim.5), calls=%async_computation.2 | async-start | bytes 1048576 | tf_op jit(solution)/shard_map/all_to_all | solution.py:189
  129.6 0.9 fusion.1
  130.5 9.9 %all-to-all-done.2 = f32[32,16,256]{2,1,0:T(8,128)S(1)} async-done(((f32[32,16,256]{2,1,0:T(8,128)}), f32[32,16,256]{2,1,0:T(8,128)S(1)}, u32[]{:S(2)}, u32[]{:S(2)}) %all-to-all-start.2) | async-done | bytes 524320 | tf_op jit(solution)/shard_map/all_to_all | solution.py:189
  140.4 0.8 broadcast_multiply_fusion
  (42 shorter events, 5.8 us)
Async XLA Ops:
  1.7 14.6 %collective-permute-start = (f32[2,256,128]{2,1,0:T(8,128)S(1)}, f32[2,256,128]{2,1,0:T(8,128)S(1)}, u32[]{:S(2)}, u32[]{:S(2)}) collective-permute-start(f32[2,256,128]{2,1,0:T(8,128)S(1)} %get-tuple-element.17), channel_id=1, source_target_pairs={{0,1},{1,2},{2,3},{3,4},{4,5},{5,6},{6,7},{7,8},{8,9},{9,10},{10,1... | collective-permute-start | bytes 786440 | tf_op jit(solution)/shard_map/ppermute | solution.py:185
  5.8 18.9 %copy-start.15 = (s32[1,1,6,2]{2,3,1,0:T(2,128)S(1)}, s32[1,1,6,2]{2,3,1,0:T(2,128)}, u32[]{:S(2)}) copy-start(s32[1,1,6,2]{2,3,1,0:T(2,128)} %param.12) | copy-start | bytes 148
  5.8 22.2 %copy-start = (f32[2,256,256]{2,1,0:T(8,128)S(1)}, f32[2,256,256]{2,1,0:T(8,128)}, u32[]{:S(2)}) copy-start(f32[2,256,256]{2,1,0:T(8,128)} %tile_ref.1) | copy-start | bytes 1572868
  5.8 22.2 %copy-start.2 = (f32[2,256,256]{2,1,0:T(8,128)S(1)}, f32[2,256,256]{2,1,0:T(8,128)}, u32[]{:S(2)}) copy-start(f32[2,256,256]{2,1,0:T(8,128)} %probe_ref.1) | copy-start | bytes 1572868
  5.8 10.5 %collective-permute-start.1 = (f32[2,256,128]{2,1,0:T(8,128)S(1)}, f32[2,256,128]{2,1,0:T(8,128)S(1)}, u32[]{:S(2)}, u32[]{:S(2)}) collective-permute-start(f32[2,256,128]{2,1,0:T(8,128)S(1)} %get-tuple-element.16), channel_id=1, source_target_pairs={{1,0},{2,1},{3,2},{4,3},{5,4},{6,5},{7,6},{8,7},{9,8},{10,9},{11,1... | collective-permute-start | bytes 786440 | tf_op jit(solution)/shard_map/ppermute | solution.py:185
  8.3 16.5 %collective-permute-start.3 = (f32[2,128,256]{2,1,0:T(8,128)S(1)}, f32[2,128,256]{2,1,0:T(8,128)S(1)}, u32[]{:S(2)}, u32[]{:S(2)}) collective-permute-start(f32[2,128,256]{2,1,0:T(8,128)S(1)} %get-tuple-element.14), channel_id=1, source_target_pairs={{32,0},{64,32},{96,64},{128,96},{160,128},{192,160},{224,192},{256... | collective-permute-start | bytes 786440 | tf_op jit(solution)/shard_map/ppermute | solution.py:185
  14.4 10.5 %collective-permute-start.2 = (f32[2,128,256]{2,1,0:T(8,128)S(1)}, f32[2,128,256]{2,1,0:T(8,128)S(1)}, u32[]{:S(2)}, u32[]{:S(2)}) collective-permute-start(f32[2,128,256]{2,1,0:T(8,128)S(1)} %get-tuple-element.15), channel_id=1, source_target_pairs={{0,32},{32,64},{64,96},{96,128},{128,160},{160,192},{192,224},{224... | collective-permute-start | bytes 786440 | tf_op jit(solution)/shard_map/ppermute | solution.py:185
  17.1 8.8 %collective-permute-start.5 = (f32[2,128,256]{2,1,0:T(8,128)}, f32[2,128,256]{2,1,0:T(8,128)S(1)}, u32[]{:S(2)}, u32[]{:S(2)}) collective-permute-start(f32[2,128,256]{2,1,0:T(8,128)} %get-tuple-element.12), channel_id=1, source_target_pairs={{32,0},{64,32},{96,64},{128,96},{160,128},{192,160},{224,192},{256... | collective-permute-start | bytes 786440 | tf_op jit(solution)/shard_map/ppermute | solution.py:185
  22.1 5.2 %collective-permute-start.4 = (f32[2,128,256]{2,1,0:T(8,128)S(1)}, f32[2,128,256]{2,1,0:T(8,128)S(1)}, u32[]{:S(2)}, u32[]{:S(2)}) collective-permute-start(f32[2,128,256]{2,1,0:T(8,128)S(1)} %get-tuple-element.13), channel_id=1, source_target_pairs={{0,32},{32,64},{64,96},{96,128},{128,160},{160,192},{192,224},{224... | collective-permute-start | bytes 786440 | tf_op jit(solution)/shard_map/ppermute | solution.py:185
  24.8 0.7 copy-start.4
  25.9 0.7 copy-start.6
  27.3 0.7 copy-start.8
  28.0 1.4 copy-start.1
  29.4 0.9 copy-start.5
  30.4 0.9 copy-start.7
  31.3 0.9 copy-start.9
  32.3 1.4 copy-start.10
  33.7 1.4 copy-start.11
  35.1 1.1 copy-start.12
  36.2 1.1 copy-start.13
  52.3 0.8 copy-start.3
  53.1 31.8 %all-to-all-start = ((f32[32,16,256]{2,1,0:T(8,128)}), f32[32,16,256]{2,1,0:T(8,128)S(1)}, u32[]{:S(2)}, u32[]{:S(2)}) async-start(f32[32,16,256]{2,1,0:T(8,128)} %bitcast.2), calls=%async_computation | async-start | bytes 1048576 | tf_op jit(solution)/shard_map/all_to_all | solution.py:189
  74.1 28.8 %collective-permute-start.6 = (f32[2,128,512]{2,1,0:T(8,128)}, f32[2,128,512]{2,1,0:T(8,128)S(1)}, u32[]{:S(2)}, u32[]{:S(2)}) collective-permute-start(f32[2,128,512]{2,1,0:T(8,128)} %copy-done.3), channel_id=1, source_target_pairs={{0,32},{32,64},{64,96},{96,128},{128,160},{160,192},{192,224},{224... | collective-permute-start | bytes 1572872 | tf_op jit(solution)/shard_map/ppermute | solution.py:185
  77.6 25.3 %collective-permute-start.7 = (f32[2,128,512]{2,1,0:T(8,128)S(1)}, f32[2,128,512]{2,1,0:T(8,128)}, u32[]{:S(2)}, u32[]{:S(2)}) collective-permute-start(f32[2,128,512]{2,1,0:T(8,128)S(1)} %get-tuple-element.8), channel_id=1, source_target_pairs={{32,0},{64,32},{96,64},{128,96},{160,128},{192,160},{224,192},{256... | collective-permute-start | bytes 1572872 | tf_op jit(solution)/shard_map/ppermute | solution.py:185
  85.7 29.9 %all-to-all-start.1 = ((f32[16,16,256]{2,1,0:T(8,128)}), f32[16,16,256]{2,1,0:T(8,128)S(1)}, u32[]{:S(2)}, u32[]{:S(2)}) async-start(f32[16,16,256]{2,1,0:T(8,128)} %broadcast_in_dim.4), calls=%async_computation.1 | async-start | bytes 524288 | tf_op jit(solution)/shard_map/all_to_all | solution.py:189
  102.9 0.8 copy-start.14
  105.1 24.4 %collective-permute-start.8 = (f32[2,256,128]{2,1,0:T(8,128)S(1)}, f32[2,256,128]{2,1,0:T(8,128)S(1)}, u32[]{:S(2)}, u32[]{:S(2)}) collective-permute-start(f32[2,256,128]{2,1,0:T(8,128)S(1)} %get-tuple-element.10), channel_id=1, source_target_pairs={{0,1},{1,2},{2,3},{3,4},{4,5},{5,6},{6,7},{7,8},{8,9},{9,10},{10,1... | collective-permute-start | bytes 786440 | tf_op jit(solution)/shard_map/ppermute | solution.py:185
  107.3 22.2 %collective-permute-start.9 = (f32[2,256,128]{2,1,0:T(8,128)S(1)}, f32[2,256,128]{2,1,0:T(8,128)S(1)}, u32[]{:S(2)}, u32[]{:S(2)}) collective-permute-start(f32[2,256,128]{2,1,0:T(8,128)S(1)} %get-tuple-element.11), channel_id=1, source_target_pairs={{1,0},{2,1},{3,2},{4,3},{5,4},{6,5},{7,6},{8,7},{9,8},{10,9},{11,1... | collective-permute-start | bytes 786440 | tf_op jit(solution)/shard_map/ppermute | solution.py:185
  116.5 23.9 %all-to-all-start.2 = ((f32[32,16,256]{2,1,0:T(8,128)}), f32[32,16,256]{2,1,0:T(8,128)S(1)}, u32[]{:S(2)}, u32[]{:S(2)}) async-start(f32[32,16,256]{2,1,0:T(8,128)} %broadcast_in_dim.5), calls=%async_computation.2 | async-start | bytes 1048576 | tf_op jit(solution)/shard_map/all_to_all | solution.py:189

commit v2 on v1

v2 whole, which is shorter than its diff:
```python
import math

import jax
import jax.numpy as jnp
import ml_dtypes
import numpy as np
from jax import lax
from jax.experimental import pallas as pl
from jax.experimental.pallas import tpu as pltpu
from jax.sharding import Mesh, PartitionSpec as P

OBJECT_RATE = 0.5
ROW = ("yh", "x", "core")
COL = ("z", "yl")
PLANE = ("yh", "x", "core", "yl")
DEEP = "z"
SIDE = 256
RIM = 128
WIDE = 2 * SIDE
F32 = jnp.float32
BF16 = jnp.bfloat16


def two_terms(table):
    high = table.astype(np.float32).astype(ml_dtypes.bfloat16)
    low = (table - high.astype(np.float64)).astype(np.float32).astype(ml_dtypes.bfloat16)
    return high, low


def spectral_tables():
    index = np.arange(SIDE)
    angles = (index[:, None] * index[None, :] % SIDE) * (2.0 * math.pi / SIDE)
    cos, sin = np.cos(angles) / 16.0, np.sin(angles) / 16.0
    left = np.concatenate(two_terms(np.concatenate([cos, sin], 1)), 1)
    right = np.concatenate(two_terms(np.block([[cos, -sin], [sin, cos]])), 0)
    return left, right


def split(value):
    high = value.astype(BF16)
    low = (value - high.astype(F32)).astype(BF16)
    return high, low


UNROLL = 3
STEP = 64
BLOCKS = [slice(k, k + STEP) for k in range(0, SIDE, STEP)]
VMEM_BYTES = 62 * 1024 * 1024


def slots_kernel(
    counts_ref, pos_ref, tile_ref, side_l_ref, side_r_ref, top_ref, bot_ref, ctop_ref, cbot_ref,
    probe_ref, intensity_ref, left_ref, right_ref,
    gprobe_out, gtop_out, gbot_out, gmid_out,
    ext_ref, over_ref, held_ref, leftv_ref, rightv_ref, shifted_ref, window_ref, stack_ref, rows_ref,
    mid_ref, far_ref, back_ref, grad_ref, gprobe_ref, sems, pattern_sems,
):
    dot = lambda a, b: jnp.dot(a, b, preferred_element_type=F32)
    low, own, high = slice(0, RIM), slice(RIM, RIM + SIDE), slice(RIM + SIDE, WIDE)
    moves = [
        (probe_ref, over_ref.at[:, 8 : 8 + SIDE]),
        (probe_ref.at[:, SIDE - 8 : SIDE], over_ref.at[:, 0:8]),
        (tile_ref, ext_ref.at[:, own, own]),
        (side_l_ref, ext_ref.at[:, own, low]),
        (side_r_ref, ext_ref.at[:, own, high]),
        (top_ref, ext_ref.at[:, low, own]),
        (bot_ref, ext_ref.at[:, high, own]),
        (ctop_ref.at[:, :, low], ext_ref.at[:, low, low]),
        (ctop_ref.at[:, :, RIM:SIDE], ext_ref.at[:, low, high]),
        (cbot_ref.at[:, :, low], ext_ref.at[:, high, low]),
        (cbot_ref.at[:, :, RIM:SIDE], ext_ref.at[:, high, high]),
        (left_ref, leftv_ref),
        (right_ref, rightv_ref),
    ]
    copies = [pltpu.make_async_copy(src, dst, sems.at[k]) for k, (src, dst) in enumerate(moves)]
    groups = (counts_ref[0] + UNROLL - 1) // UNROLL

    def patterns(group):
        some = pl.ds(group * UNROLL, UNROLL)
        return pltpu.make_async_copy(intensity_ref.at[some], held_ref.at[some], pattern_sems.at[group])

    for copy in copies:
        copy.start()
    lax.fori_loop(0, groups, lambda group, carry: (patterns(group).start(), carry)[1], 0)
    gprobe_ref[...] = jnp.zeros((2, SIDE, SIDE), F32)
    grad_ref[...] = jnp.zeros((2, WIDE, WIDE), F32)
    for copy in copies[:-2]:
        copy.wait()

    def put(u, rows, real, imag):
        real_high, real_low = split(real)
        imag_high, imag_low = split(imag)
        for base, re, im in ((0, real_high, imag_high), (WIDE, real_low, imag_low)):
            upper = slice(base + rows.start, base + rows.stop)
            lower = slice(base + SIDE + rows.start, base + SIDE + rows.stop)
            stack_ref[u, upper, 0:SIDE] = re
            stack_ref[u, upper, SIDE:] = im
            stack_ref[u, lower, 0:SIDE] = im
            stack_ref[u, lower, SIDE:] = -re

    def put_rows(u, rows, real, imag):
        for base, part in ((0, real), (SIDE, imag)):
            high_part, low_part = split(part)
            rows_ref[u, rows, base : base + SIDE] = high_part
            rows_ref[u, rows, WIDE + base : WIDE + base + SIDE] = low_part

    def by_rows(u):
        lh, ll = leftv_ref[:, 0:WIDE], leftv_ref[:, WIDE:]
        xh, xl = stack_ref[u, 0:WIDE], stack_ref[u, WIDE:]
        return dot(lh, xh) + (dot(lh, xl) + dot(ll, xh))

    def by_cols(u):
        xh, xl = rows_ref[u, :, 0:WIDE], rows_ref[u, :, WIDE:]
        rh, rl = rightv_ref[0:WIDE], rightv_ref[WIDE:]
        return dot(xh, rh) + (dot(xl, rh) + dot(xh, rl))

    def one_group(group, carry):
        lanes = lambda n: lax.broadcasted_iota(jnp.int32, (n, RIM), 1)
        first_rows = lax.broadcasted_iota(jnp.int32, (8, RIM), 0)
        slots = [group * UNROLL + u for u in range(UNROLL)]
        alive = [s < counts_ref[0] for s in slots]
        live = [jnp.where(a, 1.0, 0.0).astype(F32) for a in alive]
        row = [jnp.where(a, pos_ref[2 * s], 0) + RIM for s, a in zip(slots, alive)]
        col = [jnp.where(a, pos_ref[2 * s + 1], 0) + RIM for s, a in zip(slots, alive)]
        down = [r & 7 for r in row]
        right = [c & (RIM - 1) for c in col]
        row = [pl.multiple_of(r - d, 8) for r, d in zip(row, down)]
        col = [pl.multiple_of(c - d, RIM) for c, d in zip(col, right)]
        strips = [[pl.ds(pl.multiple_of(c + k * RIM, RIM), RIM) for k in range(3)] for c in col]
        pieces = [(0, 8)] + [(8, STEP - 8)] + [(k, STEP) for k in range(STEP, SIDE, STEP)]

        def at(u, start, count):
            return pl.ds(pl.multiple_of(row[u] + start, 8), count)

        for u in range(UNROLL):
            for start, count in pieces:
                rows = slice(start, start + count)
                for c in range(2):
                    three = [ext_ref[c, at(u, start, count), strip] for strip in strips[u]]
                    if start == 0:
                        wrapped = [ext_ref[c, at(u, SIDE, 8), strip] for strip in strips[u]]
                        three = [jnp.where(first_rows >= down[u], a, b) for a, b in zip(three, wrapped)]
                    window_ref[u, c, rows, 0:RIM] = jnp.where(lanes(count) >= right[u], three[0], three[2])
                    window_ref[u, c, rows, RIM:] = three[1]
            for rows in BLOCKS:
                for c in range(2):
                    turned = pltpu.roll(over_ref[c, rows.start : rows.stop + 8], STEP + down[u], 0)[0:STEP]
                    shifted_ref[u, c, rows] = pltpu.roll(turned, right[u], 1)
                pr, pi = shifted_ref[u, 0, rows], shifted_ref[u, 1, rows]
                wr, wi = window_ref[u, 0, rows], window_ref[u, 1, rows]
                put(u, rows, pr * wr - pi * wi, pr * wi + pi * wr)
            mid_ref[u] = by_rows(u)
        for u in range(UNROLL):
            for rows in BLOCKS:
                put_rows(u, rows, mid_ref[u, rows, 0:SIDE], mid_ref[u, rows, SIDE:])
            far_ref[u] = by_cols(u)
        patterns(group).wait()
        for u in range(UNROLL):
            for rows in BLOCKS:
                far_real, far_imag = far_ref[u, rows, 0:SIDE], far_ref[u, rows, SIDE:]
                misfit = far_real * far_real + far_imag * far_imag - held_ref[slots[u], rows]
                misfit = misfit * live[u]
                put_rows(u, rows, misfit * far_real, -misfit * far_imag)
            mid_ref[u] = by_cols(u)
        for u in range(UNROLL):
            for rows in BLOCKS:
                put(u, rows, mid_ref[u, rows, 0:SIDE], mid_ref[u, rows, SIDE:])
            mid_ref[u] = by_rows(u)
        for u in range(UNROLL):
            for start, count in pieces:
                rows = slice(start, start + count)
                br, bi = mid_ref[u, rows, 0:SIDE], -mid_ref[u, rows, SIDE:]
                pr, pi = shifted_ref[u, 0, rows], shifted_ref[u, 1, rows]
                wr, wi = window_ref[u, 0, rows], window_ref[u, 1, rows]
                here = lanes(count) >= right[u]
                for c, grad in enumerate((pr * br + pi * bi, pr * bi - pi * br)):
                    left_part = grad[:, 0:RIM]
                    three = [jnp.where(here, left_part, 0.0), grad[:, RIM:], jnp.where(here, 0.0, left_part)]
                    for part, strip in zip(three, strips[u]):
                        if start == 0:
                            near = first_rows >= down[u]
                            grad_ref[c, at(u, SIDE, 8), strip] += jnp.where(near, 0.0, part)
                            part = jnp.where(near, part, 0.0)
                        grad_ref[c, at(u, start, count), strip] += part
                for c, grad in enumerate((wr * br + wi * bi, wr * bi - wi * br)):
                    back_ref[u, c, rows] = grad
                    if start == 0:
                        back_ref[u, c, SIDE : SIDE + 8] = grad
            for rows in BLOCKS:
                for c in range(2):
                    back = jnp.where(down[u] == 0, 0, STEP + 8 - down[u])
                    turned = pltpu.roll(back_ref[u, c, rows.start : rows.stop + 8], back, 0)[0:STEP]
                    gprobe_ref[c, rows] += pltpu.roll(turned, (SIDE - right[u]) & (SIDE - 1), 1)
        return carry

    for copy in copies[-2:]:
        copy.wait()
    lax.fori_loop(0, groups, one_group, 0)
    moves = [
        (gprobe_ref, gprobe_out),
        (grad_ref.at[:, low], gtop_out),
        (grad_ref.at[:, high], gbot_out),
        (grad_ref.at[:, own], gmid_out),
    ]
    copies = [pltpu.make_async_copy(src, dst, sems.at[k]) for k, (src, dst) in enumerate(moves)]
    for copy in copies:
        copy.start()
    for copy in copies:
        copy.wait()


def all_slots(counts, positions, *arrays):
    smem = pl.BlockSpec(memory_space=pltpu.SMEM)
    anywhere = pl.BlockSpec(memory_space=pl.ANY)
    return pl.pallas_call(
        slots_kernel,
        out_shape=[
            jax.ShapeDtypeStruct((2, SIDE, SIDE), F32),
            jax.ShapeDtypeStruct((2, RIM, WIDE), F32),
            jax.ShapeDtypeStruct((2, RIM, WIDE), F32),
            jax.ShapeDtypeStruct((2, SIDE, WIDE), F32),
        ],
        in_specs=[smem, smem] + [anywhere] * len(arrays),
        out_specs=[anywhere] * 4,
        scratch_shapes=[
            pltpu.VMEM((2, WIDE, WIDE), F32),
            pltpu.VMEM((2, SIDE + 8, SIDE), F32),
            pltpu.VMEM((6, SIDE, SIDE), F32),
            pltpu.VMEM((SIDE, 2 * WIDE), BF16),
            pltpu.VMEM((2 * WIDE, WIDE), BF16),
            pltpu.VMEM((UNROLL, 2, SIDE, SIDE), F32),
            pltpu.VMEM((UNROLL, 2, SIDE, SIDE), F32),
            pltpu.VMEM((UNROLL, 2 * WIDE, WIDE), BF16),
            pltpu.VMEM((UNROLL, SIDE, 2 * WIDE), BF16),
            pltpu.VMEM((UNROLL, SIDE, WIDE), F32),
            pltpu.VMEM((UNROLL, SIDE, WIDE), F32),
            pltpu.VMEM((UNROLL, 2, SIDE + 8, SIDE), F32),
            pltpu.VMEM((2, WIDE, WIDE), F32),
            pltpu.VMEM((2, SIDE, SIDE), F32),
            pltpu.SemaphoreType.DMA((13,)),
            pltpu.SemaphoreType.DMA((6 // UNROLL,)),
        ],
        compiler_params=pltpu.CompilerParams(vmem_limit_bytes=VMEM_BYTES),
        cost_estimate=pl.CostEstimate(flops=10_000_000_000, bytes_accessed=20_000_000, transcendentals=0),
    )(counts, positions, *arrays)


def shifted(block, axes, distance):
    count = lax.axis_size(axes)
    route = [(i, i + distance) for i in range(count) if 0 <= i + distance < count]
    return lax.ppermute(block, axes, route)


def swap(pieces, axes):
    return lax.all_to_all(pieces, axes, split_axis=0, concat_axis=0, tiled=True)


def spread(block, axes):
    count = lax.axis_size(axes)
    return swap(jnp.broadcast_to(block[None], (count,) + block.shape), axes)


def summed_everywhere(grad):
    count = lax.axis_size(PLANE)
    pieces = swap(grad.reshape(count, 2 * SIDE // count, SIDE), PLANE)
    part = spread(jnp.sum(pieces, axis=0), DEEP)
    whole = spread(jnp.sum(part, axis=0), PLANE)
    return whole.reshape(2, SIDE, SIDE)


def shards(object_field, probe_field, intensity, positions, counts):
    tables = [jnp.asarray(t) for t in spectral_tables()]
    side_l = shifted(object_field[:, :, RIM:], COL, 1)
    side_r = shifted(object_field[:, :, :RIM], COL, -1)
    top = shifted(object_field[:, RIM:], ROW, 1)
    bottom = shifted(object_field[:, :RIM], ROW, -1)
    sides = jnp.concatenate([side_l, side_r], axis=2)
    corner_top = shifted(sides[:, RIM:], ROW, 1)
    corner_bottom = shifted(sides[:, :RIM], ROW, -1)
    grad_probe, grad_top, grad_bottom, grad_mid = all_slots(
        counts.reshape(1),
        positions.reshape(-1),
        object_field,
        side_l,
        side_r,
        top,
        bottom,
        corner_top,
        corner_bottom,
        probe_field,
        intensity[0, 0],
        *tables,
    )
    from_above = shifted(grad_bottom, ROW, 1)
    from_below = shifted(grad_top, ROW, -1)
    probe_gradient = summed_everywhere(grad_probe)
    rows = grad_mid + jnp.concatenate([from_above, from_below], axis=1)
    from_left = shifted(rows[:, :, RIM + SIDE :], COL, 1)
    from_right = shifted(rows[:, :, :RIM], COL, -1)
    gathered = rows[:, :, RIM : RIM + SIDE] + jnp.concatenate([from_left, from_right], axis=2)
    total_slots = lax.axis_size(ROW) * lax.axis_size(COL) * positions.shape[2]
    probe_update = probe_gradient * (1.0 / math.sqrt(total_slots))
    object_new = object_field - OBJECT_RATE * gathered
    return (object_new, probe_update)


def solution(mesh):
    chips = Mesh(mesh.devices.reshape(2, 4, 2, 16, 2), ("yh", "x", "core", "z", "yl"))
    placed = (
        P(None, ROW, COL),
        P(),
        P(ROW, COL, None, None, None),
        P(ROW, COL, None, None),
        P(ROW, COL),
    )
    return jax.shard_map(
        shards, mesh=chips, in_specs=placed, out_specs=(P(None, ROW, COL), P()), check_vma=False
    )
```

time: 142 us -> 124 us (0.87)
  local copies, waits for them, and re-layouts: 17.8 us -> 5.2 us
  starting transfers between devices: 80.4 us -> 70.5 us
  waiting for transfers between devices: 23.4 us -> 26.1 us
  Pallas kernels: 15 us -> 17.7 us
    unnamed x34 -> x20, local copies, waits for them, and re-layouts: 13.1 us -> 0.83 us
    all_to_all x3, starting transfers between devices: 51.2 us -> 41.1 us  [swap(): return lax.all_to_all(pieces, axes, split_axis=0, concat_axis=0, tiled=True)]
    pallas_call x1, Pallas kernels: 15 us -> 17.7 us  [all_slots(): pl.pallas_call(slots_kernel, out_shape=[jax.ShapeDtypeStruct((2, SIDE, SI...]
    all_to_all x3, waiting for transfers between devices: 22.3 us -> 24.1 us  [swap(): return lax.all_to_all(pieces, axes, split_axis=0, concat_axis=0, tiled=True)]
where the time goes in v2:
time: 124 us; the launch traced here: 123 us
  starting transfers between devices  70.5 us (57%)
  waiting for transfers between devices  26.1 us (21%)
  Pallas kernels  17.7 us (14%)
  local copies, waits for them, and re-layouts  5.2 us (4%)
  other arithmetic  2 us (2%)
  between operations  1.59 us (1%)
    all_to_all x3, starting transfers between devices, swap(): return lax.all_to_all(pieces, axes, split_axis=0, concat_axis=0, tiled=True)  41.1 us
    ppermute x10, starting transfers between devices, shifted(): return lax.ppermute(block, axes, route)  29.4 us
    all_to_all x3, waiting for transfers between devices, swap(): return lax.all_to_all(pieces, axes, split_axis=0, concat_axis=0, tiled=True)  24.1 us
    pallas_call x1, Pallas kernels, all_slots(): pl.pallas_call(slots_kernel, out_shape=[jax.ShapeDtypeStruct((2, SIDE, SI...  17.7 us
  transfers between devices with their start and end apart: 13, of which 5 were waited for; matrix products, arithmetic and copies ran while one was open for 4% of the time, Pallas kernels for 0%

profile of v2, /device:TPU:1, one launch (start us, length us, event | category | flops | bytes accessed | tf_op | source)
XLA Modules:
  0.0 123.2 jit_solution(10798039474996955819)
XLA Ops:
  0.6 1.1 fusion.5
  1.7 4.0 %collective-permute-start = (f32[2,256,128]{2,1,0:T(8,128)S(1)}, f32[2,256,128]{2,1,0:T(8,128)S(1)}, u32[]{:S(2)}, u32[]{:S(2)}) collective-permute-start(f32[2,256,128]{2,1,0:T(8,128)S(1)} %get-tuple-element.17), channel_id=1, source_target_pairs={{0,1},{1,2},{2,3},{3,4},{4,5},{5,6},{6,7},{7,8},{8,9},{9,10},{10,1... | collective-permute-start | bytes 786440 | tf_op jit(solution)/shard_map/ppermute | solution.py:251
  5.8 0.0 copy-start.4
  5.8 1.3 %collective-permute-start.1 = (f32[2,256,128]{2,1,0:T(8,128)S(1)}, f32[2,256,128]{2,1,0:T(8,128)S(1)}, u32[]{:S(2)}, u32[]{:S(2)}) collective-permute-start(f32[2,256,128]{2,1,0:T(8,128)S(1)} %get-tuple-element.16), channel_id=1, source_target_pairs={{1,0},{2,1},{3,2},{4,3},{5,4},{6,5},{7,6},{8,7},{9,8},{10,9},{11,1... | collective-permute-start | bytes 786440 | tf_op jit(solution)/shard_map/ppermute | solution.py:251
  7.1 1.1 fusion.4
  8.1 6.0 %collective-permute-start.3 = (f32[2,128,256]{2,1,0:T(8,128)S(1)}, f32[2,128,256]{2,1,0:T(8,128)S(1)}, u32[]{:S(2)}, u32[]{:S(2)}) collective-permute-start(f32[2,128,256]{2,1,0:T(8,128)S(1)} %get-tuple-element.14), channel_id=1, source_target_pairs={{32,0},{64,32},{96,64},{128,96},{160,128},{192,160},{224,192},{256... | collective-permute-start | bytes 786440 | tf_op jit(solution)/shard_map/ppermute | solution.py:251
  14.2 1.9 %collective-permute-start.2 = (f32[2,128,256]{2,1,0:T(8,128)S(1)}, f32[2,128,256]{2,1,0:T(8,128)S(1)}, u32[]{:S(2)}, u32[]{:S(2)}) collective-permute-start(f32[2,128,256]{2,1,0:T(8,128)S(1)} %get-tuple-element.15), channel_id=1, source_target_pairs={{0,32},{32,64},{64,96},{96,128},{128,160},{160,192},{192,224},{224... | collective-permute-start | bytes 786440 | tf_op jit(solution)/shard_map/ppermute | solution.py:251
  16.2 0.0 collective-permute-done.1.side_r_ref
  16.3 5.1 %collective-permute-start.5 = (f32[2,128,256]{2,1,0:T(8,128)S(1)}, f32[2,128,256]{2,1,0:T(8,128)S(1)}, u32[]{:S(2)}, u32[]{:S(2)}) collective-permute-start(f32[2,128,256]{2,1,0:T(8,128)S(1)} %get-tuple-element.12), channel_id=1, source_target_pairs={{32,0},{64,32},{96,64},{128,96},{160,128},{192,160},{224,192},{256... | collective-permute-start | bytes 786440 | tf_op jit(solution)/shard_map/ppermute | solution.py:251
  21.4 1.9 %collective-permute-start.4 = (f32[2,128,256]{2,1,0:T(8,128)S(1)}, f32[2,128,256]{2,1,0:T(8,128)S(1)}, u32[]{:S(2)}, u32[]{:S(2)}) collective-permute-start(f32[2,128,256]{2,1,0:T(8,128)S(1)} %get-tuple-element.13), channel_id=1, source_target_pairs={{0,32},{32,64},{64,96},{96,128},{128,160},{160,192},{192,224},{224... | collective-permute-start | bytes 786440 | tf_op jit(solution)/shard_map/ppermute | solution.py:251
  24.0 0.1 copy.11
  24.1 0.6 reshape.19.pos_ref
  24.7 0.4 collective-permute-done.5.cbot_ref
  25.0 1.6 %collective-permute-done.4.ctop_ref = f32[2,128,256]{2,1,0:T(8,128)S(1)} collective-permute-done((f32[2,128,256]{2,1,0:T(8,128)S(1)}, f32[2,128,256]{2,1,0:T(8,128)S(1)}, u32[]{:S(2)}, u32[]{:S(2)}) %collective-permute-start.4) | collective-permute-done | bytes 262176 | tf_op jit(solution)/shard_map/ppermute | solution.py:251
  26.7 0.7 copy-done.8
  27.3 17.7 %shard_map.86 = (f32[2,256,256]{2,1,0:T(8,128)}, f32[2,128,512]{2,1,0:T(8,128)}, f32[2,128,512]{2,1,0:T(8,128)}, f32[2,256,512]{2,1,0:T(8,128)}) custom-call(s32[1]{0:T(128)} %bitcast.4.counts_ref, s32[12]{0:T(128)} %reshape.19.pos_ref, f32[2,256,256]{2,1,0:T(8,128)} %tile_ref.1, f32[2,256,128]{2,1,0:T(8,128)} %copy-done.2, f32[2,256,128]{2,1,0:T(8,128)} %copy-done.3, ...), custom_call_target="tpu_custom_call" | custom-call | flops 10000000000 | bytes 20000000 | tf_op jit(solution)/shard_map/pallas_call | solution.py:215
  45.1 11.5 %all-to-all-start = ((f32[32,16,256]{2,1,0:T(8,128)}), f32[32,16,256]{2,1,0:T(8,128)S(1)}, u32[]{:S(2)}, u32[]{:S(2)}) async-start(f32[32,16,256]{2,1,0:T(8,128)} %bitcast.5), calls=%async_computation | async-start | bytes 1048576 | tf_op jit(solution)/shard_map/all_to_all | solution.py:255
  56.6 3.5 %collective-permute-start.6 = (f32[2,128,512]{2,1,0:T(8,128)}, f32[2,128,512]{2,1,0:T(8,128)S(1)}, u32[]{:S(2)}, u32[]{:S(2)}) collective-permute-start(f32[2,128,512]{2,1,0:T(8,128)} %get-tuple-element.7), channel_id=1, source_target_pairs={{0,32},{32,64},{64,96},{96,128},{128,160},{160,192},{192,224},{224... | collective-permute-start | bytes 1572872 | tf_op jit(solution)/shard_map/ppermute | solution.py:251
  60.2 1.9 %collective-permute-start.7 = (f32[2,128,512]{2,1,0:T(8,128)}, f32[2,128,512]{2,1,0:T(8,128)S(1)}, u32[]{:S(2)}, u32[]{:S(2)}) collective-permute-start(f32[2,128,512]{2,1,0:T(8,128)} %get-tuple-element.8), channel_id=1, source_target_pairs={{32,0},{64,32},{96,64},{128,96},{160,128},{192,160},{224,192},{256... | collective-permute-start | bytes 1572872 | tf_op jit(solution)/shard_map/ppermute | solution.py:251
  62.1 5.4 %all-to-all-done = f32[32,16,256]{2,1,0:T(8,128)S(1)} async-done(((f32[32,16,256]{2,1,0:T(8,128)}), f32[32,16,256]{2,1,0:T(8,128)S(1)}, u32[]{:S(2)}, u32[]{:S(2)}) %all-to-all-start) | async-done | bytes 524320 | tf_op jit(solution)/shard_map/all_to_all | solution.py:255
  67.5 0.7 broadcast_in_dim.4
  68.2 16.6 %all-to-all-start.1 = ((f32[16,16,256]{2,1,0:T(8,128)}), f32[16,16,256]{2,1,0:T(8,128)S(1)}, u32[]{:S(2)}, u32[]{:S(2)}) async-start(f32[16,16,256]{2,1,0:T(8,128)} %broadcast_in_dim.4), calls=%async_computation.1 | async-start | bytes 524288 | tf_op jit(solution)/shard_map/all_to_all | solution.py:255
  84.8 0.2 maximum_add_fusion
  85.0 0.0 copy-start
  85.1 2.3 %collective-permute-start.8 = (f32[2,256,128]{2,1,0:T(8,128)S(1)}, f32[2,256,128]{2,1,0:T(8,128)S(1)}, u32[]{:S(2)}, u32[]{:S(2)}) collective-permute-start(f32[2,256,128]{2,1,0:T(8,128)S(1)} %get-tuple-element.10), channel_id=1, source_target_pairs={{0,1},{1,2},{2,3},{3,4},{4,5},{5,6},{6,7},{7,8},{8,9},{9,10},{10,1... | collective-permute-start | bytes 786440 | tf_op jit(solution)/shard_map/ppermute | solution.py:251
  87.4 1.3 %collective-permute-start.9 = (f32[2,256,128]{2,1,0:T(8,128)S(1)}, f32[2,256,128]{2,1,0:T(8,128)S(1)}, u32[]{:S(2)}, u32[]{:S(2)}) collective-permute-start(f32[2,256,128]{2,1,0:T(8,128)S(1)} %get-tuple-element.11), channel_id=1, source_target_pairs={{1,0},{2,1},{3,2},{4,3},{5,4},{6,5},{7,6},{8,7},{9,8},{10,9},{11,1... | collective-permute-start | bytes 786440 | tf_op jit(solution)/shard_map/ppermute | solution.py:251
  88.7 8.8 %all-to-all-done.1 = f32[16,16,256]{2,1,0:T(8,128)S(1)} async-done(((f32[16,16,256]{2,1,0:T(8,128)}), f32[16,16,256]{2,1,0:T(8,128)S(1)}, u32[]{:S(2)}, u32[]{:S(2)}) %all-to-all-start.1) | async-done | bytes 262176 | tf_op jit(solution)/shard_map/all_to_all | solution.py:255
  97.6 0.9 broadcast_in_dim.5
  98.5 13.0 %all-to-all-start.2 = ((f32[32,16,256]{2,1,0:T(8,128)}), f32[32,16,256]{2,1,0:T(8,128)S(1)}, u32[]{:S(2)}, u32[]{:S(2)}) async-start(f32[32,16,256]{2,1,0:T(8,128)} %broadcast_in_dim.5), calls=%async_computation.2 | async-start | bytes 1048576 | tf_op jit(solution)/shard_map/all_to_all | solution.py:255
  111.5 0.9 fusion.1
  112.4 9.9 %all-to-all-done.2 = f32[32,16,256]{2,1,0:T(8,128)S(1)} async-done(((f32[32,16,256]{2,1,0:T(8,128)}), f32[32,16,256]{2,1,0:T(8,128)S(1)}, u32[]{:S(2)}, u32[]{:S(2)}) %all-to-all-start.2) | async-done | bytes 524320 | tf_op jit(solution)/shard_map/all_to_all | solution.py:255
  122.3 0.8 broadcast_multiply_fusion
  (28 shorter events, 0.2 us)
Async XLA Ops:
  1.7 14.4 %collective-permute-start = (f32[2,256,128]{2,1,0:T(8,128)S(1)}, f32[2,256,128]{2,1,0:T(8,128)S(1)}, u32[]{:S(2)}, u32[]{:S(2)}) collective-permute-start(f32[2,256,128]{2,1,0:T(8,128)S(1)} %get-tuple-element.17), channel_id=1, source_target_pairs={{0,1},{1,2},{2,3},{3,4},{4,5},{5,6},{6,7},{7,8},{8,9},{9,10},{10,1... | collective-permute-start | bytes 786440 | tf_op jit(solution)/shard_map/ppermute | solution.py:251
  5.8 18.2 %copy-start.4 = (s32[1,1,6,2]{2,3,1,0:T(2,128)S(1)}, s32[1,1,6,2]{2,3,1,0:T(2,128)}, u32[]{:S(2)}) copy-start(s32[1,1,6,2]{2,3,1,0:T(2,128)} %param.10) | copy-start | bytes 148
  5.8 10.4 %collective-permute-start.1 = (f32[2,256,128]{2,1,0:T(8,128)S(1)}, f32[2,256,128]{2,1,0:T(8,128)S(1)}, u32[]{:S(2)}, u32[]{:S(2)}) collective-permute-start(f32[2,256,128]{2,1,0:T(8,128)S(1)} %get-tuple-element.16), channel_id=1, source_target_pairs={{1,0},{2,1},{3,2},{4,3},{5,4},{6,5},{7,6},{8,7},{9,8},{10,9},{11,1... | collective-permute-start | bytes 786440 | tf_op jit(solution)/shard_map/ppermute | solution.py:251
  8.1 16.5 %collective-permute-start.3 = (f32[2,128,256]{2,1,0:T(8,128)S(1)}, f32[2,128,256]{2,1,0:T(8,128)S(1)}, u32[]{:S(2)}, u32[]{:S(2)}) collective-permute-start(f32[2,128,256]{2,1,0:T(8,128)S(1)} %get-tuple-element.14), channel_id=1, source_target_pairs={{32,0},{64,32},{96,64},{128,96},{160,128},{192,160},{224,192},{256... | collective-permute-start | bytes 786440 | tf_op jit(solution)/shard_map/ppermute | solution.py:251
  14.2 10.5 %collective-permute-start.2 = (f32[2,128,256]{2,1,0:T(8,128)S(1)}, f32[2,128,256]{2,1,0:T(8,128)S(1)}, u32[]{:S(2)}, u32[]{:S(2)}) collective-permute-start(f32[2,128,256]{2,1,0:T(8,128)S(1)} %get-tuple-element.15), channel_id=1, source_target_pairs={{0,32},{32,64},{64,96},{96,128},{128,160},{160,192},{192,224},{224... | collective-permute-start | bytes 786440 | tf_op jit(solution)/shard_map/ppermute | solution.py:251
  16.1 10.5 %copy-start.2 = (f32[2,256,128]{2,1,0:T(8,128)}, f32[2,256,128]{2,1,0:T(8,128)S(1)}, u32[]{:S(2)}) copy-start(f32[2,256,128]{2,1,0:T(8,128)S(1)} %collective-permute-done.side_l_ref) | copy-start | bytes 786436
  16.2 10.4 %copy-start.3 = (f32[2,256,128]{2,1,0:T(8,128)}, f32[2,256,128]{2,1,0:T(8,128)S(1)}, u32[]{:S(2)}) copy-start(f32[2,256,128]{2,1,0:T(8,128)S(1)} %collective-permute-done.1.side_r_ref) | copy-start | bytes 786436
  16.3 8.8 %collective-permute-start.5 = (f32[2,128,256]{2,1,0:T(8,128)S(1)}, f32[2,128,256]{2,1,0:T(8,128)S(1)}, u32[]{:S(2)}, u32[]{:S(2)}) collective-permute-start(f32[2,128,256]{2,1,0:T(8,128)S(1)} %get-tuple-element.12), channel_id=1, source_target_pairs={{32,0},{64,32},{96,64},{128,96},{160,128},{192,160},{224,192},{256... | collective-permute-start | bytes 786440 | tf_op jit(solution)/shard_map/ppermute | solution.py:251
  21.4 5.2 %collective-permute-start.4 = (f32[2,128,256]{2,1,0:T(8,128)S(1)}, f32[2,128,256]{2,1,0:T(8,128)S(1)}, u32[]{:S(2)}, u32[]{:S(2)}) collective-permute-start(f32[2,128,256]{2,1,0:T(8,128)S(1)} %get-tuple-element.13), channel_id=1, source_target_pairs={{0,32},{32,64},{64,96},{96,128},{128,160},{160,192},{192,224},{224... | collective-permute-start | bytes 786440 | tf_op jit(solution)/shard_map/ppermute | solution.py:251
  24.6 2.0 %copy-start.5 = (f32[2,128,256]{2,1,0:T(8,128)}, f32[2,128,256]{2,1,0:T(8,128)S(1)}, u32[]{:S(2)}) copy-start(f32[2,128,256]{2,1,0:T(8,128)S(1)} %collective-permute-done.3.bot_ref) | copy-start | bytes 786436
  24.6 2.0 %copy-start.6 = (f32[2,128,256]{2,1,0:T(8,128)}, f32[2,128,256]{2,1,0:T(8,128)S(1)}, u32[]{:S(2)}) copy-start(f32[2,128,256]{2,1,0:T(8,128)S(1)} %collective-permute-done.2.top_ref) | copy-start | bytes 786436
  25.0 1.6 %copy-start.7 = (f32[2,128,256]{2,1,0:T(8,128)}, f32[2,128,256]{2,1,0:T(8,128)S(1)}, u32[]{:S(2)}) copy-start(f32[2,128,256]{2,1,0:T(8,128)S(1)} %collective-permute-done.5.cbot_ref) | copy-start | bytes 786436
  26.6 0.7 copy-start.8
  45.1 39.7 %copy-start.1 = (f32[2,256,512]{2,1,0:T(8,128)S(1)}, f32[2,256,512]{2,1,0:T(8,128)}, u32[]{:S(2)}) copy-start(f32[2,256,512]{2,1,0:T(8,128)} %get-tuple-element.6) | copy-start | bytes 3145732
  45.1 22.4 %all-to-all-start = ((f32[32,16,256]{2,1,0:T(8,128)}), f32[32,16,256]{2,1,0:T(8,128)S(1)}, u32[]{:S(2)}, u32[]{:S(2)}) async-start(f32[32,16,256]{2,1,0:T(8,128)} %bitcast.5), calls=%async_computation | async-start | bytes 1048576 | tf_op jit(solution)/shard_map/all_to_all | solution.py:255
  56.6 28.2 %collective-permute-start.6 = (f32[2,128,512]{2,1,0:T(8,128)}, f32[2,128,512]{2,1,0:T(8,128)S(1)}, u32[]{:S(2)}, u32[]{:S(2)}) collective-permute-start(f32[2,128,512]{2,1,0:T(8,128)} %get-tuple-element.7), channel_id=1, source_target_pairs={{0,32},{32,64},{64,96},{96,128},{128,160},{160,192},{192,224},{224... | collective-permute-start | bytes 1572872 | tf_op jit(solution)/shard_map/ppermute | solution.py:251
  60.2 24.6 %collective-permute-start.7 = (f32[2,128,512]{2,1,0:T(8,128)}, f32[2,128,512]{2,1,0:T(8,128)S(1)}, u32[]{:S(2)}, u32[]{:S(2)}) collective-permute-start(f32[2,128,512]{2,1,0:T(8,128)} %get-tuple-element.8), channel_id=1, source_target_pairs={{32,0},{64,32},{96,64},{128,96},{160,128},{192,160},{224,192},{256... | collective-permute-start | bytes 1572872 | tf_op jit(solution)/shard_map/ppermute | solution.py:251
  68.2 29.3 %all-to-all-start.1 = ((f32[16,16,256]{2,1,0:T(8,128)}), f32[16,16,256]{2,1,0:T(8,128)S(1)}, u32[]{:S(2)}, u32[]{:S(2)}) async-start(f32[16,16,256]{2,1,0:T(8,128)} %broadcast_in_dim.4), calls=%async_computation.1 | async-start | bytes 524288 | tf_op jit(solution)/shard_map/all_to_all | solution.py:255
  85.0 26.5 %copy-start = (f32[2,256,256]{2,1,0:T(8,128)S(1)}, f32[2,256,256]{2,1,0:T(8,128)}, u32[]{:S(2)}) copy-start(f32[2,256,256]{2,1,0:T(8,128)} %tile_ref.1) | copy-start | bytes 1572868
  85.1 26.4 %collective-permute-start.8 = (f32[2,256,128]{2,1,0:T(8,128)S(1)}, f32[2,256,128]{2,1,0:T(8,128)S(1)}, u32[]{:S(2)}, u32[]{:S(2)}) collective-permute-start(f32[2,256,128]{2,1,0:T(8,128)S(1)} %get-tuple-element.10), channel_id=1, source_target_pairs={{0,1},{1,2},{2,3},{3,4},{4,5},{5,6},{6,7},{7,8},{8,9},{9,10},{10,1... | collective-permute-start | bytes 786440 | tf_op jit(solution)/shard_map/ppermute | solution.py:251
  87.4 24.1 %collective-permute-start.9 = (f32[2,256,128]{2,1,0:T(8,128)S(1)}, f32[2,256,128]{2,1,0:T(8,128)S(1)}, u32[]{:S(2)}, u32[]{:S(2)}) collective-permute-start(f32[2,256,128]{2,1,0:T(8,128)S(1)} %get-tuple-element.11), channel_id=1, source_target_pairs={{1,0},{2,1},{3,2},{4,3},{5,4},{6,5},{7,6},{8,7},{9,8},{10,9},{11,1... | collective-permute-start | bytes 786440 | tf_op jit(solution)/shard_map/ppermute | solution.py:251
  98.5 23.9 %all-to-all-start.2 = ((f32[32,16,256]{2,1,0:T(8,128)}), f32[32,16,256]{2,1,0:T(8,128)S(1)}, u32[]{:S(2)}, u32[]{:S(2)}) async-start(f32[32,16,256]{2,1,0:T(8,128)} %broadcast_in_dim.5), calls=%async_computation.2 | async-start | bytes 1048576 | tf_op jit(solution)/shard_map/all_to_all | solution.py:255

commit v3 on v2

--- a/solution.py
+++ b/solution.py
@@ -31,9 +31,7 @@
     index = np.arange(SIDE)
     angles = (index[:, None] * index[None, :] % SIDE) * (2.0 * math.pi / SIDE)
     cos, sin = np.cos(angles) / 16.0, np.sin(angles) / 16.0
-    left = np.concatenate(two_terms(np.concatenate([cos, sin], 1)), 1)
-    right = np.concatenate(two_terms(np.block([[cos, -sin], [sin, cos]])), 0)
-    return left, right
+    return (np.concatenate(two_terms(np.concatenate([cos, sin], 1)), 1),)
 
 
 def split(value):
@@ -45,12 +43,11 @@
 UNROLL = 3
 STEP = 64
 BLOCKS = [slice(k, k + STEP) for k in range(0, SIDE, STEP)]
-VMEM_BYTES = 62 * 1024 * 1024
+VMEM_BYTES = 50 * 1024 * 1024
 
 
 def slots_kernel(
-    counts_ref, pos_ref, tile_ref, side_l_ref, side_r_ref, top_ref, bot_ref, ctop_ref, cbot_ref,
-    probe_ref, intensity_ref, left_ref, right_ref,
+    counts_ref, pos_ref, tile_ref, side_l_ref, side_r_ref, top_ref, bot_ref, probe_ref, intensity_ref, left_ref,
     gprobe_out, gtop_out, gbot_out, gmid_out,
     ext_ref, over_ref, held_ref, leftv_ref, rightv_ref, shifted_ref, window_ref, stack_ref, rows_ref,
     mid_ref, far_ref, back_ref, grad_ref, gprobe_ref, sems, pattern_sems,
@@ -63,14 +60,9 @@
         (tile_ref, ext_ref.at[:, own, own]),
         (side_l_ref, ext_ref.at[:, own, low]),
         (side_r_ref, ext_ref.at[:, own, high]),
-        (top_ref, ext_ref.at[:, low, own]),
-        (bot_ref, ext_ref.at[:, high, own]),
-        (ctop_ref.at[:, :, low], ext_ref.at[:, low, low]),
-        (ctop_ref.at[:, :, RIM:SIDE], ext_ref.at[:, low, high]),
-        (cbot_ref.at[:, :, low], ext_ref.at[:, high, low]),
-        (cbot_ref.at[:, :, RIM:SIDE], ext_ref.at[:, high, high]),
         (left_ref, leftv_ref),
-        (right_ref, rightv_ref),
+        (top_ref, ext_ref.at[:, low]),
+        (bot_ref, ext_ref.at[:, high]),
     ]
     copies = [pltpu.make_async_copy(src, dst, sems.at[k]) for k, (src, dst) in enumerate(moves)]
     groups = (counts_ref[0] + UNROLL - 1) // UNROLL
@@ -84,8 +76,14 @@
     lax.fori_loop(0, groups, lambda group, carry: (patterns(group).start(), carry)[1], 0)
     gprobe_ref[...] = jnp.zeros((2, SIDE, SIDE), F32)
     grad_ref[...] = jnp.zeros((2, WIDE, WIDE), F32)
-    for copy in copies[:-2]:
+    for copy in copies:
         copy.wait()
+    for k in range(2):
+        cos, sin = leftv_ref[:, k * WIDE : k * WIDE + SIDE], leftv_ref[:, k * WIDE + SIDE : (k + 1) * WIDE]
+        rightv_ref[k * WIDE : k * WIDE + SIDE, 0:SIDE] = cos
+        rightv_ref[k * WIDE : k * WIDE + SIDE, SIDE:] = -sin
+        rightv_ref[k * WIDE + SIDE : (k + 1) * WIDE, 0:SIDE] = sin
+        rightv_ref[k * WIDE + SIDE : (k + 1) * WIDE, SIDE:] = cos
 
     def put(u, rows, real, imag):
         real_high, real_low = split(real)
@@ -193,8 +191,6 @@
                     gprobe_ref[c, rows] += pltpu.roll(turned, (SIDE - right[u]) & (SIDE - 1), 1)
         return carry
 
-    for copy in copies[-2:]:
-        copy.wait()
     lax.fori_loop(0, groups, one_group, 0)
     moves = [
         (gprobe_ref, gprobe_out),
@@ -237,7 +233,7 @@
             pltpu.VMEM((UNROLL, 2, SIDE + 8, SIDE), F32),
             pltpu.VMEM((2, WIDE, WIDE), F32),
             pltpu.VMEM((2, SIDE, SIDE), F32),
-            pltpu.SemaphoreType.DMA((13,)),
+            pltpu.SemaphoreType.DMA((8,)),
             pltpu.SemaphoreType.DMA((6 // UNROLL,)),
         ],
         compiler_params=pltpu.CompilerParams(vmem_limit_bytes=VMEM_BYTES),
@@ -260,11 +256,11 @@
     return swap(jnp.broadcast_to(block[None], (count,) + block.shape), axes)
 
 
-def summed_everywhere(grad):
+def summed_everywhere(grad, scale):
     count = lax.axis_size(PLANE)
     pieces = swap(grad.reshape(count, 2 * SIDE // count, SIDE), PLANE)
     part = spread(jnp.sum(pieces, axis=0), DEEP)
-    whole = spread(jnp.sum(part, axis=0), PLANE)
+    whole = spread(jnp.sum(part, axis=0) * scale, PLANE)
     return whole.reshape(2, SIDE, SIDE)
 
 
@@ -272,11 +268,9 @@
     tables = [jnp.asarray(t) for t in spectral_tables()]
     side_l = shifted(object_field[:, :, RIM:], COL, 1)
     side_r = shifted(object_field[:, :, :RIM], COL, -1)
-    top = shifted(object_field[:, RIM:], ROW, 1)
-    bottom = shifted(object_field[:, :RIM], ROW, -1)
-    sides = jnp.concatenate([side_l, side_r], axis=2)
-    corner_top = shifted(sides[:, RIM:], ROW, 1)
-    corner_bottom = shifted(sides[:, :RIM], ROW, -1)
+    middle = jnp.concatenate([side_l, object_field, side_r], axis=2)
+    top = shifted(middle[:, RIM:], ROW, 1)
+    bottom = shifted(middle[:, :RIM], ROW, -1)
     grad_probe, grad_top, grad_bottom, grad_mid = all_slots(
         counts.reshape(1),
         positions.reshape(-1),
@@ -285,21 +279,18 @@
         side_r,
         top,
         bottom,
-        corner_top,
-        corner_bottom,
         probe_field,
         intensity[0, 0],
         *tables,
     )
     from_above = shifted(grad_bottom, ROW, 1)
     from_below = shifted(grad_top, ROW, -1)
-    probe_gradient = summed_everywhere(grad_probe)
+    total_slots = lax.axis_size(ROW) * lax.axis_size(COL) * positions.shape[2]
+    probe_update = summed_everywhere(grad_probe, 1.0 / math.sqrt(total_slots))
     rows = grad_mid + jnp.concatenate([from_above, from_below], axis=1)
     from_left = shifted(rows[:, :, RIM + SIDE :], COL, 1)
     from_right = shifted(rows[:, :, :RIM], COL, -1)
     gathered = rows[:, :, RIM : RIM + SIDE] + jnp.concatenate([from_left, from_right], axis=2)
-    total_slots = lax.axis_size(ROW) * lax.axis_size(COL) * positions.shape[2]
-    probe_update = probe_gradient * (1.0 / math.sqrt(total_slots))
     object_new = object_field - OBJECT_RATE * gathered
     return (object_new, probe_update)
 

time: 124 us -> 126 us (1.016)
  waiting for transfers between devices: 26.1 us -> 34.1 us
  starting transfers between devices: 70.5 us -> 67 us
  local copies, waits for them, and re-layouts: 5.2 us -> 3.89 us
  Pallas kernels: 17.7 us -> 16.4 us
    ppermute x10 -> x8, waiting for transfers between devices: 1.98 us -> 11 us  [shifted(): return lax.ppermute(block, axes, route)]
    ppermute x10 -> x8, starting transfers between devices: 29.4 us -> 24.7 us  [shifted(): return lax.ppermute(block, axes, route)]
    pallas_call x1, Pallas kernels: 17.7 us -> 16.4 us  [all_slots(): pl.pallas_call(slots_kernel, out_shape=[jax.ShapeDtypeStruct((2, SIDE, SI...]
  transfers between devices with their start and end apart: 13 -> 11, of which waited for: 5 -> 7; matrix products, arithmetic and copies ran while one was open for 4% -> 3% of each run, Pallas kernels for 0% -> 0%
where the time goes in v3:
time: 126 us; the launch traced here: 125 us
  starting transfers between devices  67 us (53%)
  waiting for transfers between devices  34.1 us (27%)
  Pallas kernels  16.4 us (13%)
  local copies, waits for them, and re-layouts  3.89 us (3%)
  other arithmetic  2.36 us (2%)
  between operations  1.52 us (1%)
    all_to_all x3, starting transfers between devices, swap(): return lax.all_to_all(pieces, axes, split_axis=0, concat_axis=0, tiled=True)  42.3 us
    ppermute x8, starting transfers between devices, shifted(): return lax.ppermute(block, axes, route)  24.7 us
    all_to_all x3, waiting for transfers between devices, swap(): return lax.all_to_all(pieces, axes, split_axis=0, concat_axis=0, tiled=True)  23.1 us
    pallas_call x1, Pallas kernels, all_slots(): pl.pallas_call(slots_kernel, out_shape=[jax.ShapeDtypeStruct((2, SIDE, SI...  16.4 us
    ppermute x8, waiting for transfers between devices, shifted(): return lax.ppermute(block, axes, route)  11 us
  transfers between devices with their start and end apart: 11, of which 7 were waited for; matrix products, arithmetic and copies ran while one was open for 3% of the time, Pallas kernels for 0%

profile of v3, /device:TPU:1, one launch (start us, length us, event | category | flops | bytes accessed | tf_op | source)
XLA Modules:
  0.0 125.3 jit_solution(5549371918533779667)
XLA Ops:
  0.6 1.1 fusion.4
  1.8 4.0 %collective-permute-start = (f32[2,256,128]{2,1,0:T(8,128)S(1)}, f32[2,256,128]{2,1,0:T(8,128)S(1)}, u32[]{:S(2)}, u32[]{:S(2)}) collective-permute-start(f32[2,256,128]{2,1,0:T(8,128)S(1)} %get-tuple-element.15), channel_id=1, source_target_pairs={{0,1},{1,2},{2,3},{3,4},{4,5},{5,6},{6,7},{7,8},{8,9},{9,10},{10,1... | collective-permute-start | bytes 786440 | tf_op jit(solution)/shard_map/ppermute | solution.py:247
  5.8 1.3 %collective-permute-start.1 = (f32[2,256,128]{2,1,0:T(8,128)S(1)}, f32[2,256,128]{2,1,0:T(8,128)S(1)}, u32[]{:S(2)}, u32[]{:S(2)}) collective-permute-start(f32[2,256,128]{2,1,0:T(8,128)S(1)} %get-tuple-element.14), channel_id=1, source_target_pairs={{1,0},{2,1},{3,2},{4,3},{5,4},{6,5},{7,6},{8,7},{9,8},{10,9},{11,1... | collective-permute-start | bytes 786440 | tf_op jit(solution)/shard_map/ppermute | solution.py:247
  7.1 2.0 %collective-permute-done.side_l_ref = f32[2,256,128]{2,1,0:T(8,128)S(1)} collective-permute-done((f32[2,256,128]{2,1,0:T(8,128)S(1)}, f32[2,256,128]{2,1,0:T(8,128)S(1)}, u32[]{:S(2)}, u32[]{:S(2)}) %collective-permute-start) | collective-permute-done | bytes 262176 | tf_op jit(solution)/shard_map/ppermute | solution.py:247
  9.1 0.1 constant_dynamic-update-slice_fusion.1
  9.2 0.0 copy-start.2
  9.2 3.8 %collective-permute-done.1.side_r_ref = f32[2,256,128]{2,1,0:T(8,128)S(1)} collective-permute-done((f32[2,256,128]{2,1,0:T(8,128)S(1)}, f32[2,256,128]{2,1,0:T(8,128)S(1)}, u32[]{:S(2)}, u32[]{:S(2)}) %collective-permute-start.1) | collective-permute-done | bytes 262176 | tf_op jit(solution)/shard_map/ppermute | solution.py:247
  13.0 0.1 fusion.3
  13.1 8.5 %collective-permute-start.3 = (f32[2,128,512]{2,1,0:T(8,128)S(1)}, f32[2,128,512]{2,1,0:T(8,128)S(1)}, u32[]{:S(2)}, u32[]{:S(2)}) collective-permute-start(f32[2,128,512]{2,1,0:T(8,128)S(1)} %get-tuple-element.12), channel_id=1, source_target_pairs={{32,0},{64,32},{96,64},{128,96},{160,128},{192,160},{224,192},{256... | collective-permute-start | bytes 1572872 | tf_op jit(solution)/shard_map/ppermute | solution.py:247
  21.6 1.9 %collective-permute-start.2 = (f32[2,128,512]{2,1,0:T(8,128)S(1)}, f32[2,128,512]{2,1,0:T(8,128)S(1)}, u32[]{:S(2)}, u32[]{:S(2)}) collective-permute-start(f32[2,128,512]{2,1,0:T(8,128)S(1)} %get-tuple-element.13), channel_id=1, source_target_pairs={{0,32},{32,64},{64,96},{96,128},{128,160},{160,192},{192,224},{224... | collective-permute-start | bytes 1572872 | tf_op jit(solution)/shard_map/ppermute | solution.py:247
  24.2 0.1 copy.10
  24.3 0.1 reshape.21.pos_ref
  24.3 3.7 %collective-permute-done.3.bot_ref = f32[2,128,512]{2,1,0:T(8,128)S(1)} collective-permute-done((f32[2,128,512]{2,1,0:T(8,128)S(1)}, f32[2,128,512]{2,1,0:T(8,128)S(1)}, u32[]{:S(2)}, u32[]{:S(2)}) %collective-permute-start.3) | collective-permute-done | bytes 524320 | tf_op jit(solution)/shard_map/ppermute | solution.py:247
  28.0 1.6 %collective-permute-done.2.top_ref = f32[2,128,512]{2,1,0:T(8,128)S(1)} collective-permute-done((f32[2,128,512]{2,1,0:T(8,128)S(1)}, f32[2,128,512]{2,1,0:T(8,128)S(1)}, u32[]{:S(2)}, u32[]{:S(2)}) %collective-permute-start.2) | collective-permute-done | bytes 524320 | tf_op jit(solution)/shard_map/ppermute | solution.py:247
  29.6 16.4 %shard_map.77 = (f32[2,256,256]{2,1,0:T(8,128)}, f32[2,128,512]{2,1,0:T(8,128)S(1)}, f32[2,128,512]{2,1,0:T(8,128)S(1)}, f32[2,256,512]{2,1,0:T(8,128)}) custom-call(s32[1]{0:T(128)} %bitcast.4.counts_ref, s32[12]{0:T(128)S(1)} %reshape.21.pos_ref, f32[2,256,256]{2,1,0:T(8,128)S(1)} %copy-done, f32[2,256,128]{2,1,0:T(8,128)S(1)} %collective-permute-done.side_l_ref, ...), custom_call_target="tpu_custom_call" | custom-call | flops 10000000000 | bytes 20000000 | tf_op jit(solution)/shard_map/pallas_call | solution.py:211
  46.0 7.6 %all-to-all-start = ((f32[32,16,256]{2,1,0:T(8,128)}), f32[32,16,256]{2,1,0:T(8,128)S(1)}, u32[]{:S(2)}, u32[]{:S(2)}) async-start(f32[32,16,256]{2,1,0:T(8,128)} %bitcast.2), calls=%async_computation | async-start | bytes 1048576 | tf_op jit(solution)/shard_map/all_to_all | solution.py:251
  53.6 3.5 %collective-permute-start.4 = (f32[2,128,512]{2,1,0:T(8,128)S(1)}, f32[2,128,512]{2,1,0:T(8,128)}, u32[]{:S(2)}, u32[]{:S(2)}) collective-permute-start(f32[2,128,512]{2,1,0:T(8,128)S(1)} %get-tuple-element.7), channel_id=1, source_target_pairs={{0,32},{32,64},{64,96},{96,128},{128,160},{160,192},{192,224},{224... | collective-permute-start | bytes 1572872 | tf_op jit(solution)/shard_map/ppermute | solution.py:247
  57.1 1.9 %collective-permute-start.5 = (f32[2,128,512]{2,1,0:T(8,128)S(1)}, f32[2,128,512]{2,1,0:T(8,128)}, u32[]{:S(2)}, u32[]{:S(2)}) collective-permute-start(f32[2,128,512]{2,1,0:T(8,128)S(1)} %get-tuple-element.8), channel_id=1, source_target_pairs={{32,0},{64,32},{96,64},{128,96},{160,128},{192,160},{224,192},{256... | collective-permute-start | bytes 1572872 | tf_op jit(solution)/shard_map/ppermute | solution.py:247
  59.1 5.4 %all-to-all-done = f32[32,16,256]{2,1,0:T(8,128)S(1)} async-done(((f32[32,16,256]{2,1,0:T(8,128)}), f32[32,16,256]{2,1,0:T(8,128)S(1)}, u32[]{:S(2)}, u32[]{:S(2)}) %all-to-all-start) | async-done | bytes 524320 | tf_op jit(solution)/shard_map/all_to_all | solution.py:251
  64.5 0.7 broadcast_in_dim.4
  65.2 21.7 %all-to-all-start.1 = ((f32[16,16,256]{2,1,0:T(8,128)}), f32[16,16,256]{2,1,0:T(8,128)S(1)}, u32[]{:S(2)}, u32[]{:S(2)}) async-start(f32[16,16,256]{2,1,0:T(8,128)} %broadcast_in_dim.4), calls=%async_computation.1 | async-start | bytes 524288 | tf_op jit(solution)/shard_map/all_to_all | solution.py:251
  86.9 0.0 collective-permute-done.5
  86.9 1.4 %maximum_add_fusion = f32[2,256,512]{2,1,0:T(8,128)S(1)} fusion(f32[2,256,512]{2,1,0:T(8,128)S(1)} %copy-done.1, f32[2,128,512]{2,1,0:T(8,128)} %collective-permute-done.5, f32[2,128,512]{2,1,0:T(8,128)} %collective-permute-done.4), kind=kLoop, calls=%fused_computation | loop fusion | flops 524288 | bytes 3145728 | tf_op jit(solution)/shard_map/add | solution.py:290
  88.4 2.2 %collective-permute-start.6 = (f32[2,256,128]{2,1,0:T(8,128)S(1)}, f32[2,256,128]{2,1,0:T(8,128)S(1)}, u32[]{:S(2)}, u32[]{:S(2)}) collective-permute-start(f32[2,256,128]{2,1,0:T(8,128)S(1)} %get-tuple-element.10), channel_id=1, source_target_pairs={{0,1},{1,2},{2,3},{3,4},{4,5},{5,6},{6,7},{7,8},{8,9},{9,10},{10,1... | collective-permute-start | bytes 786440 | tf_op jit(solution)/shard_map/ppermute | solution.py:247
  90.6 1.3 %collective-permute-start.7 = (f32[2,256,128]{2,1,0:T(8,128)S(1)}, f32[2,256,128]{2,1,0:T(8,128)S(1)}, u32[]{:S(2)}, u32[]{:S(2)}) collective-permute-start(f32[2,256,128]{2,1,0:T(8,128)S(1)} %get-tuple-element.11), channel_id=1, source_target_pairs={{1,0},{2,1},{3,2},{4,3},{5,4},{6,5},{7,6},{8,7},{9,8},{10,9},{11,1... | collective-permute-start | bytes 786440 | tf_op jit(solution)/shard_map/ppermute | solution.py:247
  91.9 7.8 %all-to-all-done.1 = f32[16,16,256]{2,1,0:T(8,128)S(1)} async-done(((f32[16,16,256]{2,1,0:T(8,128)}), f32[16,16,256]{2,1,0:T(8,128)S(1)}, u32[]{:S(2)}, u32[]{:S(2)}) %all-to-all-start.1) | async-done | bytes 262176 | tf_op jit(solution)/shard_map/all_to_all | solution.py:251
  99.7 0.9 broadcast_in_dim.5
  100.6 13.0 %all-to-all-start.2 = ((f32[32,16,256]{2,1,0:T(8,128)}), f32[32,16,256]{2,1,0:T(8,128)S(1)}, u32[]{:S(2)}, u32[]{:S(2)}) async-start(f32[32,16,256]{2,1,0:T(8,128)} %broadcast_in_dim.5), calls=%async_computation.2 | async-start | bytes 1048576 | tf_op jit(solution)/shard_map/all_to_all | solution.py:251
  113.6 0.0 collective-permute-done.6
  113.6 0.9 fusion.1
  114.5 9.9 %all-to-all-done.2 = f32[32,16,256]{2,1,0:T(8,128)S(1)} async-done(((f32[32,16,256]{2,1,0:T(8,128)}), f32[32,16,256]{2,1,0:T(8,128)S(1)}, u32[]{:S(2)}, u32[]{:S(2)}) %all-to-all-start.2) | async-done | bytes 524320 | tf_op jit(solution)/shard_map/all_to_all | solution.py:251
  124.5 0.8 copy.15
  (13 shorter events, 0.2 us)
Async XLA Ops:
  0.6 8.5 %copy-start = (f32[2,256,256]{2,1,0:T(8,128)S(1)}, f32[2,256,256]{2,1,0:T(8,128)}, u32[]{:S(2)}) copy-start(f32[2,256,256]{2,1,0:T(8,128)} %tile_ref.1) | copy-start | bytes 1572868
  1.8 7.3 %collective-permute-start = (f32[2,256,128]{2,1,0:T(8,128)S(1)}, f32[2,256,128]{2,1,0:T(8,128)S(1)}, u32[]{:S(2)}, u32[]{:S(2)}) collective-permute-start(f32[2,256,128]{2,1,0:T(8,128)S(1)} %get-tuple-element.15), channel_id=1, source_target_pairs={{0,1},{1,2},{2,3},{3,4},{4,5},{5,6},{6,7},{7,8},{8,9},{9,10},{10,1... | collective-permute-start | bytes 786440 | tf_op jit(solution)/shard_map/ppermute | solution.py:247
  5.8 7.2 %collective-permute-start.1 = (f32[2,256,128]{2,1,0:T(8,128)S(1)}, f32[2,256,128]{2,1,0:T(8,128)S(1)}, u32[]{:S(2)}, u32[]{:S(2)}) collective-permute-start(f32[2,256,128]{2,1,0:T(8,128)S(1)} %get-tuple-element.14), channel_id=1, source_target_pairs={{1,0},{2,1},{3,2},{4,3},{5,4},{6,5},{7,6},{8,7},{9,8},{10,9},{11,1... | collective-permute-start | bytes 786440 | tf_op jit(solution)/shard_map/ppermute | solution.py:247
  9.2 15.0 %copy-start.2 = (s32[1,1,6,2]{2,3,1,0:T(2,128)S(1)}, s32[1,1,6,2]{2,3,1,0:T(2,128)}, u32[]{:S(2)}) copy-start(s32[1,1,6,2]{2,3,1,0:T(2,128)} %param.9) | copy-start | bytes 148
  13.1 14.9 %collective-permute-start.3 = (f32[2,128,512]{2,1,0:T(8,128)S(1)}, f32[2,128,512]{2,1,0:T(8,128)S(1)}, u32[]{:S(2)}, u32[]{:S(2)}) collective-permute-start(f32[2,128,512]{2,1,0:T(8,128)S(1)} %get-tuple-element.12), channel_id=1, source_target_pairs={{32,0},{64,32},{96,64},{128,96},{160,128},{192,160},{224,192},{256... | collective-permute-start | bytes 1572872 | tf_op jit(solution)/shard_map/ppermute | solution.py:247
  21.6 8.0 %collective-permute-start.2 = (f32[2,128,512]{2,1,0:T(8,128)S(1)}, f32[2,128,512]{2,1,0:T(8,128)S(1)}, u32[]{:S(2)}, u32[]{:S(2)}) collective-permute-start(f32[2,128,512]{2,1,0:T(8,128)S(1)} %get-tuple-element.13), channel_id=1, source_target_pairs={{0,32},{32,64},{64,96},{96,128},{128,160},{160,192},{192,224},{224... | collective-permute-start | bytes 1572872 | tf_op jit(solution)/shard_map/ppermute | solution.py:247
  46.0 40.9 %copy-start.1 = (f32[2,256,512]{2,1,0:T(8,128)S(1)}, f32[2,256,512]{2,1,0:T(8,128)}, u32[]{:S(2)}) copy-start(f32[2,256,512]{2,1,0:T(8,128)} %get-tuple-element.6) | copy-start | bytes 3145732
  46.0 18.4 %all-to-all-start = ((f32[32,16,256]{2,1,0:T(8,128)}), f32[32,16,256]{2,1,0:T(8,128)S(1)}, u32[]{:S(2)}, u32[]{:S(2)}) async-start(f32[32,16,256]{2,1,0:T(8,128)} %bitcast.2), calls=%async_computation | async-start | bytes 1048576 | tf_op jit(solution)/shard_map/all_to_all | solution.py:251
  53.6 33.3 %collective-permute-start.4 = (f32[2,128,512]{2,1,0:T(8,128)S(1)}, f32[2,128,512]{2,1,0:T(8,128)}, u32[]{:S(2)}, u32[]{:S(2)}) collective-permute-start(f32[2,128,512]{2,1,0:T(8,128)S(1)} %get-tuple-element.7), channel_id=1, source_target_pairs={{0,32},{32,64},{64,96},{96,128},{128,160},{160,192},{192,224},{224... | collective-permute-start | bytes 1572872 | tf_op jit(solution)/shard_map/ppermute | solution.py:247
  57.1 29.8 %collective-permute-start.5 = (f32[2,128,512]{2,1,0:T(8,128)S(1)}, f32[2,128,512]{2,1,0:T(8,128)}, u32[]{:S(2)}, u32[]{:S(2)}) collective-permute-start(f32[2,128,512]{2,1,0:T(8,128)S(1)} %get-tuple-element.8), channel_id=1, source_target_pairs={{32,0},{64,32},{96,64},{128,96},{160,128},{192,160},{224,192},{256... | collective-permute-start | bytes 1572872 | tf_op jit(solution)/shard_map/ppermute | solution.py:247
  65.2 34.5 %all-to-all-start.1 = ((f32[16,16,256]{2,1,0:T(8,128)}), f32[16,16,256]{2,1,0:T(8,128)S(1)}, u32[]{:S(2)}, u32[]{:S(2)}) async-start(f32[16,16,256]{2,1,0:T(8,128)} %broadcast_in_dim.4), calls=%async_computation.1 | async-start | bytes 524288 | tf_op jit(solution)/shard_map/all_to_all | solution.py:251
  88.4 25.2 %collective-permute-start.6 = (f32[2,256,128]{2,1,0:T(8,128)S(1)}, f32[2,256,128]{2,1,0:T(8,128)S(1)}, u32[]{:S(2)}, u32[]{:S(2)}) collective-permute-start(f32[2,256,128]{2,1,0:T(8,128)S(1)} %get-tuple-element.10), channel_id=1, source_target_pairs={{0,1},{1,2},{2,3},{3,4},{4,5},{5,6},{6,7},{7,8},{8,9},{9,10},{10,1... | collective-permute-start | bytes 786440 | tf_op jit(solution)/shard_map/ppermute | solution.py:247
  90.6 23.0 %collective-permute-start.7 = (f32[2,256,128]{2,1,0:T(8,128)S(1)}, f32[2,256,128]{2,1,0:T(8,128)S(1)}, u32[]{:S(2)}, u32[]{:S(2)}) collective-permute-start(f32[2,256,128]{2,1,0:T(8,128)S(1)} %get-tuple-element.11), channel_id=1, source_target_pairs={{1,0},{2,1},{3,2},{4,3},{5,4},{6,5},{7,6},{8,7},{9,8},{10,9},{11,1... | collective-permute-start | bytes 786440 | tf_op jit(solution)/shard_map/ppermute | solution.py:247
  100.6 23.9 %all-to-all-start.2 = ((f32[32,16,256]{2,1,0:T(8,128)}), f32[32,16,256]{2,1,0:T(8,128)S(1)}, u32[]{:S(2)}, u32[]{:S(2)}) async-start(f32[32,16,256]{2,1,0:T(8,128)} %broadcast_in_dim.5), calls=%async_computation.2 | async-start | bytes 1048576 | tf_op jit(solution)/shard_map/all_to_all | solution.py:251

commit v4 on v3

--- a/solution.py
+++ b/solution.py
@@ -31,7 +31,8 @@
     index = np.arange(SIDE)
     angles = (index[:, None] * index[None, :] % SIDE) * (2.0 * math.pi / SIDE)
     cos, sin = np.cos(angles) / 16.0, np.sin(angles) / 16.0
-    return (np.concatenate(two_terms(np.concatenate([cos, sin], 1)), 1),)
+    high, low = two_terms(np.stack([cos, -sin - cos, cos - sin]))
+    return (np.stack([high, low]),)
 
 
 def split(value):
@@ -47,10 +48,10 @@
 
 
 def slots_kernel(
-    counts_ref, pos_ref, tile_ref, side_l_ref, side_r_ref, top_ref, bot_ref, probe_ref, intensity_ref, left_ref,
-    gprobe_out, gtop_out, gbot_out, gmid_out,
-    ext_ref, over_ref, held_ref, leftv_ref, rightv_ref, shifted_ref, window_ref, stack_ref, rows_ref,
-    mid_ref, far_ref, back_ref, grad_ref, gprobe_ref, sems, pattern_sems,
+    counts_ref, pos_ref, tile_ref, side_l_ref, side_r_ref, top_ref, bot_ref, probe_ref, intensity_ref, tables_ref,
+    gprobe_out, grad_ref,
+    ext_ref, over_ref, held_ref, table_ref, shifted_ref, window_ref, terms_ref,
+    mid_ref, far_ref, back_ref, gprobe_ref, sems, pattern_sems,
 ):
     dot = lambda a, b: jnp.dot(a, b, preferred_element_type=F32)
     low, own, high = slice(0, RIM), slice(RIM, RIM + SIDE), slice(RIM + SIDE, WIDE)
@@ -60,7 +61,7 @@
         (tile_ref, ext_ref.at[:, own, own]),
         (side_l_ref, ext_ref.at[:, own, low]),
         (side_r_ref, ext_ref.at[:, own, high]),
-        (left_ref, leftv_ref),
+        (tables_ref, table_ref),
         (top_ref, ext_ref.at[:, low]),
         (bot_ref, ext_ref.at[:, high]),
     ]
@@ -78,39 +79,25 @@
     grad_ref[...] = jnp.zeros((2, WIDE, WIDE), F32)
     for copy in copies:
         copy.wait()
-    for k in range(2):
-        cos, sin = leftv_ref[:, k * WIDE : k * WIDE + SIDE], leftv_ref[:, k * WIDE + SIDE : (k + 1) * WIDE]
-        rightv_ref[k * WIDE : k * WIDE + SIDE, 0:SIDE] = cos
-        rightv_ref[k * WIDE : k * WIDE + SIDE, SIDE:] = -sin
-        rightv_ref[k * WIDE + SIDE : (k + 1) * WIDE, 0:SIDE] = sin
-        rightv_ref[k * WIDE + SIDE : (k + 1) * WIDE, SIDE:] = cos
 
     def put(u, rows, real, imag):
-        real_high, real_low = split(real)
-        imag_high, imag_low = split(imag)
-        for base, re, im in ((0, real_high, imag_high), (WIDE, real_low, imag_low)):
-            upper = slice(base + rows.start, base + rows.stop)
-            lower = slice(base + SIDE + rows.start, base + SIDE + rows.stop)
-            stack_ref[u, upper, 0:SIDE] = re
-            stack_ref[u, upper, SIDE:] = im
-            stack_ref[u, lower, 0:SIDE] = im
-            stack_ref[u, lower, SIDE:] = -re
-
-    def put_rows(u, rows, real, imag):
-        for base, part in ((0, real), (SIDE, imag)):
-            high_part, low_part = split(part)
-            rows_ref[u, rows, base : base + SIDE] = high_part
-            rows_ref[u, rows, WIDE + base : WIDE + base + SIDE] = low_part
-
-    def by_rows(u):
-        lh, ll = leftv_ref[:, 0:WIDE], leftv_ref[:, WIDE:]
-        xh, xl = stack_ref[u, 0:WIDE], stack_ref[u, WIDE:]
-        return dot(lh, xh) + (dot(lh, xl) + dot(ll, xh))
-
-    def by_cols(u):
-        xh, xl = rows_ref[u, :, 0:WIDE], rows_ref[u, :, WIDE:]
-        rh, rl = rightv_ref[0:WIDE], rightv_ref[WIDE:]
-        return dot(xh, rh) + (dot(xl, rh) + dot(xh, rl))
+        for k, part in enumerate((real + imag, real, imag)):
+            terms_ref[u, 0, k, rows], terms_ref[u, 1, k, rows] = split(part)
+
+    def three(u, left, product):
+        both, first, second = (
+            product(terms_ref[u, 0, k], table_ref[0, k])
+            + (product(terms_ref[u, 1, k], table_ref[0, k]) + product(terms_ref[u, 0, k], table_ref[1, k]))
+            for k in range(3)
+        )
+        left[u, :, 0:SIDE] = both - second
+        left[u, :, SIDE:] = both + first
+
+    def by_rows(u, left):
+        three(u, left, lambda value, table: dot(table, value))
+
+    def by_cols(u, left):
+        three(u, left, dot)
 
     def one_group(group, carry):
         lanes = lambda n: lax.broadcasted_iota(jnp.int32, (n, RIM), 1)
@@ -147,23 +134,23 @@
                 pr, pi = shifted_ref[u, 0, rows], shifted_ref[u, 1, rows]
                 wr, wi = window_ref[u, 0, rows], window_ref[u, 1, rows]
                 put(u, rows, pr * wr - pi * wi, pr * wi + pi * wr)
-            mid_ref[u] = by_rows(u)
-        for u in range(UNROLL):
-            for rows in BLOCKS:
-                put_rows(u, rows, mid_ref[u, rows, 0:SIDE], mid_ref[u, rows, SIDE:])
-            far_ref[u] = by_cols(u)
+            by_rows(u, mid_ref)
+        for u in range(UNROLL):
+            for rows in BLOCKS:
+                put(u, rows, mid_ref[u, rows, 0:SIDE], mid_ref[u, rows, SIDE:])
+            by_cols(u, far_ref)
         patterns(group).wait()
         for u in range(UNROLL):
             for rows in BLOCKS:
                 far_real, far_imag = far_ref[u, rows, 0:SIDE], far_ref[u, rows, SIDE:]
                 misfit = far_real * far_real + far_imag * far_imag - held_ref[slots[u], rows]
                 misfit = misfit * live[u]
-                put_rows(u, rows, misfit * far_real, -misfit * far_imag)
-            mid_ref[u] = by_cols(u)
+                put(u, rows, misfit * far_real, -misfit * far_imag)
+            by_cols(u, mid_ref)
         for u in range(UNROLL):
             for rows in BLOCKS:
                 put(u, rows, mid_ref[u, rows, 0:SIDE], mid_ref[u, rows, SIDE:])
-            mid_ref[u] = by_rows(u)
+            by_rows(u, mid_ref)
         for u in range(UNROLL):
             for start, count in pieces:
                 rows = slice(start, start + count)
@@ -192,17 +179,9 @@
         return carry
 
     lax.fori_loop(0, groups, one_group, 0)
-    moves = [
-        (gprobe_ref, gprobe_out),
-        (grad_ref.at[:, low], gtop_out),
-        (grad_ref.at[:, high], gbot_out),
-        (grad_ref.at[:, own], gmid_out),
-    ]
-    copies = [pltpu.make_async_copy(src, dst, sems.at[k]) for k, (src, dst) in enumerate(moves)]
-    for copy in copies:
-        copy.start()
-    for copy in copies:
-        copy.wait()
+    copy = pltpu.make_async_copy(gprobe_ref, gprobe_out, sems.at[0])
+    copy.start()
+    copy.wait()
 
 
 def all_slots(counts, positions, *arrays):
@@ -212,26 +191,21 @@
         slots_kernel,
         out_shape=[
             jax.ShapeDtypeStruct((2, SIDE, SIDE), F32),
-            jax.ShapeDtypeStruct((2, RIM, WIDE), F32),
-            jax.ShapeDtypeStruct((2, RIM, WIDE), F32),
-            jax.ShapeDtypeStruct((2, SIDE, WIDE), F32),
+            jax.ShapeDtypeStruct((2, WIDE, WIDE), F32),
         ],
         in_specs=[smem, smem] + [anywhere] * len(arrays),
-        out_specs=[anywhere] * 4,
+        out_specs=[anywhere, pl.BlockSpec(memory_space=pltpu.VMEM)],
         scratch_shapes=[
             pltpu.VMEM((2, WIDE, WIDE), F32),
             pltpu.VMEM((2, SIDE + 8, SIDE), F32),
             pltpu.VMEM((6, SIDE, SIDE), F32),
-            pltpu.VMEM((SIDE, 2 * WIDE), BF16),
-            pltpu.VMEM((2 * WIDE, WIDE), BF16),
+            pltpu.VMEM((2, 3, SIDE, SIDE), BF16),
             pltpu.VMEM((UNROLL, 2, SIDE, SIDE), F32),
             pltpu.VMEM((UNROLL, 2, SIDE, SIDE), F32),
-            pltpu.VMEM((UNROLL, 2 * WIDE, WIDE), BF16),
-            pltpu.VMEM((UNROLL, SIDE, 2 * WIDE), BF16),
+            pltpu.VMEM((UNROLL, 2, 3, SIDE, SIDE), BF16),
             pltpu.VMEM((UNROLL, SIDE, WIDE), F32),
             pltpu.VMEM((UNROLL, SIDE, WIDE), F32),
             pltpu.VMEM((UNROLL, 2, SIDE + 8, SIDE), F32),
-            pltpu.VMEM((2, WIDE, WIDE), F32),
             pltpu.VMEM((2, SIDE, SIDE), F32),
             pltpu.SemaphoreType.DMA((8,)),
             pltpu.SemaphoreType.DMA((6 // UNROLL,)),
@@ -271,7 +245,7 @@
     middle = jnp.concatenate([side_l, object_field, side_r], axis=2)
     top = shifted(middle[:, RIM:], ROW, 1)
     bottom = shifted(middle[:, :RIM], ROW, -1)
-    grad_probe, grad_top, grad_bottom, grad_mid = all_slots(
+    grad_probe, grad_wide = all_slots(
         counts.reshape(1),
         positions.reshape(-1),
         object_field,
@@ -283,11 +257,11 @@
         intensity[0, 0],
         *tables,
     )
-    from_above = shifted(grad_bottom, ROW, 1)
-    from_below = shifted(grad_top, ROW, -1)
+    from_above = shifted(grad_wide[:, RIM + SIDE :], ROW, 1)
+    from_below = shifted(grad_wide[:, :RIM], ROW, -1)
     total_slots = lax.axis_size(ROW) * lax.axis_size(COL) * positions.shape[2]
     probe_update = summed_everywhere(grad_probe, 1.0 / math.sqrt(total_slots))
-    rows = grad_mid + jnp.concatenate([from_above, from_below], axis=1)
+    rows = grad_wide[:, RIM : RIM + SIDE] + jnp.concatenate([from_above, from_below], axis=1)
     from_left = shifted(rows[:, :, RIM + SIDE :], COL, 1)
     from_right = shifted(rows[:, :, :RIM], COL, -1)
     gathered = rows[:, :, RIM : RIM + SIDE] + jnp.concatenate([from_left, from_right], axis=2)

time: 126 us -> 125 us (level)
  local copies, waits for them, and re-layouts: 3.89 us -> 7.14 us
  waiting for transfers between devices: 34.1 us -> 32.1 us
  Pallas kernels: 16.4 us -> 14.8 us
    pallas_call x1, Pallas kernels: 16.4 us -> 14.8 us  [all_slots(): pl.pallas_call(slots_kernel, out_shape=[jax.ShapeDtypeStruct((2, SIDE, SI...]
    all_to_all x3, waiting for transfers between devices: 23.1 us -> 21.8 us  [swap(): return lax.all_to_all(pieces, axes, split_axis=0, concat_axis=0, tiled=True)]
    slice x0 -> x1, local copies, waits for them, and re-layouts: none -> 1.28 us  [shards(): from_above = shifted(grad_wide[:, RIM + SIDE:], ROW, 1)]
  transfers between devices with their start and end apart: 11 -> 11, of which waited for: 7 -> 7; matrix products, arithmetic and copies ran while one was open for 3% -> 5% of each run, Pallas kernels for 0% -> 0%
where the time goes in v4:
time: 125 us
  starting transfers between devices  66.7 us (53%)
  waiting for transfers between devices  32.1 us (26%)
  Pallas kernels  14.8 us (12%)
  local copies, waits for them, and re-layouts  7.14 us (6%)
  other arithmetic  2.39 us (2%)
  between operations  1.5 us (1%)
    all_to_all x3, starting transfers between devices, swap(): return lax.all_to_all(pieces, axes, split_axis=0, concat_axis=0, tiled=True)  41.1 us
    ppermute x8, starting transfers between devices, shifted(): return lax.ppermute(block, axes, route)  25.6 us
    all_to_all x3, waiting for transfers between devices, swap(): return lax.all_to_all(pieces, axes, split_axis=0, concat_axis=0, tiled=True)  21.8 us
    pallas_call x1, Pallas kernels, all_slots(): pl.pallas_call(slots_kernel, out_shape=[jax.ShapeDtypeStruct((2, SIDE, SI...  14.8 us
    ppermute x8, waiting for transfers between devices, shifted(): return lax.ppermute(block, axes, route)  10.3 us
  transfers between devices with their start and end apart: 11, of which 7 were waited for; matrix products, arithmetic and copies ran while one was open for 5% of the time, Pallas kernels for 0%

profile of v4, /device:TPU:1, one launch (start us, length us, event | category | flops | bytes accessed | tf_op | source)
XLA Modules:
  0.0 124.7 jit_solution(18259363646209257276)
XLA Ops:
  0.6 1.1 fusion.5
  1.7 4.0 %collective-permute-start = (f32[2,256,128]{2,1,0:T(8,128)S(1)}, f32[2,256,128]{2,1,0:T(8,128)S(1)}, u32[]{:S(2)}, u32[]{:S(2)}) collective-permute-start(f32[2,256,128]{2,1,0:T(8,128)S(1)} %get-tuple-element.13), channel_id=1, source_target_pairs={{0,1},{1,2},{2,3},{3,4},{4,5},{5,6},{6,7},{7,8},{8,9},{9,10},{10,1... | collective-permute-start | bytes 786440 | tf_op jit(solution)/shard_map/ppermute | solution.py:221
  5.8 0.0 copy-start.3
  5.8 0.0 copy-start.2
  5.8 1.4 %collective-permute-start.1 = (f32[2,256,128]{2,1,0:T(8,128)S(1)}, f32[2,256,128]{2,1,0:T(8,128)S(1)}, u32[]{:S(2)}, u32[]{:S(2)}) collective-permute-start(f32[2,256,128]{2,1,0:T(8,128)S(1)} %get-tuple-element.12), channel_id=1, source_target_pairs={{1,0},{2,1},{3,2},{4,3},{5,4},{6,5},{7,6},{8,7},{9,8},{10,9},{11,1... | collective-permute-start | bytes 786440 | tf_op jit(solution)/shard_map/ppermute | solution.py:221
  7.2 1.8 %collective-permute-done.side_l_ref = f32[2,256,128]{2,1,0:T(8,128)S(1)} collective-permute-done((f32[2,256,128]{2,1,0:T(8,128)S(1)}, f32[2,256,128]{2,1,0:T(8,128)S(1)}, u32[]{:S(2)}, u32[]{:S(2)}) %collective-permute-start) | collective-permute-done | bytes 262176 | tf_op jit(solution)/shard_map/ppermute | solution.py:221
  9.1 1.1 constant_dynamic-update-slice_fusion.1
  10.2 2.9 %collective-permute-done.1.side_r_ref = f32[2,256,128]{2,1,0:T(8,128)S(1)} collective-permute-done((f32[2,256,128]{2,1,0:T(8,128)S(1)}, f32[2,256,128]{2,1,0:T(8,128)S(1)}, u32[]{:S(2)}, u32[]{:S(2)}) %collective-permute-start.1) | collective-permute-done | bytes 262176 | tf_op jit(solution)/shard_map/ppermute | solution.py:221
  13.1 1.0 fusion.4
  14.2 9.3 %collective-permute-start.3 = (f32[2,128,512]{2,1,0:T(8,128)}, f32[2,128,512]{2,1,0:T(8,128)S(1)}, u32[]{:S(2)}, u32[]{:S(2)}) collective-permute-start(f32[2,128,512]{2,1,0:T(8,128)} %get-tuple-element.10), channel_id=1, source_target_pairs={{32,0},{64,32},{96,64},{128,96},{160,128},{192,160},{224,192},{256... | collective-permute-start | bytes 1572872 | tf_op jit(solution)/shard_map/ppermute | solution.py:221
  23.5 1.9 %collective-permute-start.2 = (f32[2,128,512]{2,1,0:T(8,128)}, f32[2,128,512]{2,1,0:T(8,128)S(1)}, u32[]{:S(2)}, u32[]{:S(2)}) collective-permute-start(f32[2,128,512]{2,1,0:T(8,128)} %get-tuple-element.11), channel_id=1, source_target_pairs={{0,32},{32,64},{64,96},{96,128},{128,160},{160,192},{192,224},{224... | collective-permute-start | bytes 1572872 | tf_op jit(solution)/shard_map/ppermute | solution.py:221
  26.1 0.1 copy.10
  26.2 0.1 reshape.21.pos_ref
  26.3 3.9 %collective-permute-done.3.bot_ref = f32[2,128,512]{2,1,0:T(8,128)S(1)} collective-permute-done((f32[2,128,512]{2,1,0:T(8,128)}, f32[2,128,512]{2,1,0:T(8,128)S(1)}, u32[]{:S(2)}, u32[]{:S(2)}) %collective-permute-start.3) | collective-permute-done | bytes 524320 | tf_op jit(solution)/shard_map/ppermute | solution.py:221
  30.1 1.7 %collective-permute-done.2.top_ref = f32[2,128,512]{2,1,0:T(8,128)S(1)} collective-permute-done((f32[2,128,512]{2,1,0:T(8,128)}, f32[2,128,512]{2,1,0:T(8,128)S(1)}, u32[]{:S(2)}, u32[]{:S(2)}) %collective-permute-start.2) | collective-permute-done | bytes 524320 | tf_op jit(solution)/shard_map/ppermute | solution.py:221
  31.8 14.8 %shard_map.77 = (f32[2,256,256]{2,1,0:T(8,128)}, f32[2,512,512]{2,1,0:T(8,128)}) custom-call(s32[1]{0:T(128)} %bitcast.4.counts_ref, s32[12]{0:T(128)S(1)} %reshape.21.pos_ref, f32[2,256,256]{2,1,0:T(8,128)S(1)} %copy-done, f32[2,256,128]{2,1,0:T(8,128)S(1)} %collective-permute-done.side_l_ref, f32[2,256,128]{2,1,0:T(8,128)S(1)} %collective-permute-done.1.side_r_ref, ...), custom_call_target="tpu_custom_call" | custom-call | flops 10000000000 | bytes 20000000 | tf_op jit(solution)/shard_map/pallas_call | solution.py:190
  46.6 9.8 %all-to-all-start = ((f32[32,16,256]{2,1,0:T(8,128)}), f32[32,16,256]{2,1,0:T(8,128)S(1)}, u32[]{:S(2)}, u32[]{:S(2)}) async-start(f32[32,16,256]{2,1,0:T(8,128)} %bitcast.2), calls=%async_computation | async-start | bytes 1048576 | tf_op jit(solution)/shard_map/all_to_all | solution.py:225
  56.5 1.3 %fusion.2 = (f32[2,128,512]{2,1,0:T(8,128)S(1)}, f32[2,128,512]{2,1,0:T(8,128)S(1)}) fusion(f32[2,512,512]{2,1,0:T(8,128)} %get-tuple-element.4), kind=kLoop, calls=%fused_computation.8 | loop fusion | bytes 2097152 | tf_op jit(solution)/shard_map/slice | solution.py:260
  57.7 3.5 %collective-permute-start.4 = (f32[2,128,512]{2,1,0:T(8,128)S(1)}, f32[2,128,512]{2,1,0:T(8,128)S(1)}, u32[]{:S(2)}, u32[]{:S(2)}) collective-permute-start(f32[2,128,512]{2,1,0:T(8,128)S(1)} %get-tuple-element.6), channel_id=1, source_target_pairs={{0,32},{32,64},{64,96},{96,128},{128,160},{160,192},{192,224},{224... | collective-permute-start | bytes 1572872 | tf_op jit(solution)/shard_map/ppermute | solution.py:221
  61.3 1.9 %collective-permute-start.5 = (f32[2,128,512]{2,1,0:T(8,128)S(1)}, f32[2,128,512]{2,1,0:T(8,128)S(1)}, u32[]{:S(2)}, u32[]{:S(2)}) collective-permute-start(f32[2,128,512]{2,1,0:T(8,128)S(1)} %get-tuple-element.7), channel_id=1, source_target_pairs={{32,0},{64,32},{96,64},{128,96},{160,128},{192,160},{224,192},{256... | collective-permute-start | bytes 1572872 | tf_op jit(solution)/shard_map/ppermute | solution.py:221
  63.2 4.1 %all-to-all-done = f32[32,16,256]{2,1,0:T(8,128)S(1)} async-done(((f32[32,16,256]{2,1,0:T(8,128)}), f32[32,16,256]{2,1,0:T(8,128)S(1)}, u32[]{:S(2)}, u32[]{:S(2)}) %all-to-all-start) | async-done | bytes 524320 | tf_op jit(solution)/shard_map/all_to_all | solution.py:225
  67.3 0.7 broadcast_in_dim.4
  68.1 18.3 %all-to-all-start.1 = ((f32[16,16,256]{2,1,0:T(8,128)}), f32[16,16,256]{2,1,0:T(8,128)S(1)}, u32[]{:S(2)}, u32[]{:S(2)}) async-start(f32[16,16,256]{2,1,0:T(8,128)} %broadcast_in_dim.4), calls=%async_computation.1 | async-start | bytes 524288 | tf_op jit(solution)/shard_map/all_to_all | solution.py:225
  86.4 1.4 %maximum_add_fusion = f32[2,256,512]{2,1,0:T(8,128)S(1)} fusion(f32[2,128,512]{2,1,0:T(8,128)S(1)} %collective-permute-done.5, f32[2,128,512]{2,1,0:T(8,128)S(1)} %collective-permute-done.4, f32[2,512,512]{2,1,0:T(8,128)} %get-tuple-element.4), kind=kLoop, calls=%fused_computation | loop fusion | flops 524288 | bytes 3145728 | tf_op jit(solution)/shard_map/add | solution.py:264
  87.8 2.2 %collective-permute-start.6 = (f32[2,256,128]{2,1,0:T(8,128)S(1)}, f32[2,256,128]{2,1,0:T(8,128)S(1)}, u32[]{:S(2)}, u32[]{:S(2)}) collective-permute-start(f32[2,256,128]{2,1,0:T(8,128)S(1)} %get-tuple-element.8), channel_id=1, source_target_pairs={{0,1},{1,2},{2,3},{3,4},{4,5},{5,6},{6,7},{7,8},{8,9},{9,10},{10,1... | collective-permute-start | bytes 786440 | tf_op jit(solution)/shard_map/ppermute | solution.py:221
  90.0 1.3 %collective-permute-start.7 = (f32[2,256,128]{2,1,0:T(8,128)S(1)}, f32[2,256,128]{2,1,0:T(8,128)S(1)}, u32[]{:S(2)}, u32[]{:S(2)}) collective-permute-start(f32[2,256,128]{2,1,0:T(8,128)S(1)} %get-tuple-element.9), channel_id=1, source_target_pairs={{1,0},{2,1},{3,2},{4,3},{5,4},{6,5},{7,6},{8,7},{9,8},{10,9},{11,1... | collective-permute-start | bytes 786440 | tf_op jit(solution)/shard_map/ppermute | solution.py:221
  91.3 7.8 %all-to-all-done.1 = f32[16,16,256]{2,1,0:T(8,128)S(1)} async-done(((f32[16,16,256]{2,1,0:T(8,128)}), f32[16,16,256]{2,1,0:T(8,128)S(1)}, u32[]{:S(2)}, u32[]{:S(2)}) %all-to-all-start.1) | async-done | bytes 262176 | tf_op jit(solution)/shard_map/all_to_all | solution.py:225
  99.2 0.9 broadcast_in_dim.5
  100.0 13.0 %all-to-all-start.2 = ((f32[32,16,256]{2,1,0:T(8,128)}), f32[32,16,256]{2,1,0:T(8,128)S(1)}, u32[]{:S(2)}, u32[]{:S(2)}) async-start(f32[32,16,256]{2,1,0:T(8,128)} %broadcast_in_dim.5), calls=%async_computation.2 | async-start | bytes 1048576 | tf_op jit(solution)/shard_map/all_to_all | solution.py:225
  113.1 0.9 fusion.1
  113.9 9.9 %all-to-all-done.2 = f32[32,16,256]{2,1,0:T(8,128)S(1)} async-done(((f32[32,16,256]{2,1,0:T(8,128)}), f32[32,16,256]{2,1,0:T(8,128)S(1)}, u32[]{:S(2)}, u32[]{:S(2)}) %all-to-all-start.2) | async-done | bytes 524320 | tf_op jit(solution)/shard_map/all_to_all | solution.py:225
  123.9 0.8 copy.15
  (16 shorter events, 0.2 us)
Async XLA Ops:
  1.7 7.3 %collective-permute-start = (f32[2,256,128]{2,1,0:T(8,128)S(1)}, f32[2,256,128]{2,1,0:T(8,128)S(1)}, u32[]{:S(2)}, u32[]{:S(2)}) collective-permute-start(f32[2,256,128]{2,1,0:T(8,128)S(1)} %get-tuple-element.13), channel_id=1, source_target_pairs={{0,1},{1,2},{2,3},{3,4},{4,5},{5,6},{6,7},{7,8},{8,9},{9,10},{10,1... | collective-permute-start | bytes 786440 | tf_op jit(solution)/shard_map/ppermute | solution.py:221
  5.8 20.3 %copy-start.3 = (s32[1,1,6,2]{2,3,1,0:T(2,128)S(1)}, s32[1,1,6,2]{2,3,1,0:T(2,128)}, u32[]{:S(2)}) copy-start(s32[1,1,6,2]{2,3,1,0:T(2,128)} %param.9) | copy-start | bytes 148
  5.8 26.1 %copy-start = (f32[2,256,256]{2,1,0:T(8,128)S(1)}, f32[2,256,256]{2,1,0:T(8,128)}, u32[]{:S(2)}) copy-start(f32[2,256,256]{2,1,0:T(8,128)} %tile_ref.1) | copy-start | bytes 1572868
  5.8 26.1 %copy-start.1 = (f32[2,256,256]{2,1,0:T(8,128)S(1)}, f32[2,256,256]{2,1,0:T(8,128)}, u32[]{:S(2)}) copy-start(f32[2,256,256]{2,1,0:T(8,128)} %probe_ref.1) | copy-start | bytes 1572868
  5.8 26.1 %copy-start.2 = (bf16[2,3,256,256]{3,2,1,0:T(8,128)(2,1)S(1)}, bf16[2,3,256,256]{3,2,1,0:T(8,128)(2,1)}, u32[]{:S(2)}) copy-start(bf16[2,3,256,256]{3,2,1,0:T(8,128)(2,1)} %constant.8.clone.tables_ref) | copy-start | bytes 2359300
  5.8 7.3 %collective-permute-start.1 = (f32[2,256,128]{2,1,0:T(8,128)S(1)}, f32[2,256,128]{2,1,0:T(8,128)S(1)}, u32[]{:S(2)}, u32[]{:S(2)}) collective-permute-start(f32[2,256,128]{2,1,0:T(8,128)S(1)} %get-tuple-element.12), channel_id=1, source_target_pairs={{1,0},{2,1},{3,2},{4,3},{5,4},{6,5},{7,6},{8,7},{9,8},{10,9},{11,1... | collective-permute-start | bytes 786440 | tf_op jit(solution)/shard_map/ppermute | solution.py:221
  14.2 16.0 %collective-permute-start.3 = (f32[2,128,512]{2,1,0:T(8,128)}, f32[2,128,512]{2,1,0:T(8,128)S(1)}, u32[]{:S(2)}, u32[]{:S(2)}) collective-permute-start(f32[2,128,512]{2,1,0:T(8,128)} %get-tuple-element.10), channel_id=1, source_target_pairs={{32,0},{64,32},{96,64},{128,96},{160,128},{192,160},{224,192},{256... | collective-permute-start | bytes 1572872 | tf_op jit(solution)/shard_map/ppermute | solution.py:221
  23.5 8.3 %collective-permute-start.2 = (f32[2,128,512]{2,1,0:T(8,128)}, f32[2,128,512]{2,1,0:T(8,128)S(1)}, u32[]{:S(2)}, u32[]{:S(2)}) collective-permute-start(f32[2,128,512]{2,1,0:T(8,128)} %get-tuple-element.11), channel_id=1, source_target_pairs={{0,32},{32,64},{64,96},{96,128},{128,160},{160,192},{192,224},{224... | collective-permute-start | bytes 1572872 | tf_op jit(solution)/shard_map/ppermute | solution.py:221
  46.6 20.6 %all-to-all-start = ((f32[32,16,256]{2,1,0:T(8,128)}), f32[32,16,256]{2,1,0:T(8,128)S(1)}, u32[]{:S(2)}, u32[]{:S(2)}) async-start(f32[32,16,256]{2,1,0:T(8,128)} %bitcast.2), calls=%async_computation | async-start | bytes 1048576 | tf_op jit(solution)/shard_map/all_to_all | solution.py:225
  57.7 28.6 %collective-permute-start.4 = (f32[2,128,512]{2,1,0:T(8,128)S(1)}, f32[2,128,512]{2,1,0:T(8,128)S(1)}, u32[]{:S(2)}, u32[]{:S(2)}) collective-permute-start(f32[2,128,512]{2,1,0:T(8,128)S(1)} %get-tuple-element.6), channel_id=1, source_target_pairs={{0,32},{32,64},{64,96},{96,128},{128,160},{160,192},{192,224},{224... | collective-permute-start | bytes 1572872 | tf_op jit(solution)/shard_map/ppermute | solution.py:221
  61.3 25.1 %collective-permute-start.5 = (f32[2,128,512]{2,1,0:T(8,128)S(1)}, f32[2,128,512]{2,1,0:T(8,128)S(1)}, u32[]{:S(2)}, u32[]{:S(2)}) collective-permute-start(f32[2,128,512]{2,1,0:T(8,128)S(1)} %get-tuple-element.7), channel_id=1, source_target_pairs={{32,0},{64,32},{96,64},{128,96},{160,128},{192,160},{224,192},{256... | collective-permute-start | bytes 1572872 | tf_op jit(solution)/shard_map/ppermute | solution.py:221
  68.1 31.0 %all-to-all-start.1 = ((f32[16,16,256]{2,1,0:T(8,128)}), f32[16,16,256]{2,1,0:T(8,128)S(1)}, u32[]{:S(2)}, u32[]{:S(2)}) async-start(f32[16,16,256]{2,1,0:T(8,128)} %broadcast_in_dim.4), calls=%async_computation.1 | async-start | bytes 524288 | tf_op jit(solution)/shard_map/all_to_all | solution.py:225
  87.8 25.2 %collective-permute-start.6 = (f32[2,256,128]{2,1,0:T(8,128)S(1)}, f32[2,256,128]{2,1,0:T(8,128)S(1)}, u32[]{:S(2)}, u32[]{:S(2)}) collective-permute-start(f32[2,256,128]{2,1,0:T(8,128)S(1)} %get-tuple-element.8), channel_id=1, source_target_pairs={{0,1},{1,2},{2,3},{3,4},{4,5},{5,6},{6,7},{7,8},{8,9},{9,10},{10,1... | collective-permute-start | bytes 786440 | tf_op jit(solution)/shard_map/ppermute | solution.py:221
  90.0 23.0 %collective-permute-start.7 = (f32[2,256,128]{2,1,0:T(8,128)S(1)}, f32[2,256,128]{2,1,0:T(8,128)S(1)}, u32[]{:S(2)}, u32[]{:S(2)}) collective-permute-start(f32[2,256,128]{2,1,0:T(8,128)S(1)} %get-tuple-element.9), channel_id=1, source_target_pairs={{1,0},{2,1},{3,2},{4,3},{5,4},{6,5},{7,6},{8,7},{9,8},{10,9},{11,1... | collective-permute-start | bytes 786440 | tf_op jit(solution)/shard_map/ppermute | solution.py:221
  100.0 23.9 %all-to-all-start.2 = ((f32[32,16,256]{2,1,0:T(8,128)}), f32[32,16,256]{2,1,0:T(8,128)S(1)}, u32[]{:S(2)}, u32[]{:S(2)}) async-start(f32[32,16,256]{2,1,0:T(8,128)} %broadcast_in_dim.5), calls=%async_computation.2 | async-start | bytes 1048576 | tf_op jit(solution)/shard_map/all_to_all | solution.py:225

commit v5 on v4

--- a/solution.py
+++ b/solution.py
@@ -12,7 +12,8 @@
 OBJECT_RATE = 0.5
 ROW = ("yh", "x", "core")
 COL = ("z", "yl")
-PLANE = ("yh", "x", "core", "yl")
+PLANE = ("core", "yh", "x", "yl")
+FLOOR = ("yh", "x", "yl")
 DEEP = "z"
 SIDE = 256
 RIM = 128
@@ -234,8 +235,8 @@
     count = lax.axis_size(PLANE)
     pieces = swap(grad.reshape(count, 2 * SIDE // count, SIDE), PLANE)
     part = spread(jnp.sum(pieces, axis=0), DEEP)
-    whole = spread(jnp.sum(part, axis=0) * scale, PLANE)
-    return whole.reshape(2, SIDE, SIDE)
+    half = spread(jnp.sum(part, axis=0) * scale, FLOOR)
+    return lax.all_gather(half, "core", axis=0, tiled=True).reshape(2, SIDE, SIDE)
 
 
 def shards(object_field, probe_field, intensity, positions, counts):

time: 125 us -> 124 us (level)
  blocking collectives: 0 us -> 8.96 us
  Pallas kernels: 14.8 us -> 9.04 us
  starting transfers between devices: 66.7 us -> 62 us
    all_gather x0 -> x1, blocking collectives: none -> 8.96 us  [summed_everywhere(): lax.all_gather(half, 'core', axis=0, tiled=True).reshape(2, SIDE, SIDE)]
    pallas_call x1, Pallas kernels: 14.8 us -> 9.04 us  [all_slots(): pl.pallas_call(slots_kernel, out_shape=[jax.ShapeDtypeStruct((2, SIDE, SI...]
    all_to_all x3, starting transfers between devices: 41.1 us -> 37.3 us  [swap(): return lax.all_to_all(pieces, axes, split_axis=0, concat_axis=0, tiled=True)]
where the time goes in v5:
time: 124 us
  starting transfers between devices  62 us (50%)
  waiting for transfers between devices  32.7 us (26%)
  Pallas kernels  9.04 us (7%)
  blocking collectives  8.96 us (7%)
  local copies, waits for them, and re-layouts  7.01 us (6%)
  other arithmetic  2.39 us (2%)
  between operations  1.51 us (1%)
    all_to_all x3, starting transfers between devices, swap(): return lax.all_to_all(pieces, axes, split_axis=0, concat_axis=0, tiled=True)  37.3 us
    ppermute x8, starting transfers between devices, shifted(): return lax.ppermute(block, axes, route)  24.7 us
    all_to_all x3, waiting for transfers between devices, swap(): return lax.all_to_all(pieces, axes, split_axis=0, concat_axis=0, tiled=True)  22.4 us
    ppermute x8, waiting for transfers between devices, shifted(): return lax.ppermute(block, axes, route)  10.3 us
    pallas_call x1, Pallas kernels, all_slots(): pl.pallas_call(slots_kernel, out_shape=[jax.ShapeDtypeStruct((2, SIDE, SI...  9.04 us
    all_gather x1, blocking collectives, summed_everywhere(): lax.all_gather(half, 'core', axis=0, tiled=True).reshape(2, SIDE, SIDE)  8.96 us
  transfers between devices with their start and end apart: 11, of which 7 were waited for; matrix products, arithmetic and copies ran while one was open for 5% of the time, Pallas kernels for 0%

profile of v5, /device:TPU:1, one launch (start us, length us, event | category | flops | bytes accessed | tf_op | source)
XLA Modules:
  0.0 123.7 jit_solution(9110336329539600772)
XLA Ops:
  0.6 1.1 fusion.5
  1.7 4.0 %collective-permute-start = (f32[2,256,128]{2,1,0:T(8,128)S(1)}, f32[2,256,128]{2,1,0:T(8,128)S(1)}, u32[]{:S(2)}, u32[]{:S(2)}) collective-permute-start(f32[2,256,128]{2,1,0:T(8,128)S(1)} %get-tuple-element.13), channel_id=1, source_target_pairs={{0,1},{1,2},{2,3},{3,4},{4,5},{5,6},{6,7},{7,8},{8,9},{9,10},{10,1... | collective-permute-start | bytes 786440 | tf_op jit(solution)/shard_map/ppermute | solution.py:222
  5.8 0.0 copy-start.2
  5.8 1.4 %collective-permute-start.1 = (f32[2,256,128]{2,1,0:T(8,128)S(1)}, f32[2,256,128]{2,1,0:T(8,128)S(1)}, u32[]{:S(2)}, u32[]{:S(2)}) collective-permute-start(f32[2,256,128]{2,1,0:T(8,128)S(1)} %get-tuple-element.12), channel_id=1, source_target_pairs={{1,0},{2,1},{3,2},{4,3},{5,4},{6,5},{7,6},{8,7},{9,8},{10,9},{11,1... | collective-permute-start | bytes 786440 | tf_op jit(solution)/shard_map/ppermute | solution.py:222
  7.2 1.8 %collective-permute-done.side_l_ref = f32[2,256,128]{2,1,0:T(8,128)S(1)} collective-permute-done((f32[2,256,128]{2,1,0:T(8,128)S(1)}, f32[2,256,128]{2,1,0:T(8,128)S(1)}, u32[]{:S(2)}, u32[]{:S(2)}) %collective-permute-start) | collective-permute-done | bytes 262176 | tf_op jit(solution)/shard_map/ppermute | solution.py:222
  9.1 1.1 constant_dynamic-update-slice_fusion.1
  10.2 2.9 %collective-permute-done.1.side_r_ref = f32[2,256,128]{2,1,0:T(8,128)S(1)} collective-permute-done((f32[2,256,128]{2,1,0:T(8,128)S(1)}, f32[2,256,128]{2,1,0:T(8,128)S(1)}, u32[]{:S(2)}, u32[]{:S(2)}) %collective-permute-start.1) | collective-permute-done | bytes 262176 | tf_op jit(solution)/shard_map/ppermute | solution.py:222
  13.1 1.0 fusion.4
  14.2 9.3 %collective-permute-start.3 = (f32[2,128,512]{2,1,0:T(8,128)}, f32[2,128,512]{2,1,0:T(8,128)S(1)}, u32[]{:S(2)}, u32[]{:S(2)}) collective-permute-start(f32[2,128,512]{2,1,0:T(8,128)} %get-tuple-element.10), channel_id=1, source_target_pairs={{32,0},{64,32},{96,64},{128,96},{160,128},{192,160},{224,192},{256... | collective-permute-start | bytes 1572872 | tf_op jit(solution)/shard_map/ppermute | solution.py:222
  23.5 1.9 %collective-permute-start.2 = (f32[2,128,512]{2,1,0:T(8,128)}, f32[2,128,512]{2,1,0:T(8,128)S(1)}, u32[]{:S(2)}, u32[]{:S(2)}) collective-permute-start(f32[2,128,512]{2,1,0:T(8,128)} %get-tuple-element.11), channel_id=1, source_target_pairs={{0,32},{32,64},{64,96},{96,128},{128,160},{160,192},{192,224},{224... | collective-permute-start | bytes 1572872 | tf_op jit(solution)/shard_map/ppermute | solution.py:222
  26.1 0.1 copy.11
  26.2 0.1 reshape.21.pos_ref
  26.3 3.9 %collective-permute-done.3.bot_ref = f32[2,128,512]{2,1,0:T(8,128)S(1)} collective-permute-done((f32[2,128,512]{2,1,0:T(8,128)}, f32[2,128,512]{2,1,0:T(8,128)S(1)}, u32[]{:S(2)}, u32[]{:S(2)}) %collective-permute-start.3) | collective-permute-done | bytes 524320 | tf_op jit(solution)/shard_map/ppermute | solution.py:222
  30.1 1.7 %collective-permute-done.2.top_ref = f32[2,128,512]{2,1,0:T(8,128)S(1)} collective-permute-done((f32[2,128,512]{2,1,0:T(8,128)}, f32[2,128,512]{2,1,0:T(8,128)S(1)}, u32[]{:S(2)}, u32[]{:S(2)}) %collective-permute-start.2) | collective-permute-done | bytes 524320 | tf_op jit(solution)/shard_map/ppermute | solution.py:222
  31.8 9.0 %shard_map.77 = (f32[2,256,256]{2,1,0:T(8,128)}, f32[2,512,512]{2,1,0:T(8,128)}) custom-call(s32[1]{0:T(128)} %bitcast.4.counts_ref, s32[12]{0:T(128)S(1)} %reshape.21.pos_ref, f32[2,256,256]{2,1,0:T(8,128)S(1)} %copy-done, f32[2,256,128]{2,1,0:T(8,128)S(1)} %collective-permute-done.side_l_ref, f32[2,256,128]{2,1,0:T(8,128)S(1)} %collective-permute-done.1.side_r_ref, ...), custom_call_target="tpu_custom_call" | custom-call | flops 10000000000 | bytes 20000000 | tf_op jit(solution)/shard_map/pallas_call | solution.py:191
  40.9 13.4 %all-to-all-start = ((f32[32,16,256]{2,1,0:T(8,128)}), f32[32,16,256]{2,1,0:T(8,128)S(1)}, u32[]{:S(2)}, u32[]{:S(2)}) async-start(f32[32,16,256]{2,1,0:T(8,128)} %bitcast.2), calls=%async_computation | async-start | bytes 1048576 | tf_op jit(solution)/shard_map/all_to_all | solution.py:226
  54.3 1.3 %fusion.2 = (f32[2,128,512]{2,1,0:T(8,128)S(1)}, f32[2,128,512]{2,1,0:T(8,128)S(1)}) fusion(f32[2,512,512]{2,1,0:T(8,128)} %get-tuple-element.4), kind=kLoop, calls=%fused_computation.8 | loop fusion | bytes 2097152 | tf_op jit(solution)/shard_map/slice | solution.py:261
  55.6 3.5 %collective-permute-start.4 = (f32[2,128,512]{2,1,0:T(8,128)S(1)}, f32[2,128,512]{2,1,0:T(8,128)S(1)}, u32[]{:S(2)}, u32[]{:S(2)}) collective-permute-start(f32[2,128,512]{2,1,0:T(8,128)S(1)} %get-tuple-element.6), channel_id=1, source_target_pairs={{0,32},{32,64},{64,96},{96,128},{128,160},{160,192},{192,224},{224... | collective-permute-start | bytes 1572872 | tf_op jit(solution)/shard_map/ppermute | solution.py:222
  59.1 1.9 %collective-permute-start.5 = (f32[2,128,512]{2,1,0:T(8,128)S(1)}, f32[2,128,512]{2,1,0:T(8,128)S(1)}, u32[]{:S(2)}, u32[]{:S(2)}) collective-permute-start(f32[2,128,512]{2,1,0:T(8,128)S(1)} %get-tuple-element.7), channel_id=1, source_target_pairs={{32,0},{64,32},{96,64},{128,96},{160,128},{192,160},{224,192},{256... | collective-permute-start | bytes 1572872 | tf_op jit(solution)/shard_map/ppermute | solution.py:222
  61.1 5.4 %all-to-all-done = f32[32,16,256]{2,1,0:T(8,128)S(1)} async-done(((f32[32,16,256]{2,1,0:T(8,128)}), f32[32,16,256]{2,1,0:T(8,128)S(1)}, u32[]{:S(2)}, u32[]{:S(2)}) %all-to-all-start) | async-done | bytes 524320 | tf_op jit(solution)/shard_map/all_to_all | solution.py:226
  66.5 0.7 broadcast_in_dim.4
  67.2 20.4 %all-to-all-start.1 = ((f32[16,16,256]{2,1,0:T(8,128)}), f32[16,16,256]{2,1,0:T(8,128)S(1)}, u32[]{:S(2)}, u32[]{:S(2)}) async-start(f32[16,16,256]{2,1,0:T(8,128)} %broadcast_in_dim.4), calls=%async_computation.1 | async-start | bytes 524288 | tf_op jit(solution)/shard_map/all_to_all | solution.py:226
  87.6 1.4 %maximum_add_fusion = f32[2,256,512]{2,1,0:T(8,128)S(1)} fusion(f32[2,128,512]{2,1,0:T(8,128)S(1)} %collective-permute-done.5, f32[2,128,512]{2,1,0:T(8,128)S(1)} %collective-permute-done.4, f32[2,512,512]{2,1,0:T(8,128)} %get-tuple-element.4), kind=kLoop, calls=%fused_computation | loop fusion | flops 524288 | bytes 3145728 | tf_op jit(solution)/shard_map/add | solution.py:265
  89.1 1.3 %collective-permute-start.6 = (f32[2,256,128]{2,1,0:T(8,128)S(1)}, f32[2,256,128]{2,1,0:T(8,128)S(1)}, u32[]{:S(2)}, u32[]{:S(2)}) collective-permute-start(f32[2,256,128]{2,1,0:T(8,128)S(1)} %get-tuple-element.8), channel_id=1, source_target_pairs={{0,1},{1,2},{2,3},{3,4},{4,5},{5,6},{6,7},{7,8},{8,9},{9,10},{10,1... | collective-permute-start | bytes 786440 | tf_op jit(solution)/shard_map/ppermute | solution.py:222
  90.4 1.3 %collective-permute-start.7 = (f32[2,256,128]{2,1,0:T(8,128)S(1)}, f32[2,256,128]{2,1,0:T(8,128)S(1)}, u32[]{:S(2)}, u32[]{:S(2)}) collective-permute-start(f32[2,256,128]{2,1,0:T(8,128)S(1)} %get-tuple-element.9), channel_id=1, source_target_pairs={{1,0},{2,1},{3,2},{4,3},{5,4},{6,5},{7,6},{8,7},{9,8},{10,9},{11,1... | collective-permute-start | bytes 786440 | tf_op jit(solution)/shard_map/ppermute | solution.py:222
  91.7 10.6 %all-to-all-done.1 = f32[16,16,256]{2,1,0:T(8,128)S(1)} async-done(((f32[16,16,256]{2,1,0:T(8,128)}), f32[16,16,256]{2,1,0:T(8,128)S(1)}, u32[]{:S(2)}, u32[]{:S(2)}) %all-to-all-start.1) | async-done | bytes 262176 | tf_op jit(solution)/shard_map/all_to_all | solution.py:226
  102.3 0.7 broadcast_in_dim.5
  103.1 3.5 %all-to-all-start.2 = ((f32[16,16,256]{2,1,0:T(8,128)}), f32[16,16,256]{2,1,0:T(8,128)S(1)}, u32[]{:S(2)}, u32[]{:S(2)}) async-start(f32[16,16,256]{2,1,0:T(8,128)} %broadcast_in_dim.5), calls=%async_computation.2 | async-start | bytes 524288 | tf_op jit(solution)/shard_map/all_to_all | solution.py:226
  106.6 0.9 fusion.1
  107.5 6.4 %all-to-all-done.2 = f32[16,16,256]{2,1,0:T(8,128)S(1)} async-done(((f32[16,16,256]{2,1,0:T(8,128)}), f32[16,16,256]{2,1,0:T(8,128)S(1)}, u32[]{:S(2)}, u32[]{:S(2)}) %all-to-all-start.2) | async-done | bytes 262176 | tf_op jit(solution)/shard_map/all_to_all | solution.py:226
  113.9 9.0 %all_gather.3 = f32[32,16,256]{2,1,0:T(8,128)S(1)} all-gather(f32[16,16,256]{2,1,0:T(8,128)S(1)} %all-to-all-done.2), channel_id=1, replica_groups=mesh['yh'=2,'x'=4,'core'=2,'z'=16,'yl'=2] {'core'}, dimensions={0}, use_global_device_ids=true | all-gather | bytes 786432 | tf_op jit(solution)/shard_map/all_gather | solution.py:239
  122.9 0.8 copy.16
  (17 shorter events, 0.2 us)
Async XLA Ops:
  1.7 7.3 %collective-permute-start = (f32[2,256,128]{2,1,0:T(8,128)S(1)}, f32[2,256,128]{2,1,0:T(8,128)S(1)}, u32[]{:S(2)}, u32[]{:S(2)}) collective-permute-start(f32[2,256,128]{2,1,0:T(8,128)S(1)} %get-tuple-element.13), channel_id=1, source_target_pairs={{0,1},{1,2},{2,3},{3,4},{4,5},{5,6},{6,7},{7,8},{8,9},{9,10},{10,1... | collective-permute-start | bytes 786440 | tf_op jit(solution)/shard_map/ppermute | solution.py:222
  5.8 20.3 %copy-start.3 = (s32[1,1,6,2]{2,3,1,0:T(2,128)S(1)}, s32[1,1,6,2]{2,3,1,0:T(2,128)}, u32[]{:S(2)}) copy-start(s32[1,1,6,2]{2,3,1,0:T(2,128)} %param.9) | copy-start | bytes 148
  5.8 26.1 %copy-start = (f32[2,256,256]{2,1,0:T(8,128)S(1)}, f32[2,256,256]{2,1,0:T(8,128)}, u32[]{:S(2)}) copy-start(f32[2,256,256]{2,1,0:T(8,128)} %tile_ref.1) | copy-start | bytes 1572868
  5.8 26.1 %copy-start.1 = (f32[2,256,256]{2,1,0:T(8,128)S(1)}, f32[2,256,256]{2,1,0:T(8,128)}, u32[]{:S(2)}) copy-start(f32[2,256,256]{2,1,0:T(8,128)} %probe_ref.1) | copy-start | bytes 1572868
  5.8 26.1 %copy-start.2 = (bf16[2,3,256,256]{3,2,1,0:T(8,128)(2,1)S(1)}, bf16[2,3,256,256]{3,2,1,0:T(8,128)(2,1)}, u32[]{:S(2)}) copy-start(bf16[2,3,256,256]{3,2,1,0:T(8,128)(2,1)} %constant.8.clone.tables_ref) | copy-start | bytes 2359300
  5.8 7.3 %collective-permute-start.1 = (f32[2,256,128]{2,1,0:T(8,128)S(1)}, f32[2,256,128]{2,1,0:T(8,128)S(1)}, u32[]{:S(2)}, u32[]{:S(2)}) collective-permute-start(f32[2,256,128]{2,1,0:T(8,128)S(1)} %get-tuple-element.12), channel_id=1, source_target_pairs={{1,0},{2,1},{3,2},{4,3},{5,4},{6,5},{7,6},{8,7},{9,8},{10,9},{11,1... | collective-permute-start | bytes 786440 | tf_op jit(solution)/shard_map/ppermute | solution.py:222
  14.2 16.0 %collective-permute-start.3 = (f32[2,128,512]{2,1,0:T(8,128)}, f32[2,128,512]{2,1,0:T(8,128)S(1)}, u32[]{:S(2)}, u32[]{:S(2)}) collective-permute-start(f32[2,128,512]{2,1,0:T(8,128)} %get-tuple-element.10), channel_id=1, source_target_pairs={{32,0},{64,32},{96,64},{128,96},{160,128},{192,160},{224,192},{256... | collective-permute-start | bytes 1572872 | tf_op jit(solution)/shard_map/ppermute | solution.py:222
  23.5 8.3 %collective-permute-start.2 = (f32[2,128,512]{2,1,0:T(8,128)}, f32[2,128,512]{2,1,0:T(8,128)S(1)}, u32[]{:S(2)}, u32[]{:S(2)}) collective-permute-start(f32[2,128,512]{2,1,0:T(8,128)} %get-tuple-element.11), channel_id=1, source_target_pairs={{0,32},{32,64},{64,96},{96,128},{128,160},{160,192},{192,224},{224... | collective-permute-start | bytes 1572872 | tf_op jit(solution)/shard_map/ppermute | solution.py:222
  40.9 25.6 %all-to-all-start = ((f32[32,16,256]{2,1,0:T(8,128)}), f32[32,16,256]{2,1,0:T(8,128)S(1)}, u32[]{:S(2)}, u32[]{:S(2)}) async-start(f32[32,16,256]{2,1,0:T(8,128)} %bitcast.2), calls=%async_computation | async-start | bytes 1048576 | tf_op jit(solution)/shard_map/all_to_all | solution.py:226
  55.6 32.0 %collective-permute-start.4 = (f32[2,128,512]{2,1,0:T(8,128)S(1)}, f32[2,128,512]{2,1,0:T(8,128)S(1)}, u32[]{:S(2)}, u32[]{:S(2)}) collective-permute-start(f32[2,128,512]{2,1,0:T(8,128)S(1)} %get-tuple-element.6), channel_id=1, source_target_pairs={{0,32},{32,64},{64,96},{96,128},{128,160},{160,192},{192,224},{224... | collective-permute-start | bytes 1572872 | tf_op jit(solution)/shard_map/ppermute | solution.py:222
  59.1 28.5 %collective-permute-start.5 = (f32[2,128,512]{2,1,0:T(8,128)S(1)}, f32[2,128,512]{2,1,0:T(8,128)S(1)}, u32[]{:S(2)}, u32[]{:S(2)}) collective-permute-start(f32[2,128,512]{2,1,0:T(8,128)S(1)} %get-tuple-element.7), channel_id=1, source_target_pairs={{32,0},{64,32},{96,64},{128,96},{160,128},{192,160},{224,192},{256... | collective-permute-start | bytes 1572872 | tf_op jit(solution)/shard_map/ppermute | solution.py:222
  67.2 35.1 %all-to-all-start.1 = ((f32[16,16,256]{2,1,0:T(8,128)}), f32[16,16,256]{2,1,0:T(8,128)S(1)}, u32[]{:S(2)}, u32[]{:S(2)}) async-start(f32[16,16,256]{2,1,0:T(8,128)} %broadcast_in_dim.4), calls=%async_computation.1 | async-start | bytes 524288 | tf_op jit(solution)/shard_map/all_to_all | solution.py:226
  89.1 17.5 %collective-permute-start.6 = (f32[2,256,128]{2,1,0:T(8,128)S(1)}, f32[2,256,128]{2,1,0:T(8,128)S(1)}, u32[]{:S(2)}, u32[]{:S(2)}) collective-permute-start(f32[2,256,128]{2,1,0:T(8,128)S(1)} %get-tuple-element.8), channel_id=1, source_target_pairs={{0,1},{1,2},{2,3},{3,4},{4,5},{5,6},{6,7},{7,8},{8,9},{9,10},{10,1... | collective-permute-start | bytes 786440 | tf_op jit(solution)/shard_map/ppermute | solution.py:222
  90.4 16.2 %collective-permute-start.7 = (f32[2,256,128]{2,1,0:T(8,128)S(1)}, f32[2,256,128]{2,1,0:T(8,128)S(1)}, u32[]{:S(2)}, u32[]{:S(2)}) collective-permute-start(f32[2,256,128]{2,1,0:T(8,128)S(1)} %get-tuple-element.9), channel_id=1, source_target_pairs={{1,0},{2,1},{3,2},{4,3},{5,4},{6,5},{7,6},{8,7},{9,8},{10,9},{11,1... | collective-permute-start | bytes 786440 | tf_op jit(solution)/shard_map/ppermute | solution.py:222
  103.1 10.9 %all-to-all-start.2 = ((f32[16,16,256]{2,1,0:T(8,128)}), f32[16,16,256]{2,1,0:T(8,128)S(1)}, u32[]{:S(2)}, u32[]{:S(2)}) async-start(f32[16,16,256]{2,1,0:T(8,128)} %broadcast_in_dim.5), calls=%async_computation.2 | async-start | bytes 524288 | tf_op jit(solution)/shard_map/all_to_all | solution.py:226

commit v6 on v5

--- a/solution.py
+++ b/solution.py
@@ -50,9 +50,9 @@
 
 def slots_kernel(
     counts_ref, pos_ref, tile_ref, side_l_ref, side_r_ref, top_ref, bot_ref, probe_ref, intensity_ref, tables_ref,
-    gprobe_out, grad_ref,
+    gprobe_out, gtop_out, gbot_out, gmid_out,
     ext_ref, over_ref, held_ref, table_ref, shifted_ref, window_ref, terms_ref,
-    mid_ref, far_ref, back_ref, gprobe_ref, sems, pattern_sems,
+    mid_ref, far_ref, back_ref, grad_ref, gprobe_ref, sems, pattern_sems,
 ):
     dot = lambda a, b: jnp.dot(a, b, preferred_element_type=F32)
     low, own, high = slice(0, RIM), slice(RIM, RIM + SIDE), slice(RIM + SIDE, WIDE)
@@ -180,9 +180,17 @@
         return carry
 
     lax.fori_loop(0, groups, one_group, 0)
-    copy = pltpu.make_async_copy(gprobe_ref, gprobe_out, sems.at[0])
-    copy.start()
-    copy.wait()
+    moves = [
+        (gprobe_ref, gprobe_out),
+        (grad_ref.at[:, low], gtop_out),
+        (grad_ref.at[:, high], gbot_out),
+        (grad_ref.at[:, own], gmid_out),
+    ]
+    copies = [pltpu.make_async_copy(src, dst, sems.at[k]) for k, (src, dst) in enumerate(moves)]
+    for copy in copies:
+        copy.start()
+    for copy in copies:
+        copy.wait()
 
 
 def all_slots(counts, positions, *arrays):
@@ -192,10 +200,12 @@
         slots_kernel,
         out_shape=[
             jax.ShapeDtypeStruct((2, SIDE, SIDE), F32),
-            jax.ShapeDtypeStruct((2, WIDE, WIDE), F32),
+            jax.ShapeDtypeStruct((2, RIM, WIDE), F32),
+            jax.ShapeDtypeStruct((2, RIM, WIDE), F32),
+            jax.ShapeDtypeStruct((2, SIDE, WIDE), F32),
         ],
         in_specs=[smem, smem] + [anywhere] * len(arrays),
-        out_specs=[anywhere, pl.BlockSpec(memory_space=pltpu.VMEM)],
+        out_specs=[anywhere] * 4,
         scratch_shapes=[
             pltpu.VMEM((2, WIDE, WIDE), F32),
             pltpu.VMEM((2, SIDE + 8, SIDE), F32),
@@ -207,6 +217,7 @@
             pltpu.VMEM((UNROLL, SIDE, WIDE), F32),
             pltpu.VMEM((UNROLL, SIDE, WIDE), F32),
             pltpu.VMEM((UNROLL, 2, SIDE + 8, SIDE), F32),
+            pltpu.VMEM((2, WIDE, WIDE), F32),
             pltpu.VMEM((2, SIDE, SIDE), F32),
             pltpu.SemaphoreType.DMA((8,)),
             pltpu.SemaphoreType.DMA((6 // UNROLL,)),
@@ -246,7 +257,7 @@
     middle = jnp.concatenate([side_l, object_field, side_r], axis=2)
     top = shifted(middle[:, RIM:], ROW, 1)
     bottom = shifted(middle[:, :RIM], ROW, -1)
-    grad_probe, grad_wide = all_slots(
+    grad_probe, grad_top, grad_bottom, grad_mid = all_slots(
         counts.reshape(1),
         positions.reshape(-1),
         object_field,
@@ -258,11 +269,11 @@
         intensity[0, 0],
         *tables,
     )
-    from_above = shifted(grad_wide[:, RIM + SIDE :], ROW, 1)
-    from_below = shifted(grad_wide[:, :RIM], ROW, -1)
+    from_above = shifted(grad_bottom, ROW, 1)
+    from_below = shifted(grad_top, ROW, -1)
     total_slots = lax.axis_size(ROW) * lax.axis_size(COL) * positions.shape[2]
     probe_update = summed_everywhere(grad_probe, 1.0 / math.sqrt(total_slots))
-    rows = grad_wide[:, RIM : RIM + SIDE] + jnp.concatenate([from_above, from_below], axis=1)
+    rows = grad_mid + jnp.concatenate([from_above, from_below], axis=1)
     from_left = shifted(rows[:, :, RIM + SIDE :], COL, 1)
     from_right = shifted(rows[:, :, :RIM], COL, -1)
     gathered = rows[:, :, RIM : RIM + SIDE] + jnp.concatenate([from_left, from_right], axis=2)

time: 124 us -> 121 us (0.976)
  starting transfers between devices: 62 us -> 54.5 us
  Pallas kernels: 9.04 us -> 14.6 us
  local copies, waits for them, and re-layouts: 7.01 us -> 3.77 us
  waiting for transfers between devices: 32.7 us -> 34.7 us
    all_to_all x3, starting transfers between devices: 37.3 us -> 30.8 us  [swap(): return lax.all_to_all(pieces, axes, split_axis=0, concat_axis=0, tiled=True)]
    pallas_call x1, Pallas kernels: 9.04 us -> 14.6 us  [all_slots(): pl.pallas_call(slots_kernel, out_shape=[jax.ShapeDtypeStruct((2, SIDE, SI...]
    all_to_all x3, waiting for transfers between devices: 22.4 us -> 23.7 us  [swap(): return lax.all_to_all(pieces, axes, split_axis=0, concat_axis=0, tiled=True)]
    slice x1 -> x0, local copies, waits for them, and re-layouts: 1.28 us -> none  [shards(): from_above = shifted(grad_wide[:, RIM + SIDE:], ROW, 1)]
  transfers between devices with their start and end apart: 11 -> 11, of which waited for: 7 -> 7; matrix products, arithmetic and copies ran while one was open for 5% -> 3% of each run, Pallas kernels for 0% -> 0%
where the time goes in v6:
time: 121 us
  starting transfers between devices  54.5 us (45%)
  waiting for transfers between devices  34.7 us (29%)
  Pallas kernels  14.6 us (12%)
  blocking collectives  8.96 us (7%)
  local copies, waits for them, and re-layouts  3.77 us (3%)
  other arithmetic  2.36 us (2%)
  between operations  1.52 us (1%)
    all_to_all x3, starting transfers between devices, swap(): return lax.all_to_all(pieces, axes, split_axis=0, concat_axis=0, tiled=True)  30.8 us
    ppermute x8, starting transfers between devices, shifted(): return lax.ppermute(block, axes, route)  23.8 us
    all_to_all x3, waiting for transfers between devices, swap(): return lax.all_to_all(pieces, axes, split_axis=0, concat_axis=0, tiled=True)  23.7 us
    pallas_call x1, Pallas kernels, all_slots(): pl.pallas_call(slots_kernel, out_shape=[jax.ShapeDtypeStruct((2, SIDE, SI...  14.6 us
    ppermute x8, waiting for transfers between devices, shifted(): return lax.ppermute(block, axes, route)  11 us
    all_gather x1, blocking collectives, summed_everywhere(): lax.all_gather(half, 'core', axis=0, tiled=True).reshape(2, SIDE, SIDE)  8.96 us
  transfers between devices with their start and end apart: 11, of which 7 were waited for; matrix products, arithmetic and copies ran while one was open for 3% of the time, Pallas kernels for 0%

profile of v6, /device:TPU:1, one launch (start us, length us, event | category | flops | bytes accessed | tf_op | source)
XLA Modules:
  0.0 120.5 jit_solution(7084659984468984000)
XLA Ops:
  0.6 1.1 fusion.4
  1.8 4.0 %collective-permute-start = (f32[2,256,128]{2,1,0:T(8,128)S(1)}, f32[2,256,128]{2,1,0:T(8,128)S(1)}, u32[]{:S(2)}, u32[]{:S(2)}) collective-permute-start(f32[2,256,128]{2,1,0:T(8,128)S(1)} %get-tuple-element.15), channel_id=1, source_target_pairs={{0,1},{1,2},{2,3},{3,4},{4,5},{5,6},{6,7},{7,8},{8,9},{9,10},{10,1... | collective-permute-start | bytes 786440 | tf_op jit(solution)/shard_map/ppermute | solution.py:233
  5.8 1.3 %collective-permute-start.1 = (f32[2,256,128]{2,1,0:T(8,128)S(1)}, f32[2,256,128]{2,1,0:T(8,128)S(1)}, u32[]{:S(2)}, u32[]{:S(2)}) collective-permute-start(f32[2,256,128]{2,1,0:T(8,128)S(1)} %get-tuple-element.14), channel_id=1, source_target_pairs={{1,0},{2,1},{3,2},{4,3},{5,4},{6,5},{7,6},{8,7},{9,8},{10,9},{11,1... | collective-permute-start | bytes 786440 | tf_op jit(solution)/shard_map/ppermute | solution.py:233
  7.1 2.0 %collective-permute-done.side_l_ref = f32[2,256,128]{2,1,0:T(8,128)S(1)} collective-permute-done((f32[2,256,128]{2,1,0:T(8,128)S(1)}, f32[2,256,128]{2,1,0:T(8,128)S(1)}, u32[]{:S(2)}, u32[]{:S(2)}) %collective-permute-start) | collective-permute-done | bytes 262176 | tf_op jit(solution)/shard_map/ppermute | solution.py:233
  9.1 0.1 constant_dynamic-update-slice_fusion.1
  9.2 0.0 copy-start.2
  9.2 3.8 %collective-permute-done.1.side_r_ref = f32[2,256,128]{2,1,0:T(8,128)S(1)} collective-permute-done((f32[2,256,128]{2,1,0:T(8,128)S(1)}, f32[2,256,128]{2,1,0:T(8,128)S(1)}, u32[]{:S(2)}, u32[]{:S(2)}) %collective-permute-start.1) | collective-permute-done | bytes 262176 | tf_op jit(solution)/shard_map/ppermute | solution.py:233
  13.0 0.1 fusion.3
  13.1 8.5 %collective-permute-start.3 = (f32[2,128,512]{2,1,0:T(8,128)S(1)}, f32[2,128,512]{2,1,0:T(8,128)S(1)}, u32[]{:S(2)}, u32[]{:S(2)}) collective-permute-start(f32[2,128,512]{2,1,0:T(8,128)S(1)} %get-tuple-element.12), channel_id=1, source_target_pairs={{32,0},{64,32},{96,64},{128,96},{160,128},{192,160},{224,192},{256... | collective-permute-start | bytes 1572872 | tf_op jit(solution)/shard_map/ppermute | solution.py:233
  21.6 1.9 %collective-permute-start.2 = (f32[2,128,512]{2,1,0:T(8,128)S(1)}, f32[2,128,512]{2,1,0:T(8,128)S(1)}, u32[]{:S(2)}, u32[]{:S(2)}) collective-permute-start(f32[2,128,512]{2,1,0:T(8,128)S(1)} %get-tuple-element.13), channel_id=1, source_target_pairs={{0,32},{32,64},{64,96},{96,128},{128,160},{160,192},{192,224},{224... | collective-permute-start | bytes 1572872 | tf_op jit(solution)/shard_map/ppermute | solution.py:233
  24.2 0.1 copy.11
  24.3 0.1 reshape.21.pos_ref
  24.3 3.7 %collective-permute-done.3.bot_ref = f32[2,128,512]{2,1,0:T(8,128)S(1)} collective-permute-done((f32[2,128,512]{2,1,0:T(8,128)S(1)}, f32[2,128,512]{2,1,0:T(8,128)S(1)}, u32[]{:S(2)}, u32[]{:S(2)}) %collective-permute-start.3) | collective-permute-done | bytes 524320 | tf_op jit(solution)/shard_map/ppermute | solution.py:233
  28.0 1.6 %collective-permute-done.2.top_ref = f32[2,128,512]{2,1,0:T(8,128)S(1)} collective-permute-done((f32[2,128,512]{2,1,0:T(8,128)S(1)}, f32[2,128,512]{2,1,0:T(8,128)S(1)}, u32[]{:S(2)}, u32[]{:S(2)}) %collective-permute-start.2) | collective-permute-done | bytes 524320 | tf_op jit(solution)/shard_map/ppermute | solution.py:233
  29.6 14.6 %shard_map.77 = (f32[2,256,256]{2,1,0:T(8,128)}, f32[2,128,512]{2,1,0:T(8,128)S(1)}, f32[2,128,512]{2,1,0:T(8,128)S(1)}, f32[2,256,512]{2,1,0:T(8,128)}) custom-call(s32[1]{0:T(128)} %bitcast.4.counts_ref, s32[12]{0:T(128)S(1)} %reshape.21.pos_ref, f32[2,256,256]{2,1,0:T(8,128)S(1)} %copy-done, f32[2,256,128]{2,1,0:T(8,128)S(1)} %collective-permute-done.side_l_ref, ...), custom_call_target="tpu_custom_call" | custom-call | flops 10000000000 | bytes 20000000 | tf_op jit(solution)/shard_map/pallas_call | solution.py:199
  44.3 9.1 %all-to-all-start = ((f32[32,16,256]{2,1,0:T(8,128)}), f32[32,16,256]{2,1,0:T(8,128)S(1)}, u32[]{:S(2)}, u32[]{:S(2)}) async-start(f32[32,16,256]{2,1,0:T(8,128)} %bitcast.2), calls=%async_computation | async-start | bytes 1048576 | tf_op jit(solution)/shard_map/all_to_all | solution.py:237
  53.3 3.5 %collective-permute-start.4 = (f32[2,128,512]{2,1,0:T(8,128)S(1)}, f32[2,128,512]{2,1,0:T(8,128)}, u32[]{:S(2)}, u32[]{:S(2)}) collective-permute-start(f32[2,128,512]{2,1,0:T(8,128)S(1)} %get-tuple-element.7), channel_id=1, source_target_pairs={{0,32},{32,64},{64,96},{96,128},{128,160},{160,192},{192,224},{224... | collective-permute-start | bytes 1572872 | tf_op jit(solution)/shard_map/ppermute | solution.py:233
  56.9 1.9 %collective-permute-start.5 = (f32[2,128,512]{2,1,0:T(8,128)S(1)}, f32[2,128,512]{2,1,0:T(8,128)}, u32[]{:S(2)}, u32[]{:S(2)}) collective-permute-start(f32[2,128,512]{2,1,0:T(8,128)S(1)} %get-tuple-element.8), channel_id=1, source_target_pairs={{32,0},{64,32},{96,64},{128,96},{160,128},{192,160},{224,192},{256... | collective-permute-start | bytes 1572872 | tf_op jit(solution)/shard_map/ppermute | solution.py:233
  58.8 6.7 %all-to-all-done = f32[32,16,256]{2,1,0:T(8,128)S(1)} async-done(((f32[32,16,256]{2,1,0:T(8,128)}), f32[32,16,256]{2,1,0:T(8,128)S(1)}, u32[]{:S(2)}, u32[]{:S(2)}) %all-to-all-start) | async-done | bytes 524320 | tf_op jit(solution)/shard_map/all_to_all | solution.py:237
  65.5 0.7 broadcast_in_dim.4
  66.2 18.2 %all-to-all-start.1 = ((f32[16,16,256]{2,1,0:T(8,128)}), f32[16,16,256]{2,1,0:T(8,128)S(1)}, u32[]{:S(2)}, u32[]{:S(2)}) async-start(f32[16,16,256]{2,1,0:T(8,128)} %broadcast_in_dim.4), calls=%async_computation.1 | async-start | bytes 524288 | tf_op jit(solution)/shard_map/all_to_all | solution.py:237
  84.4 0.0 collective-permute-done.4
  84.4 1.4 %maximum_add_fusion = f32[2,256,512]{2,1,0:T(8,128)S(1)} fusion(f32[2,256,512]{2,1,0:T(8,128)S(1)} %copy-done.1, f32[2,128,512]{2,1,0:T(8,128)} %collective-permute-done.5, f32[2,128,512]{2,1,0:T(8,128)} %collective-permute-done.4), kind=kLoop, calls=%fused_computation | loop fusion | flops 524288 | bytes 3145728 | tf_op jit(solution)/shard_map/add | solution.py:276
  85.9 1.3 %collective-permute-start.6 = (f32[2,256,128]{2,1,0:T(8,128)S(1)}, f32[2,256,128]{2,1,0:T(8,128)S(1)}, u32[]{:S(2)}, u32[]{:S(2)}) collective-permute-start(f32[2,256,128]{2,1,0:T(8,128)S(1)} %get-tuple-element.10), channel_id=1, source_target_pairs={{0,1},{1,2},{2,3},{3,4},{4,5},{5,6},{6,7},{7,8},{8,9},{9,10},{10,1... | collective-permute-start | bytes 786440 | tf_op jit(solution)/shard_map/ppermute | solution.py:233
  87.2 1.3 %collective-permute-start.7 = (f32[2,256,128]{2,1,0:T(8,128)S(1)}, f32[2,256,128]{2,1,0:T(8,128)S(1)}, u32[]{:S(2)}, u32[]{:S(2)}) collective-permute-start(f32[2,256,128]{2,1,0:T(8,128)S(1)} %get-tuple-element.11), channel_id=1, source_target_pairs={{1,0},{2,1},{3,2},{4,3},{5,4},{6,5},{7,6},{8,7},{9,8},{10,9},{11,1... | collective-permute-start | bytes 786440 | tf_op jit(solution)/shard_map/ppermute | solution.py:233
  88.5 10.6 %all-to-all-done.1 = f32[16,16,256]{2,1,0:T(8,128)S(1)} async-done(((f32[16,16,256]{2,1,0:T(8,128)}), f32[16,16,256]{2,1,0:T(8,128)S(1)}, u32[]{:S(2)}, u32[]{:S(2)}) %all-to-all-start.1) | async-done | bytes 262176 | tf_op jit(solution)/shard_map/all_to_all | solution.py:237
  99.2 0.7 broadcast_in_dim.5
  99.9 3.5 %all-to-all-start.2 = ((f32[16,16,256]{2,1,0:T(8,128)}), f32[16,16,256]{2,1,0:T(8,128)S(1)}, u32[]{:S(2)}, u32[]{:S(2)}) async-start(f32[16,16,256]{2,1,0:T(8,128)} %broadcast_in_dim.5), calls=%async_computation.2 | async-start | bytes 524288 | tf_op jit(solution)/shard_map/all_to_all | solution.py:237
  103.5 0.9 fusion.1
  104.3 6.4 %all-to-all-done.2 = f32[16,16,256]{2,1,0:T(8,128)S(1)} async-done(((f32[16,16,256]{2,1,0:T(8,128)}), f32[16,16,256]{2,1,0:T(8,128)S(1)}, u32[]{:S(2)}, u32[]{:S(2)}) %all-to-all-start.2) | async-done | bytes 262176 | tf_op jit(solution)/shard_map/all_to_all | solution.py:237
  110.8 9.0 %all_gather.3 = f32[32,16,256]{2,1,0:T(8,128)S(1)} all-gather(f32[16,16,256]{2,1,0:T(8,128)S(1)} %all-to-all-done.2), channel_id=1, replica_groups=mesh['yh'=2,'x'=4,'core'=2,'z'=16,'yl'=2] {'core'}, dimensions={0}, use_global_device_ids=true | all-gather | bytes 786432 | tf_op jit(solution)/shard_map/all_gather | solution.py:250
  119.7 0.8 copy.16
  (14 shorter events, 0.2 us)
Async XLA Ops:
  0.6 8.5 %copy-start = (f32[2,256,256]{2,1,0:T(8,128)S(1)}, f32[2,256,256]{2,1,0:T(8,128)}, u32[]{:S(2)}) copy-start(f32[2,256,256]{2,1,0:T(8,128)} %tile_ref.1) | copy-start | bytes 1572868
  1.8 7.3 %collective-permute-start = (f32[2,256,128]{2,1,0:T(8,128)S(1)}, f32[2,256,128]{2,1,0:T(8,128)S(1)}, u32[]{:S(2)}, u32[]{:S(2)}) collective-permute-start(f32[2,256,128]{2,1,0:T(8,128)S(1)} %get-tuple-element.15), channel_id=1, source_target_pairs={{0,1},{1,2},{2,3},{3,4},{4,5},{5,6},{6,7},{7,8},{8,9},{9,10},{10,1... | collective-permute-start | bytes 786440 | tf_op jit(solution)/shard_map/ppermute | solution.py:233
  5.8 7.2 %collective-permute-start.1 = (f32[2,256,128]{2,1,0:T(8,128)S(1)}, f32[2,256,128]{2,1,0:T(8,128)S(1)}, u32[]{:S(2)}, u32[]{:S(2)}) collective-permute-start(f32[2,256,128]{2,1,0:T(8,128)S(1)} %get-tuple-element.14), channel_id=1, source_target_pairs={{1,0},{2,1},{3,2},{4,3},{5,4},{6,5},{7,6},{8,7},{9,8},{10,9},{11,1... | collective-permute-start | bytes 786440 | tf_op jit(solution)/shard_map/ppermute | solution.py:233
  9.2 15.0 %copy-start.2 = (s32[1,1,6,2]{2,3,1,0:T(2,128)S(1)}, s32[1,1,6,2]{2,3,1,0:T(2,128)}, u32[]{:S(2)}) copy-start(s32[1,1,6,2]{2,3,1,0:T(2,128)} %param.9) | copy-start | bytes 148
  13.1 14.9 %collective-permute-start.3 = (f32[2,128,512]{2,1,0:T(8,128)S(1)}, f32[2,128,512]{2,1,0:T(8,128)S(1)}, u32[]{:S(2)}, u32[]{:S(2)}) collective-permute-start(f32[2,128,512]{2,1,0:T(8,128)S(1)} %get-tuple-element.12), channel_id=1, source_target_pairs={{32,0},{64,32},{96,64},{128,96},{160,128},{192,160},{224,192},{256... | collective-permute-start | bytes 1572872 | tf_op jit(solution)/shard_map/ppermute | solution.py:233
  21.6 8.0 %collective-permute-start.2 = (f32[2,128,512]{2,1,0:T(8,128)S(1)}, f32[2,128,512]{2,1,0:T(8,128)S(1)}, u32[]{:S(2)}, u32[]{:S(2)}) collective-permute-start(f32[2,128,512]{2,1,0:T(8,128)S(1)} %get-tuple-element.13), channel_id=1, source_target_pairs={{0,32},{32,64},{64,96},{96,128},{128,160},{160,192},{192,224},{224... | collective-permute-start | bytes 1572872 | tf_op jit(solution)/shard_map/ppermute | solution.py:233
  44.3 40.2 %copy-start.1 = (f32[2,256,512]{2,1,0:T(8,128)S(1)}, f32[2,256,512]{2,1,0:T(8,128)}, u32[]{:S(2)}) copy-start(f32[2,256,512]{2,1,0:T(8,128)} %get-tuple-element.6) | copy-start | bytes 3145732
  44.3 21.2 %all-to-all-start = ((f32[32,16,256]{2,1,0:T(8,128)}), f32[32,16,256]{2,1,0:T(8,128)S(1)}, u32[]{:S(2)}, u32[]{:S(2)}) async-start(f32[32,16,256]{2,1,0:T(8,128)} %bitcast.2), calls=%async_computation | async-start | bytes 1048576 | tf_op jit(solution)/shard_map/all_to_all | solution.py:237
  53.3 31.1 %collective-permute-start.4 = (f32[2,128,512]{2,1,0:T(8,128)S(1)}, f32[2,128,512]{2,1,0:T(8,128)}, u32[]{:S(2)}, u32[]{:S(2)}) collective-permute-start(f32[2,128,512]{2,1,0:T(8,128)S(1)} %get-tuple-element.7), channel_id=1, source_target_pairs={{0,32},{32,64},{64,96},{96,128},{128,160},{160,192},{192,224},{224... | collective-permute-start | bytes 1572872 | tf_op jit(solution)/shard_map/ppermute | solution.py:233
  56.9 27.5 %collective-permute-start.5 = (f32[2,128,512]{2,1,0:T(8,128)S(1)}, f32[2,128,512]{2,1,0:T(8,128)}, u32[]{:S(2)}, u32[]{:S(2)}) collective-permute-start(f32[2,128,512]{2,1,0:T(8,128)S(1)} %get-tuple-element.8), channel_id=1, source_target_pairs={{32,0},{64,32},{96,64},{128,96},{160,128},{192,160},{224,192},{256... | collective-permute-start | bytes 1572872 | tf_op jit(solution)/shard_map/ppermute | solution.py:233
  66.2 32.9 %all-to-all-start.1 = ((f32[16,16,256]{2,1,0:T(8,128)}), f32[16,16,256]{2,1,0:T(8,128)S(1)}, u32[]{:S(2)}, u32[]{:S(2)}) async-start(f32[16,16,256]{2,1,0:T(8,128)} %broadcast_in_dim.4), calls=%async_computation.1 | async-start | bytes 524288 | tf_op jit(solution)/shard_map/all_to_all | solution.py:237
  85.9 17.5 %collective-permute-start.6 = (f32[2,256,128]{2,1,0:T(8,128)S(1)}, f32[2,256,128]{2,1,0:T(8,128)S(1)}, u32[]{:S(2)}, u32[]{:S(2)}) collective-permute-start(f32[2,256,128]{2,1,0:T(8,128)S(1)} %get-tuple-element.10), channel_id=1, source_target_pairs={{0,1},{1,2},{2,3},{3,4},{4,5},{5,6},{6,7},{7,8},{8,9},{9,10},{10,1... | collective-permute-start | bytes 786440 | tf_op jit(solution)/shard_map/ppermute | solution.py:233
  87.2 16.2 %collective-permute-start.7 = (f32[2,256,128]{2,1,0:T(8,128)S(1)}, f32[2,256,128]{2,1,0:T(8,128)S(1)}, u32[]{:S(2)}, u32[]{:S(2)}) collective-permute-start(f32[2,256,128]{2,1,0:T(8,128)S(1)} %get-tuple-element.11), channel_id=1, source_target_pairs={{1,0},{2,1},{3,2},{4,3},{5,4},{6,5},{7,6},{8,7},{9,8},{10,9},{11,1... | collective-permute-start | bytes 786440 | tf_op jit(solution)/shard_map/ppermute | solution.py:233
  99.9 10.9 %all-to-all-start.2 = ((f32[16,16,256]{2,1,0:T(8,128)}), f32[16,16,256]{2,1,0:T(8,128)S(1)}, u32[]{:S(2)}, u32[]{:S(2)}) async-start(f32[16,16,256]{2,1,0:T(8,128)} %broadcast_in_dim.5), calls=%async_computation.2 | async-start | bytes 524288 | tf_op jit(solution)/shard_map/all_to_all | solution.py:237
